TPU v7x, 32 devices: a whole 2x2x4 slice. The times are simulated.
32 devices in a mesh: dp: 16 (over z, x, core), head: 2 (over y).
Axes of the slice: x: 2, y: 2, z: 4, core: 2. Of those that a mesh axis runs over, the one named last changes fastest.
Arguments:
- tokens_in: bfloat16 [24576, 512], P(('dp', 'head')), may hold values from -6 to 6
- cotangent: float32 [24576, 512], P(('dp', 'head')), may hold values from -6 to 6
- data_table: float32 [2, 512], replicated, may hold values from -6 to 6
- window_group: int32 [256], P('dp'), may hold values from 0 to 1
- query_picks: int32 [256, 8, 25], P('dp', 'head'), may hold values from 0 to 95, as said below
- owner_list: int32 [6], replicated, may hold values from 0 to 15
- weight_qkv: float32 [3, 512, 512], P(None, None, 'head'), may hold values from -0.25 to 0.25
- head_bias: float32 [2, 512], P(None, 'head'), may hold values from -3 to 3
- weight_out: float32 [512, 512], P('head'), may hold values from -2 to 2
- weight_up: float32 [512, 2048], P(None, 'head'), may hold values from -0.25 to 0.25
- ff_bias: float32 [2048], P('head'), may hold values from -3 to 3
- weight_down: float32 [2048, 512], P('head'), may hold values from -0.125 to 0.125
- norm_gains: float32 [2, 512], replicated, may hold values from 0.5 to 1.5
- shifts: float32 [4, 512], replicated, may hold values from -3 to 3
- first_qkv: float32 [3, 512, 512], P(None, None, 'head'), may hold values from -512 to 512
- second_qkv: float32 [3, 512, 512], P(None, None, 'head'), may hold values from 8847.36 to 35389.44
- first_out: float32 [512, 512], P('head'), may hold values from -80 to 80
- second_out: float32 [512, 512], P('head'), may hold values from 184.32 to 742.4
- first_up: float32 [512, 2048], P(None, 'head'), may hold values from -224 to 224
- second_up: float32 [512, 2048], P(None, 'head'), may hold values from 1536 to 6144
- first_down: float32 [2048, 512], P('head'), may hold values from -448 to 448
- second_down: float32 [2048, 512], P('head'), may hold values from 4915.2 to 19660.8
- basis_qkv_left: float32 [3, 512, 512], replicated
- basis_qkv_right: float32 [3, 8, 64, 64], P(None, 'head')
- basis_out_left: float32 [8, 64, 64], P('head')
- basis_out_right: float32 [512, 512], replicated
- basis_up_left: float32 [512, 512], replicated
- basis_up_right: float32 [8, 256, 256], P('head')
- basis_down_left: float32 [8, 256, 256], P('head')
- basis_down_right: float32 [512, 512], replicated
Outputs:
- output: float32 [24576, 512], P(('dp', 'head'))
- grad_input: float32 [24576, 512], P(('dp', 'head'))
- grad_table: float32 [2, 512], replicated
- grad_gains: float32 [2, 512], replicated
- grad_shifts: float32 [4, 512], replicated
- grad_head_bias: float32 [2, 512], P(None, 'head')
- grad_ff_bias: float32 [2048], P('head')
- grad_qkv: float32 [3, 512, 512], P(None, None, 'head')
- grad_out_proj: float32 [512, 512], P('head')
- grad_up: float32 [512, 2048], P(None, 'head')
- grad_down: float32 [2048, 512], P('head')
- new_qkv: float32 [16, 3, 512, 512], P('dp', None, None, 'head')
- momentum_qkv: float32 [16, 3, 512, 512], P('dp', None, None, 'head')
- variance_qkv: float32 [16, 3, 512, 512], P('dp', None, None, 'head')
- copy_qkv: bfloat16 [16, 3, 512, 512], P('dp', None, None, 'head')
- new_out_proj: float32 [16, 512, 512], P('dp', 'head')
- moments_out_proj: float32 [16, 2, 512, 512], P('dp', None, 'head')
- copy_out_proj: bfloat16 [16, 512, 512], P('dp', 'head')
- new_up: float32 [16, 512, 2048], P('dp', None, 'head')
- momentum_up: float32 [16, 512, 2048], P('dp', None, 'head')
- variance_up: float32 [16, 512, 2048], P('dp', None, 'head')
- copy_up: bfloat16 [16, 512, 2048], P('dp', None, 'head')
- new_down: float32 [16, 2048, 512], P('dp', 'head')
- momentum_down: float32 [16, 2048, 512], P('dp', 'head')
- variance_down: float32 [16, 2048, 512], P('dp', 'head')
- copy_down: bfloat16 [16, 2048, 512], P('dp', 'head')
Inputs may be any that keep to these rules, and one draw needn't show every extreme that they name: `query_picks`: within one window and head the 25 positions are distinct.
All inputs are finite; a program needn't handle non-finite values.
Results may differ from a plain program's by a relative error of at most 0.019.
Values may be sent and summed in bfloat16 or wider, within the bound.
No kernel may reach another device: no remote copies, remote signals or barrier semaphores. Data moves between devices by JAX's collectives and lax.ppermute only.
A program may use at most 192 MiB of HBM per device.

v0:
```python
import math

import jax
import jax.numpy as jnp
from jax import lax
from jax.experimental import pallas as pl
from jax.experimental.pallas import tpu as pltpu
from jax.sharding import PartitionSpec as P

f32 = jnp.float32
bf16 = jnp.bfloat16

NDATA = 2
EPS_NORM = 1e-05
EPS_ADAM = 1e-08
BETA_ONE = 0.5
BETA_TWO = 0.5

GROUP = 4
SLOTS = 32
MB = 1 << 20


def nn(a, b):
    return jnp.dot(a, b, preferred_element_type=f32)


def nt(a, b):
    return lax.dot_general(a, b, (((1,), (1,)), ((), ())), preferred_element_type=f32)


def col_sum(x):
    return jnp.sum(x, axis=0, keepdims=True)


def row_mean(x):
    return jnp.mean(x, axis=-1, keepdims=True)


VMEM = pl.BlockSpec(memory_space=pltpu.VMEM)
SMEM = pl.BlockSpec(memory_space=pltpu.SMEM)
HBM = pl.BlockSpec(memory_space=pl.ANY)
FAR = pl.BlockSpec(memory_space=pl.ANY)


def whole(*shape):
    return pl.BlockSpec(shape, lambda i: (0,) * len(shape))


def cut(*shape):
    return pl.BlockSpec(shape, lambda i: (i,) + (0,) * (len(shape) - 1))


US = 1_000_000_000


def in_hbm(x, spec):
    if spec is SMEM or spec is HBM or x.size * x.dtype.itemsize < 1 << 16:
        return x
    return pltpu.with_memory_space_constraint(x, pltpu.HBM)


def call(body, outs, ins, args, scratch, limit, flops, nbytes, aliases={}, grid=(), hbm_in=True, hbm_out=True):
    if hbm_in:
        args = [in_hbm(x, spec) for x, spec in zip(args, ins)]
    kind = pltpu.HBM if hbm_out else jax.ShapeDtypeStruct
    return pl.pallas_call(
        body,
        grid=grid,
        out_shape=tuple(kind(s, d) for s, d, _ in outs),
        in_specs=ins,
        out_specs=tuple(spec for _, _, spec in outs),
        scratch_shapes=scratch,
        input_output_aliases=aliases,
        compiler_params=pltpu.CompilerParams(vmem_limit_bytes=limit * MB),
        cost_estimate=pl.CostEstimate(
            flops=int(flops), bytes_accessed=int(nbytes), transcendentals=0
        ),
    )(*args)


def head_mask(cols):
    width = cols // GROUP
    shape = (GROUP * SLOTS, cols)
    return (
        lax.broadcasted_iota(jnp.int32, shape, 0) // SLOTS
        == lax.broadcasted_iota(jnp.int32, shape, 1) // width
    )


def one_hot(picks, w, length):
    row = picks[pl.ds(w, 1), :]
    spots = lax.broadcasted_iota(jnp.int32, (length, GROUP * SLOTS), 0).astype(f32)
    columns = (spots == row).astype(f32)
    return columns.astype(bf16), columns.T.astype(bf16)


def copy_all(pairs, sems):
    copies = [pltpu.make_async_copy(a, b, sems.at[i]) for i, (a, b) in enumerate(pairs)]
    for copy in copies:
        copy.start()
    return copies


def split_sum(parts, at):
    return parts[at : at + 1] + parts[at + 1 : at + 2] + parts[at + 2 : at + 3]


def put_parts(extra, at, row):
    for i in range(3):
        part = row.astype(bf16).astype(f32)
        extra[at + i : at + i + 1, :] = part
        row = row - part


def pack_qkv(windows, info, w, bias, picks, piece, low, extra):
    core = info[0]
    half = w.shape[1] // 2
    for j in range(3):
        low[j] = w[j].astype(bf16)
        piece[j * half : (j + 1) * half, :] = w[j, pl.ds(pl.multiple_of(core * half, half), half), :].astype(bf16)
    extra[...] = jnp.zeros_like(extra)
    for i in range(windows):
        extra[i : i + 1, : GROUP * SLOTS] = picks[pl.ds(info[2] + i, 1), :]
    put_parts(extra, windows, bias[0:1, :])
    put_parts(extra, windows + 3, bias[1:2, :])
    piece[3 * half :, :] = extra[...].astype(bf16)


def pack_rest(info, w_out, w_up, w_down, bias, piece, down_piece, low, down_low, extra):
    hid = w_up.shape[1] // 2
    n_out, n_up, n_down = w_out.shape[0] // 2, w_up.shape[0] // 2, w_down.shape[0] // 2
    extra[...] = jnp.zeros_like(extra)
    put_parts(extra, 0, bias[:, :hid])
    put_parts(extra, 3, bias[:, hid:])
    for m in range(2):
        low[m, :n_out, :] = w_out[m * n_out : (m + 1) * n_out, :].astype(bf16)
        for h in range(2):
            at = n_out + h * n_up
            low[m, at : at + n_up, :] = w_up[
                m * n_up : (m + 1) * n_up, h * hid : (h + 1) * hid
            ].astype(bf16)
        low[m, low.shape[1] - 16 :, :] = extra[...].astype(bf16)
    down_low[...] = w_down[...].astype(bf16)
    piece[...] = low[info[0]]
    down_piece[...] = down_low[pl.ds(pl.multiple_of(info[0] * n_down, n_down), n_down), :]


def attend(wq, bias, picks, start, emb, q_out, k_out, v_out, ctx, att, picked, length, scale):
    cols = wq.shape[2]
    e = emb[...]
    for j, out in enumerate((q_out, k_out, v_out)):
        out[...] = (nn(e, wq[j]) + bias[j]).astype(bf16)
    mask = head_mask(cols)
    mask_low = mask.astype(f32).astype(bf16)
    for i in range(emb.shape[0] // length):
        here = slice(i * length, (i + 1) * length)
        up, down = one_hot(picks, start + i, length)
        q, k, v = q_out[here, :], k_out[here, :], v_out[here, :]
        sel = jnp.where(mask, nn(down, q), 0.0).astype(bf16)
        scores = nt(sel, k) * scale
        exponent = jnp.exp(scores - jnp.max(scores, axis=-1, keepdims=True))
        probs = exponent / jnp.sum(exponent, axis=-1, keepdims=True)
        mixed = jnp.where(mask, nn(probs.astype(bf16), v), 0.0).astype(bf16)
        mean = col_sum(v.astype(f32)) * (1.0 / length)
        active = nn(up, mask_low)
        ctx[here, :] = (nn(up, mixed) + (1.0 - active) * mean).astype(bf16)
        att[i] = probs
        picked[i] = sel


def attend_own(length, scale, info, groups, tokens, table, wq, bias, picks,
               q, k, v, ctx, att, picked, emb):
    per = tokens.shape[0] // length
    first = pl.program_id(0) * per
    for i in range(per):
        here = slice(i * length, (i + 1) * length)
        row = table[pl.ds(groups[info[3] + first + i], 1), :]
        emb[here, :] = (tokens[here, :].astype(f32) + row).astype(bf16)
    rows = (bias[0:1, :], jnp.zeros_like(bias[0:1, :]), bias[1:2, :])
    attend(wq, rows, picks, info[1] + first, emb, q, k, v, ctx, att, picked, length, scale)


def attend_far(length, scale, info, emb, y_piece, c_piece,
               q, k, v, ctx, att, picked, wq, picks, extra, bias, sems):
    core = info[0]
    half = wq.shape[1] // 2
    windows = picks.shape[0]

    @pl.when(pl.program_id(0) == 0)
    def _():
        pairs = [(y_piece.at[pl.ds(3 * half, extra.shape[0]), :], extra)]
        for j in range(3):
            for piece, spot in ((y_piece, core), (c_piece, 1 - core)):
                pairs.append(
                    (
                        piece.at[pl.ds(j * half, half), :],
                        wq.at[j, pl.ds(pl.multiple_of(spot * half, half), half), :],
                    )
                )
        for copy in copy_all(pairs, sems):
            copy.wait()
        rest = extra[...].astype(f32)
        picks[...] = rest[:windows, : GROUP * SLOTS]
        bias[0:1, :] = split_sum(rest, windows)
        bias[1:2, :] = split_sum(rest, windows + 3)

    rows = (bias[0:1, :], jnp.zeros_like(bias[0:1, :]), bias[1:2, :])
    first = pl.program_id(0) * (emb.shape[0] // length)
    attend(wq, rows, picks, first, emb, q, k, v, ctx, att, picked, length, scale)


def gelu_pair(x):
    bell = jnp.exp(-0.5 * (x * x))
    t = 1.0 / (1.0 + (0.3275911 * math.sqrt(0.5)) * jnp.abs(x))
    poly = t * (
        0.5 * 0.254829592
        + t * (0.5 * -0.284496736 + t * (0.5 * 1.421413741 + t * (0.5 * -1.453152027 + t * (0.5 * 1.061405429))))
    )
    tail = poly * bell
    phi = jnp.where(x >= 0.0, 1.0 - tail, tail)
    return x * phi, phi + x * bell * (1.0 / math.sqrt(2.0 * math.pi))


def ff_in(length, info, groups, tokens, table, ctx0, ctx1, near, y_piece, c_piece, ff_bias, gains, shifts,
          resid, act, slope, wo, up, pre, ffb, extra, sems):
    core = info[0]
    step = pl.program_id(0)
    block, width = tokens.shape
    cols = wo.shape[1]
    half = up.shape[2] // 2
    per = block // length

    @pl.when(step == 0)
    def _():
        pairs = [(y_piece.at[pl.ds(y_piece.shape[0] - 16, 16), :], extra)]
        for g, piece, spot in (
            (0, near.at[0], 0), (0, near.at[1], 1), (1, y_piece, core), (1, c_piece, 1 - core)
        ):
            n = cols // 2
            pairs.append(
                (piece.at[pl.ds(0, n), :], wo.at[g, pl.ds(pl.multiple_of(spot * n, n), n), :])
            )
            at, n = n, width // 2
            for h in range(2):
                pairs.append(
                    (
                        piece.at[pl.ds(at + h * n, n), :],
                        up.at[g, pl.ds(pl.multiple_of(spot * n, n), n), pl.ds(h * half, half)],
                    )
                )
        copies = copy_all(pairs, sems)
        ffb[0:1, :] = ff_bias[...]
        for copy in copies:
            copy.wait()
        rest = extra[...].astype(f32)
        ffb[1:2, :half] = split_sum(rest, 0)
        ffb[1:2, half:] = split_sum(rest, 3)

    for i in range(per):
        part = slice(i * length, (i + 1) * length)
        pre[part, :] = tokens[part, :].astype(f32) + table[pl.ds(groups[info[3] + step * per + i], 1), :]
    x = pre[...] + (nn(ctx0[...], wo[0]) + nn(ctx1[...], wo[1]) + shifts[0:1, :])
    resid[...] = x
    center = x - row_mean(x)
    unit = center * lax.rsqrt(row_mean(center * center) + EPS_NORM)
    low = (unit * gains[0:1, :] + shifts[2:3, :]).astype(bf16)
    for ch in range(4):
        g, o = ch // 2, (ch % 2) * half
        z = nn(low, up[g, :, o : o + half]) + ffb[g : g + 1, o : o + half]
        a, d = gelu_pair(z)
        act[:, ch * half : (ch + 1) * half] = a.astype(bf16)
        slope[:, ch * half : (ch + 1) * half] = d.astype(bf16)


def ff_back(length, info, groups, resid, act_in, slope, up, near, y_piece, c_piece, gains, shifts, cot, ctx0, ctx1,
            out, gp1, ga, keep, send, sums,
            dn, act, gpre, nl, gb, ga_all, nl_t, gb_t, buf, sems, act_sems):
    core = info[0]
    step = pl.program_id(0)
    block, width = resid.shape
    rows = nl.shape[0]
    cols = ctx0.shape[1]
    hid = up.shape[2]
    half = hid // 2
    per = block // length
    blocks = rows // block
    act_copies = [
        pltpu.make_async_copy(
            act_in.at[pl.ds(i * block, block), :], act.at[pl.ds(i * block, block), :], act_sems.at[i]
        )
        for i in range(blocks)
    ]

    @pl.when(step == 0)
    def _():
        n = hid // 2
        pairs = [
            (near, dn.at[0]),
            (y_piece, dn.at[1, pl.ds(pl.multiple_of(core * n, n), n), :]),
            (c_piece, dn.at[1, pl.ds(pl.multiple_of((1 - core) * n, n), n), :]),
        ]
        copies = copy_all(pairs, sems)
        for copy in act_copies:
            copy.start()
        sums[...] = jnp.zeros_like(sums)
        for copy in copies:
            copy.wait()

    for i, copy in enumerate(act_copies):

        @pl.when(step == i)
        def _(copy=copy):
            copy.wait()

    here = pl.ds(pl.multiple_of(step * block, 32), block)
    x = resid[...]
    center = x - row_mean(x)
    inv_one = lax.rsqrt(row_mean(center * center) + EPS_NORM)
    unit_one = center * inv_one
    normed = unit_one * gains[0:1, :] + shifts[2:3, :]
    nl[here, :] = normed.astype(bf16)
    branch = shifts[1:2, :]
    for g in range(2):
        branch = branch + nn(act[here, g * hid : (g + 1) * hid], dn[g])
    y = normed + branch
    center = y - row_mean(y)
    inv_two = lax.rsqrt(row_mean(center * center) + EPS_NORM)
    unit_two = center * inv_two
    out[...] = unit_two * gains[1:2, :] + shifts[3:4, :]
    c = cot[...]
    sums[1:2, :] += col_sum(c * unit_two)
    sums[5:6, :] += col_sum(c)
    g2 = c * gains[1:2, :]
    gp2 = (g2 - row_mean(g2) - unit_two * row_mean(g2 * unit_two)) * inv_two
    low = gp2.astype(bf16)
    gb[here, :] = low
    sums[3:4, :] += col_sum(low.astype(f32))
    total = gp2
    for ch in range(4):
        g, o = ch // 2, (ch % 2) * half
        p = nt(low, dn[g, o : o + half, :]) * slope[:, ch * half : (ch + 1) * half].astype(f32)
        p = p.astype(bf16)
        gpre[here, ch * half : (ch + 1) * half] = p
        sums[6 + ch : 7 + ch, :] += col_sum(p.astype(f32))
        total = total + nt(p, up[g, :, o : o + half])
    sums[0:1, :] += col_sum(total * unit_one)
    sums[4:5, :] += col_sum(total)
    g1 = total * gains[0:1, :]
    gp = (g1 - row_mean(g1) - unit_one * row_mean(g1 * unit_one)) * inv_one
    gp1[...] = gp
    low = gp.astype(bf16)
    ga[...] = low
    ga_all[here, :] = low
    sums[2:3, :] += col_sum(low.astype(f32))
    for i in range(per):
        spot = pl.ds(10 + groups[info[3] + step * per + i], 1)
        sums[spot, :] += col_sum(gp[i * length : (i + 1) * length, :])

    @pl.when(step == blocks - 1)
    def _():
        nl_t[...] = nl[...].astype(f32).T.astype(bf16)
        gb_t[...] = gb[...].astype(f32).T.astype(bf16)
        for ch in range(4):
            g, o = ch // 2, (ch % 2) * half
            at = slice(ch * half, (ch + 1) * half)
            buf[g, o : o + half, :] = nn(nl_t[...], gpre[:, at]).astype(bf16)
            buf[g, hid + o : hid + o + half, :] = nn(gb_t[...], act[:, at]).astype(bf16)
        for g, ctx in enumerate((ctx0, ctx1)):
            buf[g, 2 * hid : 2 * hid + cols, :] = nn(
                ctx[...].astype(f32).T.astype(bf16), ga_all[...]
            ).astype(bf16)
        n = buf.shape[1] // 2
        pairs = []
        for g in range(2):
            for dst, spot in ((keep, core), (send, 1 - core)):
                pairs.append((buf.at[g, pl.ds(pl.multiple_of(spot * n, 32), n), :], dst.at[g]))
        for copy in copy_all(pairs, sems):
            copy.wait()


def attend_back(length, scale, info, groups, ga, emb, wo, sums, picks0, picks1, wq0, wq1,
                k0, v0, att0, picked0, k1, v1, att1, picked1,
                gq, gk, gv, keep, send,
                gq_all, gk_all, gv_all, emb_all, wq0_all, wq1_all, emb_t, tsum, buf, small, sems):
    core = info[0]
    step = pl.program_id(0)
    rows, width = emb.shape
    block = ga.shape[0]
    per = block // length
    cols = wq0.shape[2]
    mask = head_mask(cols)
    mask_low = mask.astype(f32).astype(bf16)

    late = [
        pltpu.make_async_copy(a, b, sems.at[8 + i])
        for i, (a, b) in enumerate(((emb, emb_all), (wq0, wq0_all), (wq1, wq1_all)))
    ]

    @pl.when(step == 0)
    def _():
        for copy in late:
            copy.start()
        tsum[...] = jnp.zeros_like(tsum)

    e = ga[...]
    sides = ((k0, v0, att0, picked0, picks0, info[1]), (k1, v1, att1, picked1, picks1, 0))
    for g, (k_in, v_in, att, picked, picks, start) in enumerate(sides):
        at = slice(g * cols, (g + 1) * cols)
        g_ctx = nt(e, wo[g]).astype(bf16)
        for i in range(per):
            here = slice(i * length, (i + 1) * length)
            up, down = one_hot(picks, start + step * per + i, length)
            k, v = k_in[here, :], v_in[here, :]
            gc = g_ctx[here, :]
            ge = jnp.where(mask, nn(down, gc), 0.0).astype(bf16)
            active = nn(up, mask_low)
            gmean = col_sum((1.0 - active) * gc.astype(f32)) * (1.0 / length)
            probs = att[i]
            gprobs = nt(ge, v)
            low_t = probs.T.astype(bf16)
            g_value = (nn(low_t, ge) + gmean).astype(bf16)
            weighted = probs * gprobs
            graw = (weighted - probs * jnp.sum(weighted, axis=-1, keepdims=True)) * scale
            g_key = nn(graw.T.astype(bf16), picked[i]).astype(bf16)
            gpick = jnp.where(mask, nn(graw.astype(bf16), k), 0.0).astype(bf16)
            g_query = nn(up, gpick).astype(bf16)
            rows_here = pl.ds(pl.multiple_of(step * block + i * length, 32), length)
            group = groups[info[3] + step * per + i]
            for j, (x, dst, dst_all) in enumerate(
                ((g_query, gq, gq_all), (g_key, gk, gk_all), (g_value, gv, gv_all))
            ):
                dst[here, at] = x
                dst_all[rows_here, at] = x
                tsum[pl.ds(2 * j + group, 1), at] += col_sum(x.astype(f32))

    @pl.when(step == rows // block - 1)
    def _():
        for copy in late:
            copy.wait()
        emb_t[...] = emb_all[...].astype(f32).T.astype(bf16)
        half = width // 2
        for g in range(2):
            at = slice(g * cols, (g + 1) * cols)
            for j, x in enumerate((gq_all, gk_all, gv_all)):
                r = nn(emb_t[...], x[:, at]).astype(bf16)
                buf[g, j * half : (j + 1) * half, :cols] = r[:half]
                buf[g, j * half : (j + 1) * half, cols:] = r[half:]
        total = jnp.zeros((8, width), f32)
        for j in range(3):
            for g, wq in enumerate((wq0_all, wq1_all)):
                x = tsum[2 * j : 2 * j + 8, g * cols : (g + 1) * cols]
                hi = x.astype(bf16)
                lo = (x - hi.astype(f32)).astype(bf16)
                total = total + nt(hi, wq[j]) + nt(lo, wq[j])
        for g in range(2):
            at = slice(g * cols, (g + 1) * cols)
            small[g] = jnp.zeros_like(small[g])
            small[g, 0:2, :] = total[0:2] + sums[10:12, :]
            small[g, 2:8, :] = sums[0:6, :]
            small[g, 8:10, :] = sums[6 + 2 * g : 8 + 2 * g, :]
            small[g, 10:11, :cols] = tsum[0:1, at] + tsum[1:2, at]
            small[g, 10:11, cols:] = tsum[4:5, at] + tsum[5:6, at]
            buf[g, 3 * half : 3 * half + 16, :] = small[g].astype(bf16)
        n = 3 * half // 2
        pairs = []
        for g in range(2):
            for dst, spot in ((keep, core), (send, 1 - core)):
                pairs.append((buf.at[g, pl.ds(pl.multiple_of(spot * n, 32), n), :], dst.at[g, pl.ds(0, n), :]))
                pairs.append((buf.at[g, pl.ds(2 * n, 16), :], dst.at[g, pl.ds(n, 16), :]))
        for copy in copy_all(pairs, sems):
            copy.wait()


def input_grad(gq, gk, gv, wq0, wq1, gp1, out):
    cols = wq0.shape[2]
    total = gp1[...]
    for j, x in enumerate((gq, gk, gv)):
        for g, wq in enumerate((wq0, wq1)):
            total = total + nt(x[:, g * cols : (g + 1) * cols], wq[j])
    out[...] = total


def hop(x, *bits):
    heads = lax.axis_size("head")
    flip = sum((1 << k) * (heads if axis == "dp" else 1) for axis, k in bits)
    count = lax.axis_size("dp") * heads
    return lax.ppermute(x, ("dp", "head"), [(i, i ^ flip) for i in range(count)])


def side(bit):
    axis, k = bit
    return (lax.axis_index(axis) >> k) & 1


def subsets(bits):
    return [[b for i, b in enumerate(bits) if (r >> i) & 1] for r in range(1 << len(bits))]


def pair_sum(terms):
    while len(terms) > 1:
        terms = [terms[i] + terms[i + 1] for i in range(0, len(terms), 2)]
    return terms[0]


def pick(x, bits, far, flips):
    for bit in bits:
        flipped = bit in flips
        if bit == far:
            x = x[1:] if flipped else x[:1]
        else:
            n = x.shape[1] // 2
            x = lax.dynamic_slice_in_dim(x, (side(bit) ^ int(flipped)) * n, n, 1)
    return x


def scatter_sum(x, bits, far, small=None):
    terms, rest = [], []
    for flips in subsets(bits):
        part = pick(x, bits, far, flips)
        if small is not None:
            part = jnp.concatenate([part, pick(small, [far] if far in bits else [], far, flips)], 1)
        if flips:
            part = hop(part, *flips)
        terms.append(part.astype(f32))
    total = pair_sum(terms).astype(bf16)
    if small is None:
        return total
    n = total.shape[1] - small.shape[1]
    return total[:, :n], total[:, n:]


def gather(x, bits):
    parts = {}
    for r, flips in enumerate(subsets(bits)):
        parts[r] = hop(x, *flips) if flips else x
    for i, bit in enumerate(bits):
        m = side(bit) == 0
        parts = {
            r: jnp.where(m, parts[r], parts[r ^ (1 << i)]) for r in parts
        }
    order = sorted(parts, key=lambda r: [(r >> i) & 1 for i in range(len(bits))])
    return jnp.concatenate([parts[r] for r in order], axis=0)


def plus(a, b):
    return (a.astype(f32) + b.astype(f32)).astype(bf16)


def late_steps(small_rows, bits, far, core):
    stages = [[far, bits[0]]] + [bits[i : i + 2] for i in range(1, len(bits), 2)]

    def cores(state):
        x = plus(state[0], hop(state[1], core))
        return x[:, :-small_rows], x[:, -small_rows:]

    def down(stage):
        return lambda state: scatter_sum(state[0], stage, far, state[1])

    def up(stage):
        wanted = [b for b in stage if b != far]

        def step(state):
            x = state[0] if state[0].ndim == 2 else state[0][0]
            return gather(x, wanted), state[1]

        return step

    return [cores] + [down(s) for s in stages] + [up(s) for s in reversed(stages)] + [up([core])]


def early_steps(bits, far, core):
    first, second, rest = bits[0], bits[1], bits[2:]
    orders = ((far, first, second), (first, second, far), (second, far, first))

    def start(x):
        part = x.shape[1] // 3
        return down(0)([x[:, i * part : (i + 1) * part] for i in range(3)])

    def down(stage):
        return lambda chunks: [scatter_sum(c, [order[stage]], far) for c, order in zip(chunks, orders)]

    def swap(chunks):
        x = jnp.concatenate(chunks, axis=2)[0]
        for bit in rest:
            x = plus(x, hop(x, bit))
        width = x.shape[1] // 3
        return [x[:, : 2 * width], x[:, 2 * width :]]

    def up_one(parts):
        return [gather(parts[0], [second]), gather(parts[1], [first])]

    def up_two(parts):
        two, one = gather(parts[0], [first]), gather(parts[1], [second])
        width = one.shape[1]
        return jnp.concatenate([two[:, :width], two[:, width:], one], axis=0)

    return [start, down(1), down(2), swap, up_one, up_two, lambda x: gather(x, [core])]


def add(a, b):
    return a.astype(f32) + b.astype(f32)


def at_row(start, n):
    return pl.ds(pl.multiple_of(start, 16), n)


def merge_cores(info, keep, got, stay0, far0, stay1, first1, stay2, second2):
    n = keep.shape[1] // 3
    h = n // 2
    a, b = info[4], info[5]
    stay0[...] = add(keep[0, :n], got[0, :n]).astype(bf16)
    far0[...] = add(keep[1, :n], got[1, :n]).astype(bf16)
    for base, bit, stay, send in ((n, a, stay1, first1), (2 * n, b, stay2, second2)):
        for dst, m in ((stay, bit), (send, 1 - bit)):
            here = at_row(base + m * h, h)
            for g in range(2):
                dst[g] = add(keep[g, here], got[g, here]).astype(bf16)


def merge_two(info, stay0, got0, stay1, got1, stay2, got2, keep0, first0, keep1, second1, keep2, far2):
    a, b = info[4], info[5]
    h = stay0.shape[0] // 2
    for dst, m in ((keep0, a), (first0, 1 - a)):
        here = at_row(m * h, h)
        dst[...] = add(stay0[here], got0[here]).astype(bf16)
    q = stay1.shape[1] // 2
    for dst, m in ((keep1, b), (second1, 1 - b)):
        here = at_row(m * q, q)
        for g in range(2):
            dst[g] = add(stay1[g, here], got1[g, here]).astype(bf16)
    keep2[...] = add(stay2[0], got2[0]).astype(bf16)
    far2[...] = add(stay2[1], got2[1]).astype(bf16)


def merge_three(info, in0, got0, in1, got1, in2, got2, keep, got, stay, mine, to_second, to_far, to_first, to_both):
    a, b = info[4], info[5]
    q = in0.shape[0] // 2
    stay[:q] = add(in0[at_row(b * q, q)], got0[at_row(b * q, q)]).astype(bf16)
    to_second[...] = add(in0[at_row((1 - b) * q, q)], got0[at_row((1 - b) * q, q)]).astype(bf16)
    stay[q : 2 * q] = add(in1[0], got1[0]).astype(bf16)
    to_far[:q] = add(in1[1], got1[1]).astype(bf16)
    stay[2 * q :] = add(in2[at_row(a * q, q)], got2[at_row(a * q, q)]).astype(bf16)
    to_first[:q] = add(in2[at_row((1 - a) * q, q)], got2[at_row((1 - a) * q, q)]).astype(bf16)
    n = mine.shape[0]
    h = n - 16
    for dst, base, g, m in (
        (mine, 0, 0, a), (to_first, q, 0, 1 - a), (to_far, q, 1, a), (to_both, 0, 1, 1 - a)
    ):
        here = at_row(m * h, h)
        dst[base : base + h] = add(keep[g, here], got[g, here]).astype(bf16)
        dst[base + h : base + n] = add(keep[g, 2 * h :], got[g, 2 * h :]).astype(bf16)


def merge_four(info, stay, mine, second, far, first, both, part, own, to_second, to_third, to_both, total):
    q = second.shape[0]
    e = part
    e[:q] = add(stay[:q], second[...]).astype(bf16)
    e[q : 2 * q] = add(stay[q : 2 * q], far[:q]).astype(bf16)
    e[2 * q :] = add(stay[2 * q :], first[:q]).astype(bf16)
    to_third[: 3 * q] = e[...]
    total[...] = (add(mine[...], first[q:]) + add(far[q:], both[...])).astype(bf16)
    n = own.shape[0] - 16
    spot = 2 * info[5] + info[6]
    for dst, base, flip in ((own, 0, 0), (to_second, 0, 2), (to_third, 3 * q, 1), (to_both, 0, 3)):
        dst[base : base + n] = total[at_row((spot ^ flip) * n, n)]
        dst[base + n : base + n + 16] = total[4 * n :]


def merge_five(part, own, second, third, both, to_second, to_first, table, gains, shifts, ff, bias):
    n = part.shape[0]
    total = add(part[...], third[:n]).astype(bf16)
    q = n // 3
    to_second[...] = total[: 2 * q]
    to_first[:q] = total[2 * q :]
    s = add(own[...], second[...]) + add(third[n:], both[...])
    h = own.shape[0] - 16
    to_first[q:] = s[:h].astype(bf16)
    s = s[h:]
    width = s.shape[1]
    table[...] = s[0:2]
    gains[...] = s[2:4]
    shifts[...] = s[4:8]
    ff[:, :width] = s[8:9]
    ff[:, width:] = s[9:10]
    bias[0:1] = s[10:11, : width // 2]
    bias[1:2] = s[10:11, width // 2 :]


def merge_six(info, near2, got2, near1, got1, to_first, to_second, to_third):
    a, b = info[4], info[5]
    q = near2.shape[0] // 2
    for c in range(2):
        to_first[at_row(2 * c * q + b * q, q)] = near2[c * q : (c + 1) * q]
        to_first[at_row(2 * c * q + (1 - b) * q, q)] = got2[c * q : (c + 1) * q]
    to_second[at_row(a * q, q)] = near1[:q]
    to_second[at_row((1 - a) * q, q)] = got1[:q]
    h = near1.shape[0] - q
    to_third[at_row(a * h, h)] = near1[q:]
    to_third[at_row((1 - a) * h, h)] = got1[q:]
    to_second[2 * q :] = to_third[...]


def merge_seven(info, near1, got1, near2, got2, near3, got3, both, out):
    a, b = info[4], info[5]
    h = near1.shape[0] // 2
    for c in range(2):
        out[at_row(2 * c * h + a * h, h)] = near1[c * h : (c + 1) * h]
        out[at_row(2 * c * h + (1 - a) * h, h)] = got1[c * h : (c + 1) * h]
    out[at_row(4 * h + b * h, h)] = near2[:h]
    out[at_row(4 * h + (1 - b) * h, h)] = got2[:h]
    spot = 2 * b + info[6]
    n = near3.shape[0] // 2
    for src, base, flip in ((near3, 0, 0), (got2, h, 2), (got3, 0, 1), (both, 0, 3)):
        for m in range(2):
            out[at_row(6 * h + m * 4 * n + (spot ^ flip) * n, n)] = src[base + m * n : base + (m + 1) * n]


def merge(body, info, ins, outs, width, with_info=True):
    shapes = [(s if isinstance(s, tuple) else (s, width), bf16, VMEM) for s in outs]
    return call(
        body,
        shapes,
        [SMEM] * with_info + [VMEM] * len(ins),
        ((info,) if with_info else ()) + tuple(ins),
        [],
        24,
        2 * US,
        2e6,
        hbm_in=False,
        hbm_out=False,
    )


def sum_start(info, keep, send, bits, far, core):
    first, second, _ = bits
    width = keep.shape[2]
    n = keep.shape[1] // 3
    two = (2, n // 2, width)
    stay0, far0, stay1, first1, stay2, second2 = merge(
        merge_cores, info, (keep, hop(send, core)), (n, n, two, two, two, two), width
    )
    return (stay0, hop(far0, far), stay1, hop(first1, first), stay2, hop(second2, second))


def sum_finish(info, state, keep, send, bits, far, core, beside):
    first, second, third = bits
    width = keep.shape[2]
    n = state[0].shape[0]
    q = n // 4
    keep0, first0, keep1, second1, keep2, far2 = merge(
        merge_two, info, state, (n // 2, n // 2, (2, q, width), (2, q, width), n // 2, n // 2), width
    )
    keep0, send = lax.optimization_barrier((keep0, send))
    got = hop(send, core)
    h = (keep.shape[1] - 16) // 2 + 16
    stay, mine, to_second, to_far, to_first, to_both = merge(
        merge_three,
        info,
        (keep0, hop(first0, first), keep1, hop(second1, second), keep2, hop(far2, far), keep, got),
        (3 * q, h, q, q + h, q + h, h),
        width,
    )
    m = (h - 16) // 4
    part, own, to_second, to_third, to_both, _ = merge(
        merge_four,
        info,
        (stay, mine, hop(to_second, second), hop(to_far, far), hop(to_first, first), hop(to_both, first, far)),
        (3 * q, m + 16, m + 16, 3 * q + m + 16, m + 16, h),
        width,
    )
    many = beside[0](part)
    part, many[0] = lax.optimization_barrier((part, many[0]))
    c = width // 2
    to_second, to_first, *small = call(
        merge_five,
        [((2 * q, width), bf16, VMEM), ((q + m, width), bf16, VMEM)]
        + [(shape, f32, VMEM) for shape in ((2, width), (2, width), (4, width), (1, 2 * width), (2, c))],
        [VMEM] * 5,
        (part, own, hop(to_second, second), hop(to_third, third), hop(to_both, second, third)),
        [],
        24,
        2 * US,
        2e6,
        hbm_in=False,
        hbm_out=False,
    )
    got2, got1 = hop(to_second, second), hop(to_first, first)
    to_first, to_second, to_third = merge(
        merge_six, info, (to_second, got2, to_first, got1), (4 * q, 2 * q + 2 * m, 2 * m), width
    )
    rows = beside[1](to_third)
    got1, got2 = hop(to_first, first), hop(to_second, second)
    got3, both = hop(to_third, third), hop(to_third, second, third)
    to_first, rows = lax.optimization_barrier((to_first, rows))
    (mine,) = merge(
        merge_seven, info, (to_first, got1, to_second, got2, to_third, got3, both), (12 * q + 8 * m,), width
    )
    few = beside[2](mine)
    return mine, hop(mine, core), small, (many, rows, few)


def wipe(*refs):
    sems = refs[-1]
    count = sems.shape[0]
    outs, zeros = refs[1 : 1 + count], refs[1 + count : -1]
    for zero in zeros:
        zero[...] = jnp.zeros_like(zero)
    copies = []
    for i, out in enumerate(outs):
        src = next(z for z in zeros if z.dtype == out.dtype and z.shape[1] == out.shape[1])
        rows = out.shape[0]
        n = next(c for c in (256, 192, 128, 64, 32, 16) if rows % c == 0)
        for at in range(0, rows, n):
            copies.append(
                pltpu.make_async_copy(
                    src.at[pl.ds(0, n), :], out.at[pl.ds(at, n), :], sems.at[i]
                )
            )
    for copy in copies:
        copy.start()
    for copy in copies:
        copy.wait()


def blanks_for(gate, likes):
    flat = [(math.prod(x.shape[:-1]), x.shape[-1]) for x in likes]
    widths = sorted({n for _, n in flat})
    outs = call(
        wipe,
        [(s, x.dtype, HBM) for s, x in zip(flat, likes)],
        [HBM],
        (gate,),
        [pltpu.VMEM((256, n), k) for n in widths for k in (f32, bf16)]
        + [pltpu.SemaphoreType.DMA((len(likes),))],
        8,
        5 * US,
        14e6,
        hbm_in=False,
    )
    return [x.reshape(like.shape) for x, like in zip(outs, likes)]


def moments(turned, m, v):
    first = BETA_ONE * m[...] + (1.0 - BETA_ONE) * turned
    second = BETA_TWO * v[...] + (1.0 - BETA_TWO) * (turned * turned)
    m[...] = first
    v[...] = second
    return (first / (jnp.sqrt(second) + EPS_ADAM)).astype(bf16)


def fetch(pairs, sems):
    for copy in copy_all(pairs, sems):
        copy.wait()


def step_wide(g, w, m, v, ql, qr, rate, scratch):
    low_l, low_r, mid, back = scratch
    low_l[...] = ql[...].astype(bf16)
    low_r[...] = qr[...].astype(bf16)
    blocks, size = qr.shape[0], qr.shape[1]
    mid[...] = nn(ql[...].T.astype(bf16), g).astype(bf16)
    for b in range(blocks):
        at = slice(b * size, (b + 1) * size)
        u = moments(nn(mid[:, at], low_r[b]), m.at[:, at], v.at[:, at])
        back[:, at] = nt(u, low_r[b]).astype(bf16)
    w[...] = w[...] - rate * nn(low_l[...], back[...])


def step_tall(g, w, m, v, ql, qr, rate, scratch):
    low_r, mid, back = scratch
    low_r[...] = qr[...].astype(bf16)
    blocks, size = ql.shape[0], ql.shape[1]
    for b in range(blocks):
        at = slice(b * size, (b + 1) * size)
        mid[at, :] = nn(ql[b].T.astype(bf16), g[at, :]).astype(bf16)
    u = moments(nn(mid[...], low_r[...]), m, v)
    back[...] = nt(u, low_r[...]).astype(bf16)
    for b in range(blocks):
        at = slice(b * size, (b + 1) * size)
        w[at, :] = w[at, :] - rate * nn(ql[b].astype(bf16), back[at, :])


def update_qkv(rate, mine, g, w_in, m_in, v_in, ql_in, qr_in, *refs):
    outs, (grad, new, mom, var, copy) = refs[:4], refs[4:9]
    w, m, v, c, ql, qr, low_l, low_r, mid, back, sems = refs[9:]
    for j in range(3):
        grad[j] = g[j].astype(f32)

        @pl.when(mine[j] == 1)
        def _():
            fetch(
                [(w_in.at[j], w), (m_in.at[j], m), (v_in.at[j], v), (ql_in.at[j], ql), (qr_in.at[j], qr)], sems
            )
            step_wide(g[j], w, m, v, ql, qr, rate, (low_l, low_r, mid, back))
            c[...] = w[...].astype(bf16)
            fetch([(w, new.at[j]), (m, mom.at[j]), (v, var.at[j]), (c, copy.at[j])], sems)


def update_rest(rate_out, rate_up, rate_down, mine, g_out, g_up, g_down_t, *refs):
    (wo_in, mo_in, vo_in, lo_in, ro_in, wu_in, mu_in, vu_in, lu_in, ru_in,
     wd_in, md_in, vd_in, ld_in, rd_in) = refs[:15]
    refs = refs[15 + 11 :]
    grad_o, grad_u, grad_d = refs[:3]
    new_o, moments_o, copy_o, new_u, mom_u, var_u, copy_u, new_d, mom_d, var_d, copy_d = refs[3:14]
    (wo, mo, vo, co, lo, ro, low_ro, mid_o, back_o,
     wu, mu, vu, cu, lu, ru, low_lu, low_ru, mid_u, back_u,
     wd, md, vd, cd, mid_d, back_d, sems) = refs[14:]
    grad_o[...] = g_out[...].astype(f32)
    grad_u[...] = g_up[...].astype(f32)
    grad_d[...] = g_down_t[...].astype(f32).T

    @pl.when(mine[3] == 1)
    def _():
        fetch([(wo_in, wo), (mo_in, mo), (vo_in, vo), (lo_in, lo), (ro_in, ro)], sems)
        step_tall(g_out[...], wo, mo, vo, lo, ro, rate_out, (low_ro, mid_o, back_o))
        co[...] = wo[...].astype(bf16)
        fetch([(wo, new_o), (mo, moments_o.at[0]), (vo, moments_o.at[1]), (co, copy_o)], sems)

    @pl.when(mine[4] == 1)
    def _():
        fetch([(wu_in, wu), (mu_in, mu), (vu_in, vu), (lu_in, lu), (ru_in, ru)], sems)
        step_wide(g_up[...], wu, mu, vu, lu, ru, rate_up, (low_lu, low_ru, mid_u, back_u))
        cu[...] = wu[...].astype(bf16)
        fetch([(wu, new_u), (mu, mom_u), (vu, var_u), (cu, copy_u)], sems)

    @pl.when(mine[5] == 1)
    def _():
        fetch([(wd_in, wd), (md_in, md), (vd_in, vd), (ld_in, ru), (rd_in, lu)], sems)
        step_tall(grad_d[...].astype(bf16), wd, md, vd, ru, lu, rate_down, (low_lu, mid_d, back_d))
        cd[...] = wd[...].astype(bf16)
        fetch([(wd, new_d), (md, mom_d), (vd, var_d), (cd, copy_d)], sems)


def owned_step(flag, ins, outs, bufs, in_sems, out_sems):
    loads = [pltpu.make_async_copy(a, b, in_sems.at[i]) for i, (a, b) in enumerate(zip(ins, bufs[:5]))]
    stores = [
        pltpu.make_async_copy(b, a, out_sems.at[i])
        for i, (a, b) in enumerate(zip(outs, (bufs[0], bufs[1], bufs[2], bufs[5])))
    ]

    @pl.when(flag)
    def _():
        for copy in loads:
            copy.start()

    return loads, stores


def update_all(rate_out, rate_wide, rate_down, cols, hid, owned, info, mine, other, *refs):
    wq, mq, vq, lq, rq, wo, mo, vo, lo, ro, wu, mu, vu, lu, ru, wd, md, vd, ld, rd = refs[:20]
    refs = refs[20 + 15 :]
    grad_q, grad_o, grad_u, grad_d = refs[:4]
    new_q, mom_q, var_q, copy_q, new_o, mom_o, copy_o, new_u, mom_u, var_u, copy_u, new_d, mom_d, var_d, copy_d = refs[4:19]
    refs = refs[19:]
    buf, gq, go, gu, gd = refs[:5]
    bufs_q, bufs_o, bufs_u, bufs_d = refs[5:11], refs[11:17], refs[17:23], refs[23:29]
    low_l, low_r64, low_r256, mid_q, mid_o, mid_u, mid_d, back_q, back_o, back_u, back_d = refs[29:40]
    sems, in_sems, out_sems = refs[40:]
    core = info[0]
    width = buf.shape[1]
    half = width // 2
    one = mine.shape[0] // 4 * 3
    two = mine.shape[0] - one
    pairs = []
    for piece, spot in ((mine, core), (other, 1 - core)):
        pairs.append((piece.at[pl.ds(0, one)], buf.at[at_row(spot * one, one)]))
        pairs.append((piece.at[pl.ds(one, two)], buf.at[at_row(2 * one + spot * two, two)]))
    fills = copy_all(pairs, sems)
    jobs = []
    for j in range(3):
        jobs.append(
            owned_step(
                owned[j] == 1,
                [x.at[j] for x in (wq, mq, vq, lq, rq)],
                [x.at[j] for x in (new_q, mom_q, var_q, copy_q)],
                [x.at[j] for x in bufs_q],
                in_sems.at[j],
                out_sems.at[j],
            )
        )
    jobs.append(
        owned_step(owned[3] == 1, (wo, mo, vo, lo, ro), (new_o, mom_o.at[0], mom_o.at[1], copy_o), bufs_o,
                   in_sems.at[3], out_sems.at[3])
    )
    jobs.append(
        owned_step(owned[4] == 1, (wu, mu, vu, lu, ru), (new_u, mom_u, var_u, copy_u), bufs_u,
                   in_sems.at[4], out_sems.at[4])
    )
    jobs.append(
        owned_step(owned[5] == 1, (wd, md, vd, ld, rd), (new_d, mom_d, var_d, copy_d), bufs_d,
                   in_sems.at[5], out_sems.at[5])
    )
    for copy in fills:
        copy.wait()
    grads = []

    def give(scratch, out):
        copy = pltpu.make_async_copy(scratch, out, sems.at[4 + len(grads)])
        copy.start()
        grads.append(copy)

    n = hid // 2
    for h in range(2):
        gu[:, h * n : (h + 1) * n] = buf[h * width : (h + 1) * width, :].astype(f32)
    give(gu, grad_u)
    go[...] = buf[2 * hid : 2 * hid + cols, :].astype(f32)
    give(go, grad_o)
    base = 2 * hid + cols
    for j in range(3):
        x = buf[base + j * half : base + (j + 1) * half, :].astype(f32)
        gq[j, :half, :] = x[:, :cols]
        gq[j, half:, :] = x[:, cols:]
    give(gq, grad_q)
    for h in range(2):
        gd[h * n : (h + 1) * n, :] = buf[hid + h * width : hid + (h + 1) * width, :].astype(f32).T
    give(gd, grad_d)

    def finish(k, bufs, run):
        loads, stores = jobs[k]

        @pl.when(owned[k] == 1)
        def _():
            for copy in loads:
                copy.wait()
            run()
            bufs[5][...] = bufs[0][...].astype(bf16)
            for copy in stores:
                copy.start()

    w, m, v, l, r, _ = bufs_u
    finish(4, bufs_u, lambda: step_wide(gu[...].astype(bf16), w, m, v, l, r, rate_wide,
                                        (low_l, low_r256, mid_u, back_u)))
    wt, mt, vt, lt, rt, _ = bufs_d
    finish(5, bufs_d, lambda: step_tall(gd[...].astype(bf16), wt, mt, vt, lt, rt, rate_down,
                                        (low_l, mid_d, back_d)))
    ws, ms, vs, ls, rs, _ = bufs_o
    finish(3, bufs_o, lambda: step_tall(go[...].astype(bf16), ws, ms, vs, ls, rs, rate_out,
                                        (low_l, mid_o, back_o)))
    for j in range(3):
        here = [x.at[j] for x in bufs_q]
        finish(j, here, lambda here=here, j=j: step_wide(gq[j].astype(bf16), *here[:5], rate_wide,
                                                         (low_l, low_r64, mid_q, back_q)))
    for k in range(6):

        @pl.when(owned[k] == 1)
        def _(k=k):
            for copy in jobs[k][1]:
                copy.wait()

    for copy in grads:
        copy.wait()


def pad_picks(picks):
    windows, heads, slots = picks.shape
    return jnp.pad(picks, ((0, 0), (0, 0), (0, SLOTS - slots)), constant_values=-1).reshape(
        windows, heads * SLOTS
    )


def per_device(
    tokens_in,
    cotangent,
    data_table,
    window_group,
    query_picks,
    owner_list,
    weight_qkv,
    head_bias,
    weight_out,
    weight_up,
    ff_bias,
    weight_down,
    norm_gains,
    shifts,
    first_qkv,
    second_qkv,
    first_out,
    second_out,
    first_up,
    second_up,
    first_down,
    second_down,
    basis_qkv_left,
    basis_qkv_right,
    basis_out_left,
    basis_out_right,
    basis_up_left,
    basis_up_right,
    basis_down_left,
    basis_down_right,
):
    head_count = lax.axis_size("head")
    head = lax.axis_index("head")
    my_rank = lax.axis_index("dp")
    rows, width = tokens_in.shape
    length = rows * head_count // window_group.shape[0]
    windows = rows // length
    head_dim = basis_qkv_right.shape[-1]
    cols = GROUP * head_dim
    scale = 1.0 / math.sqrt(head_dim)
    head_bits = head_count.bit_length() - 1
    far = ("head", head_bits - 1)
    core_bit = ("dp", 0)
    dp_bits = lax.axis_size("dp").bit_length() - 1
    bits = [("dp", k) for k in range(1, dp_bits)] + [("head", k) for k in range(head_bits - 1)]
    core = my_rank & 1
    slots = GROUP * SLOTS
    half = width // 2

    if head_count == 2:
        n_qkv, n_bias, n_out, n_up, n_ff, n_down = (
            weight_qkv, head_bias, weight_out, weight_up, ff_bias, weight_down
        )
        picks = pad_picks(query_picks).astype(f32)
        near_at, far_at = head * windows, (1 - head) * windows
    else:
        def whole_of(x, dim):
            return lax.all_gather(x, "head", axis=dim, tiled=True)

        def pick_group(x, dim, g):
            n = x.shape[dim] // 2
            return lax.dynamic_slice_in_dim(x, (side(far) ^ g) * n, n, dim)

        both = [
            (whole_of(weight_qkv.astype(bf16), 2).astype(f32), 2),
            (whole_of(head_bias, 1), 1),
            (whole_of(weight_out.astype(bf16), 0).astype(f32), 0),
            (whole_of(weight_up.astype(bf16), 1).astype(f32), 1),
            (whole_of(ff_bias, 0), 0),
            (whole_of(weight_down.astype(bf16), 0).astype(f32), 0),
        ]
        n_qkv, n_bias, n_out, n_up, n_ff, n_down = (pick_group(x, d, 0) for x, d in both)
        away = [pick_group(x, d, 1) for x, d in both]
        picks = lax.dynamic_slice_in_dim(whole_of(query_picks, 1), head * windows, windows, 0)
        picks = jnp.concatenate([pad_picks(pick_group(picks, 1, g)) for g in range(2)]).astype(f32)
        near_at, far_at = jnp.int32(0), jnp.int32(windows)
    info = jnp.stack([core, near_at, far_at, head * windows] + [side(b) for b in bits]).astype(jnp.int32)
    quick = head_count == 2 and len(bits) == 3
    hid = n_up.shape[1]
    extra_rows = -(-(windows + 6) // 16) * 16
    buf_rows = 2 * hid + cols
    rest_rows = cols // 2 + width + 16

    def send_qkv(info, w, bias):
        return call(
            lambda *refs: pack_qkv(windows, *refs),
            [((3 * half + extra_rows, cols), bf16, VMEM), ((3, width, cols), bf16, VMEM)],
            [SMEM, VMEM, VMEM, VMEM],
            (info, w, bias, picks),
            [pltpu.VMEM((extra_rows, cols), f32)],
            12,
            2 * US,
            3e6,
            hbm_in=False,
            hbm_out=False,
        )

    def send_rest(info, w_out, w_up, w_down, bias):
        return call(
            pack_rest,
            [
                ((rest_rows, width), bf16, VMEM),
                ((hid // 2, width), bf16, VMEM),
                ((2, rest_rows, width), bf16, VMEM),
                ((hid, width), bf16, VMEM),
            ],
            [SMEM, VMEM, VMEM, VMEM, VMEM],
            (info, w_out, w_up, w_down, bias[None]),
            [pltpu.VMEM((16, width), f32)],
            24,
            4 * US,
            8e6,
            hbm_in=False,
            hbm_out=False,
        )

    qkv_piece, wq0 = send_qkv(info, n_qkv, n_bias)
    if head_count == 2:
        qkv_y = hop(qkv_piece, far)
        rest_piece, down_piece, rest0, down0 = send_rest(info, n_out, n_up, n_down, n_ff)
        rest_piece, qkv_y = lax.optimization_barrier((rest_piece, qkv_y))
        rest_y = hop(rest_piece, far)
        down_piece, rest_y = lax.optimization_barrier((down_piece, rest_y))
        down_y = hop(down_piece, far)
    else:
        other = info.at[0].set(1 - core)
        rest0, down0 = send_rest(info, n_out, n_up, n_down, n_ff)[2:]
        qkv_y, qkv_c = (send_qkv(m, away[0], away[1])[0] for m in (info, other))
        (rest_y, down_y), (rest_c, down_c) = (
            send_rest(m, away[2], away[3], away[5], away[4])[:2] for m in (info, other)
        )

    block = 2 * length
    steps = (rows // block,)
    seen = [
        ((rows, cols), bf16, cut(block, cols)),
        ((rows, cols), bf16, cut(block, cols)),
        ((rows, cols), bf16, cut(block, cols)),
        ((rows, cols), bf16, cut(block, cols)),
        ((windows, slots, length), f32, cut(2, slots, length)),
        ((windows, slots, cols), bf16, cut(2, slots, cols)),
    ]
    q0, k0, v0, ctx0, att0, picked0, emb = call(
        lambda *refs: attend_own(length, scale, *refs),
        seen + [((rows, width), bf16, cut(block, width))],
        [SMEM, SMEM, cut(block, width), whole(NDATA, width), whole(3, width, cols),
         whole(2, cols), whole(*picks.shape)],
        (info, window_group, tokens_in, data_table, wq0, n_bias, picks),
        [],
        24,
        9 * US,
        6e6,
        grid=steps,
        hbm_in=False,
    )
    if head_count == 2:
        qkv_y, ctx0 = lax.optimization_barrier((qkv_y, ctx0))
        qkv_c = hop(qkv_y, core_bit)
    q1, k1, v1, ctx1, att1, picked1, wq1, picks1 = call(
        lambda *refs: attend_far(length, scale, *refs),
        seen + [((3, width, cols), bf16, whole(3, width, cols)), ((windows, slots), f32, whole(windows, slots))],
        [SMEM, cut(block, width), HBM, HBM],
        (info, emb, qkv_y, qkv_c),
        [
            pltpu.VMEM((extra_rows, cols), bf16),
            pltpu.VMEM((2, cols), f32),
            pltpu.SemaphoreType.DMA((7,)),
        ],
        24,
        9 * US,
        6e6,
        grid=steps,
    )
    if head_count == 2:
        rest_y, ctx1 = lax.optimization_barrier((rest_y, ctx1))
        rest_c = hop(rest_y, core_bit)

    def kinds(x):
        return [jax.ShapeDtypeStruct(x.shape, k) for k in (f32, f32, f32, bf16)]

    few = kinds(first_qkv) + [
        jax.ShapeDtypeStruct(first_out.shape, f32),
        jax.ShapeDtypeStruct((2,) + first_out.shape, f32),
        jax.ShapeDtypeStruct(first_out.shape, bf16),
    ]
    many = kinds(first_up) + kinds(first_down)

    def make_few(gate):
        return blanks_for(gate, few)

    def make_many(gate):
        return blanks_for(gate, many)

    def make_input_grad(gq, gp1):
        return call(
            input_grad,
            [((rows, width), f32, cut(block, width))],
            [cut(block, width)] * 3 + [whole(3, width, cols)] * 2 + [cut(block, width)],
            (gq, gk, gv, wq0, wq1, gp1),
            [],
            24,
            4 * US,
            8e6,
            grid=steps,
        )[0]

    big = rows // 2 if rows // 2 % block == 0 else block
    resid, act, slope, wo, up = call(
        lambda *refs: ff_in(length, *refs),
        [
            ((rows, width), f32, cut(big, width)),
            ((rows, 2 * hid), bf16, cut(big, 2 * hid)),
            ((rows, 2 * hid), bf16, cut(big, 2 * hid)),
            ((2, cols, width), bf16, whole(2, cols, width)),
            ((2, width, hid), bf16, whole(2, width, hid)),
        ],
        [SMEM, SMEM, cut(big, width), whole(NDATA, width), cut(big, cols), cut(big, cols), FAR, HBM, HBM,
         whole(1, hid), whole(2, width), whole(4, width)],
        (info, window_group, tokens_in, data_table, ctx0, ctx1, rest0, rest_y, rest_c,
         n_ff[None], norm_gains, shifts),
        [
            pltpu.VMEM((big, width), f32),
            pltpu.VMEM((2, hid), f32),
            pltpu.VMEM((16, width), bf16),
            pltpu.SemaphoreType.DMA((13,)),
        ],
        40,
        10 * US,
        14e6,
        grid=(rows // big,),
    )
    if head_count == 2:
        down_y, resid = lax.optimization_barrier((down_y, resid))
        down_c = hop(down_y, core_bit)
    output_rows, gp1, ga, keep_one, send_one, sums = call(
        lambda *refs: ff_back(length, *refs),
        [
            ((rows, width), f32, cut(big, width)),
            ((rows, width), f32, cut(big, width)),
            ((rows, width), bf16, cut(big, width)),
            ((2, buf_rows // 2, width), bf16, HBM),
            ((2, buf_rows // 2, width), bf16, HBM),
            ((16, width), f32, whole(16, width)),
        ],
        [SMEM, SMEM, cut(big, width), FAR, cut(big, 2 * hid), whole(2, width, hid), FAR, HBM, HBM,
         whole(2, width), whole(4, width), cut(big, width), whole(rows, cols), whole(rows, cols)],
        (info, window_group, resid, act, slope, up, down0, down_y, down_c,
         norm_gains, shifts, cotangent, ctx0, ctx1),
        [
            pltpu.VMEM((2, hid, width), bf16),
            pltpu.VMEM((rows, 2 * hid), bf16),
            pltpu.VMEM((rows, 2 * hid), bf16),
            pltpu.VMEM((rows, width), bf16),
            pltpu.VMEM((rows, width), bf16),
            pltpu.VMEM((rows, width), bf16),
            pltpu.VMEM((width, rows), bf16),
            pltpu.VMEM((width, rows), bf16),
            pltpu.VMEM((2, buf_rows, width), bf16),
            pltpu.SemaphoreType.DMA((4,)),
            pltpu.SemaphoreType.DMA((rows // big,)),
        ],
        56,
        20 * US,
        20e6,
        grid=(rows // big,),
    )
    if quick:
        state_one = sum_start(info, keep_one, send_one, bits, far, core_bit)
        ga, held = lax.optimization_barrier((ga, state_one[0]))
        state_one = (held, *state_one[1:])
    else:
        sum_one = plus(keep_one, hop(send_one, core_bit))
        sum_one, ga = lax.optimization_barrier((sum_one, ga))
    piece_two = 3 * half // 2 + 16
    gq, gk, gv, keep_two, send_two = call(
        lambda *refs: attend_back(length, scale, *refs),
        [
            ((rows, width), bf16, cut(block, width)),
            ((rows, width), bf16, cut(block, width)),
            ((rows, width), bf16, cut(block, width)),
            ((2, piece_two, width), bf16, HBM),
            ((2, piece_two, width), bf16, HBM),
        ],
        [SMEM, SMEM, cut(block, width), FAR, whole(2, cols, width), whole(16, width),
         whole(*picks.shape), whole(windows, slots), FAR, FAR]
        + [cut(block, cols), cut(block, cols), cut(2, slots, length), cut(2, slots, cols)] * 2,
        (info, window_group, ga, emb, wo, sums, picks, picks1, wq0, wq1,
         k0, v0, att0, picked0, k1, v1, att1, picked1),
        [pltpu.VMEM((rows, width), bf16)] * 4
        + [pltpu.VMEM((3, width, cols), bf16)] * 2
        + [
            pltpu.VMEM((width, rows), bf16),
            pltpu.VMEM((16, width), f32),
            pltpu.VMEM((2, 3 * half + 16, width), bf16),
            pltpu.VMEM((2, 16, width), f32),
            pltpu.SemaphoreType.DMA((11,)),
        ],
        40,
        14 * US,
        10e6,
        grid=steps,
    )
    shards = head_count // 2
    mine = head % shards

    def shard(x, dim):
        n = x.shape[dim] // shards
        return x if shards == 1 else lax.dynamic_slice_in_dim(x, mine * n, n, dim)

    owned = (owner_list == my_rank).astype(jnp.int32)

    rate_wide = width ** (-0.5)
    rate_out = max(width // head_dim, 1) ** (-0.5)
    rate_down = (n_down.shape[0] * 2) ** (-0.5)
    moments_in = (
        weight_qkv, first_qkv, second_qkv, basis_qkv_left, basis_qkv_right,
        weight_out, first_out, second_out, basis_out_left, basis_out_right,
        weight_up, first_up, second_up, basis_up_left, basis_up_right,
        weight_down, first_down, second_down, basis_down_left, basis_down_right,
    )
    if quick:
        held, keep_two, send_two = lax.optimization_barrier((state_one[0], keep_two, send_two))
        beside = (make_many, lambda gate: make_input_grad(lax.optimization_barrier((gq, gate))[0], gp1), make_few)
        mine, other, small, (many, grad_rows, few) = sum_finish(
            info, (held, *state_one[1:]), keep_two, send_two, bits, far, core_bit, beside
        )
        blanks = few + many
        grads = [first_qkv, first_out, first_up, first_down]
        sets = [moments_in[5 * i : 5 * i + 5] for i in range(4)]
        scratch = [pltpu.VMEM((buf_rows + 3 * half, width), bf16)] + [pltpu.VMEM(x.shape, f32) for x in grads]
        for group in sets:
            scratch += [pltpu.VMEM(x.shape, f32) for x in group] + [pltpu.VMEM(group[0].shape, bf16)]
        scratch += [
            pltpu.VMEM((width, width), bf16),
            pltpu.VMEM(basis_qkv_right.shape[1:], bf16),
            pltpu.VMEM(basis_up_right.shape, bf16),
        ]
        temps = [first_qkv.shape[1:], first_out.shape, first_up.shape, first_down.shape]
        scratch += [pltpu.VMEM(x, bf16) for x in temps * 2]
        scratch += [
            pltpu.SemaphoreType.DMA((8,)),
            pltpu.SemaphoreType.DMA((6, 5)),
            pltpu.SemaphoreType.DMA((6, 4)),
        ]
        outs = call(
            lambda *refs: update_all(rate_out, rate_wide, rate_down, cols, hid, *refs),
            [(x.shape, f32, HBM) for x in grads] + [(x.shape, x.dtype, HBM) for x in blanks],
            [SMEM, SMEM] + [HBM] * 2 + [FAR] * (20 + 15),
            (owned, info, mine, other, *moments_in, *blanks),
            scratch,
            60,
            12 * US,
            30e6,
            {24 + i: 4 + i for i in range(15)},
        )
        grad_qkv_all, grad_out_all, grad_up_all, grad_down_all = outs[:4]
        qkv_outs, rest_outs = outs[3:8], outs[5:]
        grad_table_all, grad_gains_all, grad_shifts_all, grad_ff_all, grad_bias_all = small
        grad_ff_all = grad_ff_all.reshape(-1)
    else:
        grad_rows = make_input_grad(gq, gp1)
        blanks = make_few(sums) + make_many(sums)
        early, late = early_steps(bits, far, core_bit), late_steps(16, bits, far, core_bit)
        state_one, state_two = early[0](sum_one), (keep_two, send_two)
        for i in range(1, max(len(early), len(late) + 1)):
            state_one, state_two = lax.optimization_barrier((state_one, state_two))
            if i < len(early):
                state_one = early[i](state_one)
            if i <= len(late):
                state_two = late[i - 1](state_two)
        sum_one, (sum_two, small) = state_one, state_two
        small = small[0]
        g_up = shard(jnp.concatenate([sum_one[:width], sum_one[width : 2 * width]], 1), 1)
        g_down_t = shard(
            jnp.concatenate([sum_one[2 * width : 3 * width], sum_one[3 * width : 4 * width]], 1), 1
        )
        g_out = shard(sum_one[4 * width :], 0)

        def rest_body(*refs):
            update_rest(rate_out, rate_wide, rate_down, *refs)

        tall, wide, low = first_out.shape, first_up.shape, first_down.shape
        rest_outs = call(
            rest_body,
            [(tall, f32, VMEM), (wide, f32, VMEM), (low, f32, VMEM)]
            + [(x.shape, x.dtype, HBM) for x in blanks[4:]],
            [SMEM, VMEM, VMEM, VMEM] + [HBM] * (15 + 11),
            (owned, g_out, g_up, g_down_t,
             weight_out, first_out, second_out, basis_out_left, basis_out_right,
             weight_up, first_up, second_up, basis_up_left, basis_up_right,
             weight_down, first_down, second_down, basis_down_left, basis_down_right, *blanks[4:]),
            [pltpu.VMEM(tall, f32)] * 3
            + [
                pltpu.VMEM(tall, bf16),
                pltpu.VMEM(basis_out_left.shape, f32),
                pltpu.VMEM(basis_out_right.shape, f32),
                pltpu.VMEM(basis_out_right.shape, bf16),
                pltpu.VMEM(tall, bf16),
                pltpu.VMEM(tall, bf16),
            ]
            + [pltpu.VMEM(wide, f32)] * 3
            + [
                pltpu.VMEM(wide, bf16),
                pltpu.VMEM(basis_up_left.shape, f32),
                pltpu.VMEM(basis_up_right.shape, f32),
                pltpu.VMEM(basis_up_left.shape, bf16),
                pltpu.VMEM(basis_up_right.shape, bf16),
                pltpu.VMEM(wide, bf16),
                pltpu.VMEM(wide, bf16),
            ]
            + [pltpu.VMEM(low, f32)] * 3
            + [pltpu.VMEM(low, bf16)] * 3
            + [pltpu.SemaphoreType.DMA((5,))],
            48,
            12 * US,
            20e6,
            {4 + 15 + i: 3 + i for i in range(11)},
        )
        grad_out_all, grad_up_all, grad_down_all = rest_outs[:3]

        pairs = sum_two.reshape(3, half, width)
        g_qkv = shard(jnp.concatenate([pairs[:, :, :cols], pairs[:, :, cols:]], 1), 2)
        small = small.astype(f32)

        def qkv_body(*refs):
            update_qkv(rate_wide, *refs)

        one = first_qkv.shape[1:]
        qkv_outs = call(
            qkv_body,
            [(first_qkv.shape, f32, VMEM)] + [(x.shape, x.dtype, HBM) for x in blanks[:4]],
            [SMEM, VMEM] + [HBM] * 9,
            (owned, g_qkv, weight_qkv, first_qkv, second_qkv, basis_qkv_left, basis_qkv_right, *blanks[:4]),
            [pltpu.VMEM(one, f32)] * 3
            + [
                pltpu.VMEM(one, bf16),
                pltpu.VMEM(basis_qkv_left.shape[1:], f32),
                pltpu.VMEM(basis_qkv_right.shape[1:], f32),
                pltpu.VMEM(basis_qkv_left.shape[1:], bf16),
                pltpu.VMEM(basis_qkv_right.shape[1:], bf16),
                pltpu.VMEM(one, bf16),
                pltpu.VMEM(one, bf16),
                pltpu.SemaphoreType.DMA((5,)),
            ],
            24,
            6 * US,
            8e6,
            {7 + i: 1 + i for i in range(4)},
        )
        grad_qkv_all = qkv_outs[0]
        grad_table_all = small[0:2]
        grad_gains_all = small[2:4]
        grad_shifts_all = small[4:8]
        grad_ff_all = shard(small[8:10].reshape(-1), 0)
        grad_bias_all = shard(small[10].reshape(2, cols), 1)
    return (
        output_rows,
        grad_rows,
        grad_table_all,
        grad_gains_all,
        grad_shifts_all,
        grad_bias_all,
        grad_ff_all,
        grad_qkv_all,
        grad_out_all,
        grad_up_all,
        grad_down_all,
        *(x[None] for x in qkv_outs[1:]),
        *(x[None] for x in rest_outs[3:]),
    )


def solution(mesh):
    in_specs = (
        P(("dp", "head"), None),
        P(("dp", "head"), None),
        P(),
        P("dp"),
        P("dp", "head", None),
        P(),
        P(None, None, "head"),
        P(None, "head"),
        P("head", None),
        P(None, "head"),
        P("head"),
        P("head", None),
        P(),
        P(),
        P(None, None, "head"),
        P(None, None, "head"),
        P("head", None),
        P("head", None),
        P(None, "head"),
        P(None, "head"),
        P("head", None),
        P("head", None),
        P(),
        P(None, "head", None, None),
        P("head", None, None),
        P(),
        P(),
        P("head", None, None),
        P("head", None, None),
        P(),
    )
    out_specs = (
        P(("dp", "head"), None),
        P(("dp", "head"), None),
        P(),
        P(),
        P(),
        P(None, "head"),
        P("head"),
        P(None, None, "head"),
        P("head", None),
        P(None, "head"),
        P("head", None),
        P("dp", None, None, "head"),
        P("dp", None, None, "head"),
        P("dp", None, None, "head"),
        P("dp", None, None, "head"),
        P("dp", "head", None),
        P("dp", None, "head", None),
        P("dp", "head", None),
        P("dp", None, "head"),
        P("dp", None, "head"),
        P("dp", None, "head"),
        P("dp", None, "head"),
        P("dp", "head", None),
        P("dp", "head", None),
        P("dp", "head", None),
        P("dp", "head", None),
    )
    return jax.shard_map(
        per_device, mesh=mesh, in_specs=in_specs, out_specs=out_specs, check_vma=False
    )
```

profile of v0, /device:TPU:0, one launch (start us, length us, event | category | flops | bytes accessed | tf_op | source)
XLA Modules:
  0.0 191.0 jit_solution(6804021303225904036)
XLA Ops:
  0.7 0.8 pad_convert_fusion
  1.6 1.4 copy-done.2
  3.0 0.7 copy-done.12
  3.7 0.7 shard_map.486
  4.4 3.0 %collective-permute-start = (bf16[784,256]{1,0:T(8,128)(2,1)S(1)}, bf16[784,256]{1,0:T(8,128)(2,1)S(1)}, u32[]{:S(2)}, u32[]{:S(2)}) collective-permute-start(bf16[784,256]{1,0:T(8,128)(2,1)S(1)} %get-tuple-element.152), channel_id=1, source_target_pairs={{0,1},{1,0},{2,3},{3,2},{4,5},{5,4},{6,7},{7,6},{8,9},{9,8},{10,11... | collective-permute-start | bytes 1204232 | tf_op jit(solution)/shard_map/ppermute | solution.py:488
  7.5 7.0 %shard_map.487 = (bf16[768,256]{1,0:T(8,128)(2,1)}, bf16[768,256]{1,0:T(8,128)(2,1)}, bf16[768,256]{1,0:T(8,128)(2,1)}, bf16[768,256]{1,0:T(8,128)(2,1)}, f32[8,...) custom-call(s32[7]{0:T(128)S(1)} %stack.28.info.refs_0_.refs_1_, s32[16]{0:T(128)S(1)} %copy-done.14, ...), custom_call_target="tpu_custom_call" | custom-call | flops 8999999488 | bytes 6000000 | tf_op jit(solution)/shard_map/pallas_call | solution.py:67
  14.6 0.9 shard_map.485
  15.5 1.3 collective-permute-done.refs_2_
  16.8 1.7 collective-permute-start.1
  18.5 8.6 %shard_map.488 = (bf16[768,256]{1,0:T(8,128)(2,1)}, bf16[768,256]{1,0:T(8,128)(2,1)}, bf16[768,256]{1,0:T(8,128)(2,1)}, bf16[768,256]{1,0:T(8,128)(2,1)}, f32[8,...) custom-call(s32[7]{0:T(128)S(1)} %stack.28.info.refs_0_.refs_1_, ...), custom_call_target="tpu_custom_call" | custom-call | flops 8999999488 | bytes 6000000 | tf_op jit(solution)/shard_map/pallas_call | solution.py:67
  27.1 7.2 %collective-permute-done.1.refs_7_ = bf16[656,512]{1,0:T(8,128)(2,1)S(1)} collective-permute-done((bf16[656,512]{1,0:T(8,128)(2,1)S(1)}, bf16[656,512]{1,0:T(8,128)(2,1)S(1)}, u32[]{:S(2)}, u32[]{:S(2)}) %collective-permute-start.1) | collective-permute-done | bytes 671776 | tf_op jit(solution)/shard_map/ppermute | solution.py:488
  34.3 1.7 collective-permute-start.2
  36.4 11.9 %shard_map.489 = (f32[768,512]{1,0:T(8,128)}, bf16[768,2048]{1,0:T(8,128)(2,1)}, bf16[768,2048]{1,0:T(8,128)(2,1)}, bf16[2,256,512]{2,1,0:T(8,128)(2,1)}, bf16[2,512,1024]{2,1,0:T(8,128)(2,1)}) custom-call(s32[7]{0:T(128)S(1)} %stack.28.info.refs_0_.refs_1_, s32[16]{0:T(128)S(1)} %copy-done.14, bf16[768,512]{1,0:T(8,128)(2,1)} %refs_2_.5, ...), custom_call_target="tpu_custom_call" | custom-call | flops 10000000000 | bytes 14000000 | tf_op jit(solution)/shard_map/pallas_call | solution.py:67
  48.6 1.9 collective-permute-done.5.refs_8_
  50.5 0.8 copy-done.26
  51.3 21.0 %shard_map.490 = (f32[768,512]{1,0:T(8,128)}, f32[768,512]{1,0:T(8,128)}, bf16[768,512]{1,0:T(8,128)(2,1)}, bf16[2,1152,512]{2,1,0:T(8,128)(2,1)}, bf16[2,1152,512]{2,1,0:T(8,128)(2,1)}, /*index=5*/f32[16,512]{1,0:T(8,128)}) custom-call(s32[7]{0:T(128)} %copy-done.5, s32[16]{0:T(128)} %refs_1_.9, f32[768,512]{1,0:T(8,128)} %get-tuple-element.167.refs_2_, ...), custom_call_target="tpu_custom_call" | custom-call | flops 20000000000 | bytes 20000000 | tf_op jit(solution)/shard_map/pallas_call | solution.py:67
  72.6 4.6 %collective-permute-done.6.got = bf16[2,1152,512]{2,1,0:T(8,128)(2,1)S(1)} collective-permute-done((bf16[2,1152,512]{2,1,0:T(8,128)(2,1)}, bf16[2,1152,512]{2,1,0:T(8,128)(2,1)S(1)}, u32[]{:S(2)}, u32[]{:S(2)}) %collective-permute-start.6) | collective-permute-done | bytes 2359328 | tf_op jit(solution)/shard_map/ppermute | solution.py:488
  77.2 1.7 copy-done.16
  78.9 1.1 shard_map.491
  80.0 1.8 collective-permute-start.7
  81.8 1.5 collective-permute-start.8
  83.3 1.6 collective-permute-start.9
  84.9 16.2 %shard_map.492 = (bf16[768,512]{1,0:T(8,128)(2,1)}, bf16[768,512]{1,0:T(8,128)(2,1)}, bf16[768,512]{1,0:T(8,128)(2,1)}, bf16[2,400,512]{2,1,0:T(8,128)(2,1)}, bf16[2,400,512]{2,1,0:T(8,128)(2,1)}) custom-call(s32[7]{0:T(128)S(1)} %copy-done.6, s32[16]{0:T(128)S(1)} %copy-done.15, bf16[768,512]{1,0:T(8,128)(2,1)} %get-tuple-element.179.refs_2_, ...), custom_call_target="tpu_custom_call" | custom-call | flops 14000000000 | bytes 10000000 | tf_op jit(solution)/shard_map/pallas_call | solution.py:67
  101.1 0.8 shard_map.493
  103.5 6.0 %collective-permute-done.10.got0 = bf16[192,512]{1,0:T(8,128)(2,1)S(1)} collective-permute-done((bf16[192,512]{1,0:T(8,128)(2,1)S(1)}, bf16[192,512]{1,0:T(8,128)(2,1)S(1)}, u32[]{:S(2)}, u32[]{:S(2)}) %collective-permute-start.10) | collective-permute-done | bytes 196640 | tf_op jit(solution)/shard_map/ppermute | solution.py:488
  110.0 0.9 shard_map.494
  111.3 1.6 collective-permute-start.16
  112.9 1.5 collective-permute-start.17
  114.4 1.6 collective-permute-start.14
  116.0 3.0 %collective-permute-done.14.second = bf16[96,512]{1,0:T(8,128)(2,1)S(1)} collective-permute-done((bf16[96,512]{1,0:T(8,128)(2,1)S(1)}, bf16[96,512]{1,0:T(8,128)(2,1)S(1)}, u32[]{:S(2)}, u32[]{:S(2)}) %collective-permute-start.14) | collective-permute-done | bytes 98336 | tf_op jit(solution)/shard_map/ppermute | solution.py:488
  119.0 6.2 %collective-permute-done.17.both = bf16[208,512]{1,0:T(8,128)(2,1)S(1)} collective-permute-done((bf16[208,512]{1,0:T(8,128)(2,1)S(1)}, bf16[208,512]{1,0:T(8,128)(2,1)S(1)}, u32[]{:S(2)}, u32[]{:S(2)}) %collective-permute-start.17) | collective-permute-done | bytes 213024 | tf_op jit(solution)/shard_map/ppermute | solution.py:488
  125.3 1.5 shard_map.495
  126.8 1.3 collective-permute-start.18
  128.1 2.7 %collective-permute-start.20 = (bf16[64,512]{1,0:T(8,128)(2,1)S(1)}, bf16[64,512]{1,0:T(8,128)(2,1)S(1)}, u32[]{:S(2)}, u32[]{:S(2)}) collective-permute-start(bf16[64,512]{1,0:T(8,128)(2,1)S(1)} %get-tuple-element.222), channel_id=1, source_target_pairs={{0,24},{1,25},{2,26},{3,27},{4,28},{5,29},{6,30},{7,31},{8,16},{9,... | collective-permute-start | bytes 196616 | tf_op jit(solution)/shard_map/ppermute | solution.py:488
  130.8 5.3 %shard_map.496 = (f32[512,1024]{1,0:T(8,128)}, f32[512,1024]{1,0:T(8,128)}, f32[512,1024]{1,0:T(8,128)}, bf16[512,1024]{1,0:T(8,128)(2,1)}, f32[1024,512]{1,0:T(...) custom-call(bf16[288,512]{1,0:T(8,128)(2,1)S(1)} %get-tuple-element.218.refs_0_.part), custom_call_target="tpu_custom_call" | custom-call | flops 5000000000 | bytes 14000000 | tf_op jit(solution)/shard_map/pallas_call | solution.py:67
  136.2 12.2 %collective-permute-done.19.third = bf16[352,512]{1,0:T(8,128)(2,1)S(1)} collective-permute-done((bf16[352,512]{1,0:T(8,128)(2,1)S(1)}, bf16[352,512]{1,0:T(8,128)(2,1)S(1)}, u32[]{:S(2)}, u32[]{:S(2)}) %collective-permute-start.19) | collective-permute-done | bytes 360480 | tf_op jit(solution)/shard_map/ppermute | solution.py:488
  149.0 1.5 collective-permute-start.22
  150.5 3.7 %collective-permute-done.22.got1 = bf16[144,512]{1,0:T(8,128)(2,1)S(1)} collective-permute-done((bf16[144,512]{1,0:T(8,128)(2,1)S(1)}, bf16[144,512]{1,0:T(8,128)(2,1)S(1)}, u32[]{:S(2)}, u32[]{:S(2)}) %collective-permute-start.22) | collective-permute-done | bytes 147488 | tf_op jit(solution)/shard_map/ppermute | solution.py:488
  154.1 1.0 collective-permute-done.21.got2
  155.8 1.5 collective-permute-start.23
  157.3 1.4 collective-permute-start.26
  158.8 1.0 collective-permute-start.25
  159.8 1.9 %collective-permute-start.24 = (bf16[288,512]{1,0:T(8,128)(2,1)S(1)}, bf16[288,512]{1,0:T(8,128)(2,1)S(1)}, u32[]{:S(2)}, u32[]{:S(2)}) collective-permute-start(bf16[288,512]{1,0:T(8,128)(2,1)S(1)} %get-tuple-element.239.near2), channel_id=1, source_target_pairs={{0,8},{1,9},{2,10},{3,11},{4,12},{5,13},{6,14},{7,15},{8,0},{9,1},... | collective-permute-start | bytes 884744 | tf_op jit(solution)/shard_map/ppermute | solution.py:488
  161.7 6.1 %shard_map.499 = f32[768,512]{1,0:T(8,128)} custom-call(bf16[768,512]{1,0:T(8,128)(2,1)} %get-tuple-element.228.gq, bf16[768,512]{1,0:T(8,128)(2,1)} %get-tuple-element.229.gk, bf16[768,512]{1,0:T(8,128)(2,1)} %get-tuple-element.230.gv, bf16[3,512,256]{2,1,0:T(8,128)(2,1)} %copy-done.18, bf16[3,512,256]{2,1,0:T(8,128)(2,1)} %get-tuple-element.183.refs_9_.wq1, ...), custom_call_target="tpu_custom_call" | custom-call | flops 4000000000 | bytes 8000000 | tf_op jit(solution)/shard_map/pallas_call | solution.py:67
  167.8 2.1 %collective-permute-done.24.got2 = bf16[288,512]{1,0:T(8,128)(2,1)S(1)} collective-permute-done((bf16[288,512]{1,0:T(8,128)(2,1)S(1)}, bf16[288,512]{1,0:T(8,128)(2,1)S(1)}, u32[]{:S(2)}, u32[]{:S(2)}) %collective-permute-start.24) | collective-permute-done | bytes 294944 | tf_op jit(solution)/shard_map/ppermute | solution.py:488
  171.3 3.0 %shard_map.501 = (f32[1536,256]{1,0:T(8,128)}, f32[1536,256]{1,0:T(8,128)}, f32[1536,256]{1,0:T(8,128)}, bf16[1536,256]{1,0:T(8,128)(2,1)}, f32[256,512]{1,0:T(8...) custom-call(bf16[1536,512]{1,0:T(8,128)(2,1)S(1)} %shard_map.500.refs_0_.refs_2_), custom_call_target="tpu_custom_call" | custom-call | flops 5000000000 | bytes 14000000 | tf_op jit(solution)/shard_map/pallas_call | solution.py:67
  174.3 1.1 copy-done.23
  175.5 15.3 %shard_map.502 = (f32[3,512,256]{2,1,0:T(8,128)}, f32[256,512]{1,0:T(8,128)}, f32[512,1024]{1,0:T(8,128)}, f32[1024,512]{1,0:T(8,128)}, f32[3,512,256]{2,1,0:T(8...) custom-call(s32[6]{0:T(128)} %compare_convert_fusion.refs_0_, ...), custom_call_target="tpu_custom_call", output_to_operand_aliasing={{4}: (24, {}), {5}: (25, {}), {6}: (26, {}), {7}: (27, {}),... | custom-call | flops 12000000000 | bytes 30000000 | tf_op jit(solution)/shard_map/pallas_call | solution.py:67
  (86 shorter events, 6.2 us)
Async XLA Ops:
  3.7 32.7 %copy-start.5 = (s32[7]{0:T(128)}, s32[7]{0:T(128)S(1)}, u32[]{:S(2)}) copy-start(s32[7]{0:T(128)S(1)} %stack.28.info.refs_0_.refs_1_) | copy-start | bytes 88
  3.7 3.8 %copy-start.7 = (bf16[768,512]{1,0:T(8,128)(2,1)S(1)}, bf16[768,512]{1,0:T(8,128)(2,1)}, u32[]{:S(2)}) copy-start(bf16[768,512]{1,0:T(8,128)(2,1)} %refs_2_.5) | copy-start | bytes 2359300
  3.7 3.8 %copy-start.9 = (f32[2,512]{1,0:T(2,128)S(1)}, f32[2,512]{1,0:T(2,128)}, u32[]{:S(2)}) copy-start(f32[2,512]{1,0:T(2,128)} %refs_3_.3) | copy-start | bytes 12292
  3.7 3.8 %copy-start.13 = (f32[2,256]{1,0:T(2,128)S(1)}, f32[2,256]{1,0:T(2,128)}, u32[]{:S(2)}) copy-start(f32[2,256]{1,0:T(2,128)} %refs_5_.2) | copy-start | bytes 6148
  3.7 3.8 %copy-start.14 = (s32[16]{0:T(128)S(1)}, s32[16]{0:T(128)}, u32[]{:S(2)}) copy-start(s32[16]{0:T(128)} %refs_1_.9) | copy-start | bytes 196
  4.4 10.1 %copy-start.18 = (bf16[3,512,256]{2,1,0:T(8,128)(2,1)}, bf16[3,512,256]{2,1,0:T(8,128)(2,1)S(1)}, u32[]{:S(2)}) copy-start(bf16[3,512,256]{2,1,0:T(8,128)(2,1)S(1)} %get-tuple-element.156.refs_4_.refs_8_.wq0) | copy-start | bytes 2359300
  4.4 12.3 %collective-permute-start = (bf16[784,256]{1,0:T(8,128)(2,1)S(1)}, bf16[784,256]{1,0:T(8,128)(2,1)S(1)}, u32[]{:S(2)}, u32[]{:S(2)}) collective-permute-start(bf16[784,256]{1,0:T(8,128)(2,1)S(1)} %get-tuple-element.152), channel_id=1, source_target_pairs={{0,1},{1,0},{2,3},{3,2},{4,5},{5,4},{6,7},{7,6},{8,9},{9,8},{10,11... | collective-permute-start | bytes 1204232 | tf_op jit(solution)/shard_map/ppermute | solution.py:488
  7.5 7.1 %copy-start = (f32[512,1024]{1,0:T(8,128)S(1)}, f32[512,1024]{1,0:T(8,128)}, u32[]{:S(2)}) copy-start(f32[512,1024]{1,0:T(8,128)} %refs_14_.1) | copy-start | bytes 6291460
  7.5 7.1 %copy-start.1 = (f32[1024,512]{1,0:T(8,128)S(1)}, f32[1024,512]{1,0:T(8,128)}, u32[]{:S(2)}) copy-start(f32[1024,512]{1,0:T(8,128)} %refs_19_.1) | copy-start | bytes 6291460
  7.5 7.1 %copy-start.4 = (f32[256,512]{1,0:T(8,128)S(1)}, f32[256,512]{1,0:T(8,128)}, u32[]{:S(2)}) copy-start(f32[256,512]{1,0:T(8,128)} %refs_9_.3) | copy-start | bytes 1572868
  7.5 7.1 %copy-start.10 = (f32[1024]{0:T(1024)S(1)}, f32[1024]{0:T(1024)}, u32[]{:S(2)}) copy-start(f32[1024]{0:T(1024)} %param.40) | copy-start | bytes 12292
  15.5 11.6 %copy-start.19 = (bf16[2,656,512]{2,1,0:T(8,128)(2,1)}, bf16[2,656,512]{2,1,0:T(8,128)(2,1)S(1)}, u32[]{:S(2)}) copy-start(bf16[2,656,512]{2,1,0:T(8,128)(2,1)S(1)} %get-tuple-element.164.refs_6_) | copy-start | bytes 4030468
  15.5 11.6 %copy-start.20 = (bf16[1024,512]{1,0:T(8,128)(2,1)}, bf16[1024,512]{1,0:T(8,128)(2,1)S(1)}, u32[]{:S(2)}) copy-start(bf16[1024,512]{1,0:T(8,128)(2,1)S(1)} %get-tuple-element.171.refs_6_) | copy-start | bytes 3145732
  16.8 1.7 collective-permute-start.3
  16.8 17.5 %collective-permute-start.1 = (bf16[656,512]{1,0:T(8,128)(2,1)S(1)}, bf16[656,512]{1,0:T(8,128)(2,1)S(1)}, u32[]{:S(2)}, u32[]{:S(2)}) collective-permute-start(bf16[656,512]{1,0:T(8,128)(2,1)S(1)} %get-tuple-element.153), channel_id=1, source_target_pairs={{0,1},{1,0},{2,3},{3,2},{4,5},{5,4},{6,7},{7,6},{8,9},{9,8},{10,11... | collective-permute-start | bytes 2015240 | tf_op jit(solution)/shard_map/ppermute | solution.py:488
  18.5 17.9 %copy-start.8 = (f32[4,512]{1,0:T(4,128)S(1)}, f32[4,512]{1,0:T(4,128)}, u32[]{:S(2)}) copy-start(f32[4,512]{1,0:T(4,128)} %refs_10_.4) | copy-start | bytes 24580
  18.5 17.9 %copy-start.11 = (f32[2,512]{1,0:T(2,128)S(1)}, f32[2,512]{1,0:T(2,128)}, u32[]{:S(2)}) copy-start(f32[2,512]{1,0:T(2,128)} %refs_9_.2) | copy-start | bytes 12292
  34.3 2.1 %collective-permute-start.4 = (bf16[656,512]{1,0:T(8,128)(2,1)S(1)}, bf16[656,512]{1,0:T(8,128)(2,1)S(1)}, u32[]{:S(2)}, u32[]{:S(2)}) collective-permute-start(bf16[656,512]{1,0:T(8,128)(2,1)S(1)} %collective-permute-done.1.refs_7_), channel_id=1, source_target_pairs={{0,2},{1,3},{2,0},{3,1},{4,6},{5,7},{6,4},{7,5},{8,10},{9,11},{10,... | collective-permute-start | bytes 2015240 | tf_op jit(solution)/shard_map/ppermute | solution.py:488
  34.3 14.3 %collective-permute-start.2 = (bf16[512,512]{1,0:T(8,128)(2,1)S(1)}, bf16[512,512]{1,0:T(8,128)(2,1)S(1)}, u32[]{:S(2)}, u32[]{:S(2)}) collective-permute-start(bf16[512,512]{1,0:T(8,128)(2,1)S(1)} %get-tuple-element.154), channel_id=1, source_target_pairs={{0,1},{1,0},{2,3},{3,2},{4,5},{5,4},{6,7},{7,6},{8,9},{9,8},{10,11... | collective-permute-start | bytes 1572872 | tf_op jit(solution)/shard_map/ppermute | solution.py:488
  48.6 1.9 %collective-permute-start.5 = (bf16[512,512]{1,0:T(8,128)(2,1)S(1)}, bf16[512,512]{1,0:T(8,128)(2,1)S(1)}, u32[]{:S(2)}, u32[]{:S(2)}) collective-permute-start(bf16[512,512]{1,0:T(8,128)(2,1)S(1)} %collective-permute-done.2.refs_7_), channel_id=1, source_target_pairs={{0,2},{1,3},{2,0},{3,1},{4,6},{5,7},{6,4},{7,5},{8,10},{9,11},{10,... | collective-permute-start | bytes 1572872 | tf_op jit(solution)/shard_map/ppermute | solution.py:488
  51.3 25.9 %copy-start.6 = (s32[7]{0:T(128)S(1)}, s32[7]{0:T(128)}, u32[]{:S(2)}) copy-start(s32[7]{0:T(128)} %copy-done.5) | copy-start | bytes 88
  72.4 4.8 %collective-permute-start.6 = (bf16[2,1152,512]{2,1,0:T(8,128)(2,1)}, bf16[2,1152,512]{2,1,0:T(8,128)(2,1)S(1)}, u32[]{:S(2)}, u32[]{:S(2)}) collective-permute-start(bf16[2,1152,512]{2,1,0:T(8,128)(2,1)} %get-tuple-element.176), channel_id=1, source_target_pairs={{0,2},{1,3},{2,0},{3,1},{4,6},{5,7},{6,4},{7,5},{8,10},{9,11},{10,... | collective-permute-start | bytes 7077896 | tf_op jit(solution)/shard_map/ppermute | solution.py:488
  78.8 6.0 %copy-start.15 = (s32[16]{0:T(128)S(1)}, s32[16]{0:T(128)}, u32[]{:S(2)}) copy-start(s32[16]{0:T(128)} %refs_1_.9) | copy-start | bytes 196
  78.8 6.0 %copy-start.21 = (f32[16,512]{1,0:T(8,128)S(1)}, f32[16,512]{1,0:T(8,128)}, u32[]{:S(2)}) copy-start(f32[16,512]{1,0:T(8,128)} %get-tuple-element.181.refs_5_) | copy-start | bytes 98308
  78.8 6.0 %copy-start.22 = (f32[8,128]{1,0:T(8,128)S(1)}, f32[8,128]{1,0:T(8,128)}, u32[]{:S(2)}) copy-start(f32[8,128]{1,0:T(8,128)} %get-tuple-element.182.refs_7_) | copy-start | bytes 12292
  80.0 21.0 %collective-permute-start.7 = (bf16[384,512]{1,0:T(8,128)(2,1)S(1)}, bf16[384,512]{1,0:T(8,128)(2,1)S(1)}, u32[]{:S(2)}, u32[]{:S(2)}) collective-permute-start(bf16[384,512]{1,0:T(8,128)(2,1)S(1)} %get-tuple-element.195), channel_id=1, source_target_pairs={{0,1},{1,0},{2,3},{3,2},{4,5},{5,4},{6,7},{7,6},{8,9},{9,8},{10,11... | collective-permute-start | bytes 1179656 | tf_op jit(solution)/shard_map/ppermute | solution.py:488
  81.8 19.2 %collective-permute-start.8 = (bf16[2,192,512]{2,1,0:T(8,128)(2,1)S(1)}, bf16[2,192,512]{2,1,0:T(8,128)(2,1)S(1)}, u32[]{:S(2)}, u32[]{:S(2)}) collective-permute-start(bf16[2,192,512]{2,1,0:T(8,128)(2,1)S(1)} %get-tuple-element.197), channel_id=1, source_target_pairs={{0,4},{1,5},{2,6},{3,7},{4,0},{5,1},{6,2},{7,3},{8,12},{9,13},{10,... | collective-permute-start | bytes 1179656 | tf_op jit(solution)/shard_map/ppermute | solution.py:488
  83.3 17.8 %collective-permute-start.9 = (bf16[2,192,512]{2,1,0:T(8,128)(2,1)S(1)}, bf16[2,192,512]{2,1,0:T(8,128)(2,1)S(1)}, u32[]{:S(2)}, u32[]{:S(2)}) collective-permute-start(bf16[2,192,512]{2,1,0:T(8,128)(2,1)S(1)} %get-tuple-element.199), channel_id=1, source_target_pairs={{0,8},{1,9},{2,10},{3,11},{4,12},{5,13},{6,14},{7,15},{8,0},{9,1},... | collective-permute-start | bytes 1179656 | tf_op jit(solution)/shard_map/ppermute | solution.py:488
  101.1 8.9 %copy-start.17 = (bf16[2,400,512]{2,1,0:T(8,128)(2,1)S(1)}, bf16[2,400,512]{2,1,0:T(8,128)(2,1)}, u32[]{:S(2)}) copy-start(bf16[2,400,512]{2,1,0:T(8,128)(2,1)} %get-tuple-element.208.keep) | copy-start | bytes 2457604
  102.2 7.8 %collective-permute-start.13 = (bf16[2,400,512]{2,1,0:T(8,128)(2,1)S(1)}, bf16[2,400,512]{2,1,0:T(8,128)(2,1)S(1)}, u32[]{:S(2)}, u32[]{:S(2)}) collective-permute-start(bf16[2,400,512]{2,1,0:T(8,128)(2,1)S(1)} %copy-done.24), channel_id=1, source_target_pairs={{0,2},{1,3},{2,0},{3,1},{4,6},{5,7},{6,4},{7,5},{8,10},{9,11},{10,... | collective-permute-start | bytes 2457608 | tf_op jit(solution)/shard_map/ppermute | solution.py:488
  102.2 7.3 %collective-permute-start.10 = (bf16[192,512]{1,0:T(8,128)(2,1)S(1)}, bf16[192,512]{1,0:T(8,128)(2,1)S(1)}, u32[]{:S(2)}, u32[]{:S(2)}) collective-permute-start(bf16[192,512]{1,0:T(8,128)(2,1)S(1)} %get-tuple-element.203), channel_id=1, source_target_pairs={{0,4},{1,5},{2,6},{3,7},{4,0},{5,1},{6,2},{7,3},{8,12},{9,13},{10,... | collective-permute-start | bytes 589832 | tf_op jit(solution)/shard_map/ppermute | solution.py:488
  102.7 7.0 %collective-permute-start.11 = (bf16[2,96,512]{2,1,0:T(8,128)(2,1)S(1)}, bf16[2,96,512]{2,1,0:T(8,128)(2,1)S(1)}, u32[]{:S(2)}, u32[]{:S(2)}) collective-permute-start(bf16[2,96,512]{2,1,0:T(8,128)(2,1)S(1)} %get-tuple-element.205), channel_id=1, source_target_pairs={{0,8},{1,9},{2,10},{3,11},{4,12},{5,13},{6,14},{7,15},{8,0},{9,1},... | collective-permute-start | bytes 589832 | tf_op jit(solution)/shard_map/ppermute | solution.py:488
  103.2 6.8 %collective-permute-start.12 = (bf16[192,512]{1,0:T(8,128)(2,1)S(1)}, bf16[192,512]{1,0:T(8,128)(2,1)S(1)}, u32[]{:S(2)}, u32[]{:S(2)}) collective-permute-start(bf16[192,512]{1,0:T(8,128)(2,1)S(1)} %get-tuple-element.207), channel_id=1, source_target_pairs={{0,1},{1,0},{2,3},{3,2},{4,5},{5,4},{6,7},{7,6},{8,9},{9,8},{10,11... | collective-permute-start | bytes 589832 | tf_op jit(solution)/shard_map/ppermute | solution.py:488
  110.9 14.4 %collective-permute-start.15 = (bf16[304,512]{1,0:T(8,128)(2,1)S(1)}, bf16[304,512]{1,0:T(8,128)(2,1)S(1)}, u32[]{:S(2)}, u32[]{:S(2)}) collective-permute-start(bf16[304,512]{1,0:T(8,128)(2,1)S(1)} %get-tuple-element.213), channel_id=1, source_target_pairs={{0,1},{1,0},{2,3},{3,2},{4,5},{5,4},{6,7},{7,6},{8,9},{9,8},{10,11... | collective-permute-start | bytes 933896 | tf_op jit(solution)/shard_map/ppermute | solution.py:488
  111.3 14.0 %collective-permute-start.16 = (bf16[304,512]{1,0:T(8,128)(2,1)S(1)}, bf16[304,512]{1,0:T(8,128)(2,1)S(1)}, u32[]{:S(2)}, u32[]{:S(2)}) collective-permute-start(bf16[304,512]{1,0:T(8,128)(2,1)S(1)} %get-tuple-element.214), channel_id=1, source_target_pairs={{0,4},{1,5},{2,6},{3,7},{4,0},{5,1},{6,2},{7,3},{8,12},{9,13},{10,... | collective-permute-start | bytes 933896 | tf_op jit(solution)/shard_map/ppermute | solution.py:488
  112.9 12.3 %collective-permute-start.17 = (bf16[208,512]{1,0:T(8,128)(2,1)S(1)}, bf16[208,512]{1,0:T(8,128)(2,1)S(1)}, u32[]{:S(2)}, u32[]{:S(2)}) collective-permute-start(bf16[208,512]{1,0:T(8,128)(2,1)S(1)} %get-tuple-element.215), channel_id=1, source_target_pairs={{0,5},{1,4},{2,7},{3,6},{4,1},{5,0},{6,3},{7,2},{8,13},{9,12},{10,... | collective-permute-start | bytes 638984 | tf_op jit(solution)/shard_map/ppermute | solution.py:488
  114.4 4.6 %collective-permute-start.14 = (bf16[96,512]{1,0:T(8,128)(2,1)S(1)}, bf16[96,512]{1,0:T(8,128)(2,1)S(1)}, u32[]{:S(2)}, u32[]{:S(2)}) collective-permute-start(bf16[96,512]{1,0:T(8,128)(2,1)S(1)} %get-tuple-element.212), channel_id=1, source_target_pairs={{0,8},{1,9},{2,10},{3,11},{4,12},{5,13},{6,14},{7,15},{8,0},{9,1},... | collective-permute-start | bytes 294920 | tf_op jit(solution)/shard_map/ppermute | solution.py:488
  126.8 9.4 %collective-permute-start.18 = (bf16[64,512]{1,0:T(8,128)(2,1)S(1)}, bf16[64,512]{1,0:T(8,128)(2,1)S(1)}, u32[]{:S(2)}, u32[]{:S(2)}) collective-permute-start(bf16[64,512]{1,0:T(8,128)(2,1)S(1)} %get-tuple-element.220), channel_id=1, source_target_pairs={{0,8},{1,9},{2,10},{3,11},{4,12},{5,13},{6,14},{7,15},{8,0},{9,1},... | collective-permute-start | bytes 196616 | tf_op jit(solution)/shard_map/ppermute | solution.py:488
  128.1 8.1 %collective-permute-start.20 = (bf16[64,512]{1,0:T(8,128)(2,1)S(1)}, bf16[64,512]{1,0:T(8,128)(2,1)S(1)}, u32[]{:S(2)}, u32[]{:S(2)}) collective-permute-start(bf16[64,512]{1,0:T(8,128)(2,1)S(1)} %get-tuple-element.222), channel_id=1, source_target_pairs={{0,24},{1,25},{2,26},{3,27},{4,28},{5,29},{6,30},{7,31},{8,16},{9,... | collective-permute-start | bytes 196616 | tf_op jit(solution)/shard_map/ppermute | solution.py:488
  130.8 17.6 %collective-permute-start.19 = (bf16[352,512]{1,0:T(8,128)(2,1)S(1)}, bf16[352,512]{1,0:T(8,128)(2,1)S(1)}, u32[]{:S(2)}, u32[]{:S(2)}) collective-permute-start(bf16[352,512]{1,0:T(8,128)(2,1)S(1)} %get-tuple-element.221), channel_id=1, source_target_pairs={{0,16},{1,17},{2,18},{3,19},{4,20},{5,21},{6,22},{7,23},{8,24},{9,... | collective-permute-start | bytes 1081352 | tf_op jit(solution)/shard_map/ppermute | solution.py:488
  149.0 6.2 %collective-permute-start.21 = (bf16[192,512]{1,0:T(8,128)(2,1)S(1)}, bf16[192,512]{1,0:T(8,128)(2,1)S(1)}, u32[]{:S(2)}, u32[]{:S(2)}) collective-permute-start(bf16[192,512]{1,0:T(8,128)(2,1)S(1)} %get-tuple-element.223.near2), channel_id=1, source_target_pairs={{0,8},{1,9},{2,10},{3,11},{4,12},{5,13},{6,14},{7,15},{8,0},{9,1},... | collective-permute-start | bytes 589832 | tf_op jit(solution)/shard_map/ppermute | solution.py:488
  149.0 5.1 %collective-permute-start.22 = (bf16[144,512]{1,0:T(8,128)(2,1)S(1)}, bf16[144,512]{1,0:T(8,128)(2,1)S(1)}, u32[]{:S(2)}, u32[]{:S(2)}) collective-permute-start(bf16[144,512]{1,0:T(8,128)(2,1)S(1)} %get-tuple-element.224.near1), channel_id=1, source_target_pairs={{0,4},{1,5},{2,6},{3,7},{4,0},{5,1},{6,2},{7,3},{8,12},{9,13},{10,... | collective-permute-start | bytes 442376 | tf_op jit(solution)/shard_map/ppermute | solution.py:488
  155.8 14.1 %collective-permute-start.23 = (bf16[384,512]{1,0:T(8,128)(2,1)S(1)}, bf16[384,512]{1,0:T(8,128)(2,1)S(1)}, u32[]{:S(2)}, u32[]{:S(2)}) collective-permute-start(bf16[384,512]{1,0:T(8,128)(2,1)S(1)} %get-tuple-element.238.near1), channel_id=1, source_target_pairs={{0,4},{1,5},{2,6},{3,7},{4,0},{5,1},{6,2},{7,3},{8,12},{9,13},{10,... | collective-permute-start | bytes 1179656 | tf_op jit(solution)/shard_map/ppermute | solution.py:488
  157.3 10.5 %collective-permute-start.26 = (bf16[96,512]{1,0:T(8,128)(2,1)S(1)}, bf16[96,512]{1,0:T(8,128)(2,1)S(1)}, u32[]{:S(2)}, u32[]{:S(2)}) collective-permute-start(bf16[96,512]{1,0:T(8,128)(2,1)S(1)} %get-tuple-element.227.near3), channel_id=1, source_target_pairs={{0,24},{1,25},{2,26},{3,27},{4,28},{5,29},{6,30},{7,31},{8,16},{9,... | collective-permute-start | bytes 294920 | tf_op jit(solution)/shard_map/ppermute | solution.py:488
  158.8 9.0 %collective-permute-start.25 = (bf16[96,512]{1,0:T(8,128)(2,1)S(1)}, bf16[96,512]{1,0:T(8,128)(2,1)S(1)}, u32[]{:S(2)}, u32[]{:S(2)}) collective-permute-start(bf16[96,512]{1,0:T(8,128)(2,1)S(1)} %get-tuple-element.227.near3), channel_id=1, source_target_pairs={{0,16},{1,17},{2,18},{3,19},{4,20},{5,21},{6,22},{7,23},{8,24},{9,... | collective-permute-start | bytes 294920 | tf_op jit(solution)/shard_map/ppermute | solution.py:488
  159.8 10.1 %collective-permute-start.24 = (bf16[288,512]{1,0:T(8,128)(2,1)S(1)}, bf16[288,512]{1,0:T(8,128)(2,1)S(1)}, u32[]{:S(2)}, u32[]{:S(2)}) collective-permute-start(bf16[288,512]{1,0:T(8,128)(2,1)S(1)} %get-tuple-element.239.near2), channel_id=1, source_target_pairs={{0,8},{1,9},{2,10},{3,11},{4,12},{5,13},{6,14},{7,15},{8,0},{9,1},... | collective-permute-start | bytes 884744 | tf_op jit(solution)/shard_map/ppermute | solution.py:488
  170.6 3.8 %copy-start.3 = (bf16[1536,512]{1,0:T(8,128)(2,1)}, bf16[1536,512]{1,0:T(8,128)(2,1)S(1)}, u32[]{:S(2)}) copy-start(bf16[1536,512]{1,0:T(8,128)(2,1)S(1)} %shard_map.500.refs_0_.refs_2_) | copy-start | bytes 4718596
  170.6 3.8 %collective-permute-start.27 = (bf16[1536,512]{1,0:T(8,128)(2,1)S(1)}, bf16[1536,512]{1,0:T(8,128)(2,1)S(1)}, u32[]{:S(2)}, u32[]{:S(2)}) collective-permute-start(bf16[1536,512]{1,0:T(8,128)(2,1)S(1)} %shard_map.500.refs_0_.refs_2_), channel_id=1, source_target_pairs={{0,2},{1,3},{2,0},{3,1},{4,6},{5,7},{6,4},{7,5},{8,10},{9,11},{10,... | collective-permute-start | bytes 4718600 | tf_op jit(solution)/shard_map/ppermute | solution.py:488
  (8 other events, 11.6 us)
where the time goes:
time: 188 us; the launch traced here: 191 us
  Pallas kernels  102 us (54%)
  waiting for transfers between devices  50.4 us (27%)
  starting transfers between devices  29.5 us (16%)
  local copies, waits for them, and re-layouts  6.26 us (3%)
    pallas_call x18, Pallas kernels, call(): pl.pallas_call(body, grid=grid, out_shape=tuple((kind(s, d) for s, d, _ i...  102 us
    ppermute x28, waiting for transfers between devices, hop(): lax.ppermute(x, ('dp', 'head'), [(i, i ^ flip) for i in range(count)])  50.4 us
    ppermute x28, starting transfers between devices, hop(): lax.ppermute(x, ('dp', 'head'), [(i, i ^ flip) for i in range(count)])  29.5 us
    unnamed x56, local copies, waits for them, and re-layouts  6.09 us
  transfers between devices with their start and end apart: 28, of which 15 were waited for; matrix products, arithmetic and copies ran while one was open for 0% of the time, Pallas kernels for 31%

commit v1 on v0

v1 whole, which is shorter than its diff:
```python
import math

import jax
import jax.numpy as jnp
from jax import lax
from jax.experimental import pallas as pl
from jax.experimental.pallas import tpu as pltpu
from jax.sharding import PartitionSpec as P

f32 = jnp.float32
bf16 = jnp.bfloat16

NDATA = 2
EPS_NORM = 1e-05
EPS_ADAM = 1e-08
BETA_ONE = 0.5
BETA_TWO = 0.5

GROUP = 4
SLOTS = 32
MB = 1 << 20


def nn(a, b):
    return jnp.dot(a, b, preferred_element_type=f32)


def nt(a, b):
    return lax.dot_general(a, b, (((1,), (1,)), ((), ())), preferred_element_type=f32)


def col_sum(x):
    return jnp.sum(x, axis=0, keepdims=True)


def row_mean(x):
    return jnp.mean(x, axis=-1, keepdims=True)


VMEM = pl.BlockSpec(memory_space=pltpu.VMEM)
SMEM = pl.BlockSpec(memory_space=pltpu.SMEM)
HBM = pl.BlockSpec(memory_space=pl.ANY)
FAR = pl.BlockSpec(memory_space=pl.ANY)


def whole(*shape):
    return pl.BlockSpec(shape, lambda i: (0,) * len(shape))


def cut(*shape):
    return pl.BlockSpec(shape, lambda i: (i,) + (0,) * (len(shape) - 1))


US = 1_000_000_000


def in_hbm(x, spec):
    if spec is SMEM or spec is HBM or x.size * x.dtype.itemsize < 1 << 16:
        return x
    return pltpu.with_memory_space_constraint(x, pltpu.HBM)


def call(body, outs, ins, args, scratch, limit, flops, nbytes, aliases={}, grid=(), hbm_in=True, hbm_out=True):
    if hbm_in:
        args = [in_hbm(x, spec) for x, spec in zip(args, ins)]
    kind = pltpu.HBM if hbm_out else jax.ShapeDtypeStruct
    return pl.pallas_call(
        body,
        grid=grid,
        out_shape=tuple(kind(s, d) for s, d, _ in outs),
        in_specs=ins,
        out_specs=tuple(spec for _, _, spec in outs),
        scratch_shapes=scratch,
        input_output_aliases=aliases,
        compiler_params=pltpu.CompilerParams(vmem_limit_bytes=limit * MB),
        cost_estimate=pl.CostEstimate(
            flops=int(flops), bytes_accessed=int(nbytes), transcendentals=0
        ),
    )(*args)


def head_mask(cols):
    width = cols // GROUP
    shape = (GROUP * SLOTS, cols)
    return (
        lax.broadcasted_iota(jnp.int32, shape, 0) // SLOTS
        == lax.broadcasted_iota(jnp.int32, shape, 1) // width
    )


def one_hot(picks, w, length):
    row = picks[pl.ds(w, 1), :]
    spots = lax.broadcasted_iota(jnp.int32, (length, GROUP * SLOTS), 0).astype(f32)
    columns = (spots == row).astype(f32)
    return columns.astype(bf16), columns.T.astype(bf16)


def copy_all(pairs, sems):
    copies = [pltpu.make_async_copy(a, b, sems.at[i]) for i, (a, b) in enumerate(pairs)]
    for copy in copies:
        copy.start()
    return copies


def split_sum(parts, at):
    return parts[at : at + 1] + parts[at + 1 : at + 2] + parts[at + 2 : at + 3]


def put_parts(extra, at, row):
    for i in range(3):
        part = row.astype(bf16).astype(f32)
        extra[at + i : at + i + 1, :] = part
        row = row - part


def pack_qkv(windows, info, w, bias, picks, piece, part, extra, sems):
    n = part.shape[1]
    rows = pl.ds(pl.multiple_of(info[7] * n, n), n)
    copies = copy_all([(w.at[j, rows, :], part.at[j]) for j in range(3)], sems)
    extra[...] = jnp.zeros_like(extra)
    for i in range(windows):
        extra[i : i + 1, : GROUP * SLOTS] = picks[pl.ds(info[2] + i, 1), :]
    put_parts(extra, windows, bias[0:1, :])
    put_parts(extra, windows + 3, bias[1:2, :])
    piece[3 * n :, :] = extra[...].astype(bf16)
    for j, copy in enumerate(copies):
        copy.wait()
        piece[j * n : (j + 1) * n, :] = part[j].astype(bf16)


def pack_rest(info, w_out, w_up, w_down, bias, piece, down_piece, out_low, up_low, down_low, extra):
    hid = w_up.shape[1] // 2
    n_out, n_up, n_down = w_out.shape[0] // 4, w_up.shape[0] // 4, w_down.shape[0] // 4
    out_low[...] = w_out[...].astype(bf16)
    up_low[...] = w_up[...].astype(bf16)
    down_low[...] = w_down[...].astype(bf16)
    extra[...] = jnp.zeros_like(extra)
    put_parts(extra, 0, bias[:, :hid])
    put_parts(extra, 3, bias[:, hid:])
    piece[:n_out, :] = out_low[pl.ds(pl.multiple_of(info[7] * n_out, n_out), n_out), :]
    rows = pl.ds(pl.multiple_of(info[7] * n_up, n_up), n_up)
    for h in range(2):
        piece[n_out + h * n_up : n_out + (h + 1) * n_up, :] = up_low[rows, h * hid : (h + 1) * hid]
    piece[n_out + 2 * n_up :, :] = extra[...].astype(bf16)
    down_piece[...] = down_low[pl.ds(pl.multiple_of(info[7] * n_down, n_down), n_down), :]


def attend(wq, bias, picks, start, emb, q_out, k_out, v_out, ctx, att, picked, length, scale):
    cols = wq.shape[2]
    e = emb[...]
    for j, out in enumerate((q_out, k_out, v_out)):
        out[...] = (nn(e, wq[j]) + bias[j]).astype(bf16)
    mask = head_mask(cols)
    mask_low = mask.astype(f32).astype(bf16)
    spots = [slice(i * length, (i + 1) * length) for i in range(emb.shape[0] // length)]
    hots = [one_hot(picks, start + i, length) for i in range(len(spots))]
    sel = [nn(down, q_out[here, :]) for (_, down), here in zip(hots, spots)]
    sel = [jnp.where(mask, x, 0.0).astype(bf16) for x in sel]
    for i, x in enumerate(sel):
        picked[i] = x
    scores = [nt(x, k_out[here, :]) * scale for x, here in zip(sel, spots)]
    active = [nn(up, mask_low) for up, _ in hots]
    exponent = [jnp.exp(x - jnp.max(x, axis=-1, keepdims=True)) for x in scores]
    probs = [x * (1.0 / jnp.sum(x, axis=-1, keepdims=True)) for x in exponent]
    for i, x in enumerate(probs):
        att[i] = x
    mixed = [nn(x.astype(bf16), v_out[here, :]) for x, here in zip(probs, spots)]
    mixed = [jnp.where(mask, x, 0.0).astype(bf16) for x in mixed]
    mean = [col_sum(v_out[here, :].astype(f32)) * (1.0 / length) for here in spots]
    mixed = [nn(up, x) for (up, _), x in zip(hots, mixed)]
    for here, x, act, m in zip(spots, mixed, active, mean):
        ctx[here, :] = (x + (1.0 - act) * m).astype(bf16)


def attend_own(length, scale, info, groups, tokens, table, w, bias, picks,
               q, k, v, ctx, att, picked, emb, emb_t, wq):
    @pl.when(pl.program_id(0) == 0)
    def _():
        for j in range(3):
            wq[j] = w[j].astype(bf16)

    per = tokens.shape[0] // length
    first = pl.program_id(0) * per
    for i in range(per):
        here = slice(i * length, (i + 1) * length)
        row = table[pl.ds(groups[info[3] + first + i], 1), :]
        emb[here, :] = (tokens[here, :].astype(f32) + row).astype(bf16)
    emb_t[...] = emb[...].astype(f32).T.astype(bf16)
    rows = (bias[0:1, :], jnp.zeros_like(bias[0:1, :]), bias[1:2, :])
    attend(wq, rows, picks, info[1] + first, emb, q, k, v, ctx, att, picked, length, scale)


def attend_far(length, scale, info, emb, p0, p1, p2, p3,
               q, k, v, ctx, att, picked, wq, picks, extra, bias, sems):
    n = wq.shape[1] // 4
    windows = picks.shape[0]

    @pl.when(pl.program_id(0) == 0)
    def _():
        pairs = [(p0.at[pl.ds(3 * n, extra.shape[0]), :], extra)]
        for i, piece in enumerate((p0, p1, p2, p3)):
            for j in range(3):
                pairs.append(
                    (
                        piece.at[pl.ds(j * n, n), :],
                        wq.at[j, pl.ds(pl.multiple_of((info[7] ^ i) * n, n), n), :],
                    )
                )
        for copy in copy_all(pairs, sems):
            copy.wait()
        rest = extra[...].astype(f32)
        picks[...] = rest[:windows, : GROUP * SLOTS]
        bias[0:1, :] = split_sum(rest, windows)
        bias[1:2, :] = split_sum(rest, windows + 3)

    rows = (bias[0:1, :], jnp.zeros_like(bias[0:1, :]), bias[1:2, :])
    first = pl.program_id(0) * (emb.shape[0] // length)
    attend(wq, rows, picks, first, emb, q, k, v, ctx, att, picked, length, scale)


def gelu_pair(x):
    bell = jnp.exp2((x * x) * (-0.5 * math.log2(math.e)))
    y = 1.0 + (0.3275911 * math.sqrt(0.5)) * jnp.abs(x)
    t = pl.reciprocal(y, approx=True)
    t = t * (2.0 - y * t)
    poly = t * (
        0.5 * 0.254829592
        + t * (0.5 * -0.284496736 + t * (0.5 * 1.421413741 + t * (0.5 * -1.453152027 + t * (0.5 * 1.061405429))))
    )
    tail = poly * bell
    phi = jnp.where(x >= 0.0, 1.0 - tail, tail)
    return x * phi, phi + (x * (1.0 / math.sqrt(2.0 * math.pi))) * bell


def feed_forward(length, parts, info, groups, tokens, table, ctx0, ctx1, near_out, near_up, near_down,
                 p0, p1, p2, p3, d0, d1, d2, d3, ff_bias, gains, shifts, cot_in,
                 out_far, gp1_far, ga_far, keep, send, sums, wo_far,
                 wo, up, dn, act, gpre, slope, nl, gb, ga, out, gp1, pre, cot, nl_t, gb_t, ffb, extra, buf,
                 sems, row_sems, end_sems):
    core, quarter = info[0], info[7]
    rows, width = tokens.shape
    block = rows // parts
    cols = wo.shape[1]
    hid = up.shape[2]
    half = hid // 2

    def rows_of(x, i, n, *rest):
        return x.at[(1, pl.ds(pl.multiple_of((quarter ^ i) * n, n), n)) + rest]

    n_out, n_up, n_down = cols // 4, width // 4, hid // 4
    pairs = [[(near_out, wo.at[0])], [(near_up, up.at[0])], [(near_down, dn.at[0])], [(cot_in, cot)]]
    pairs[1].append((p0.at[pl.ds(n_out + 2 * n_up, 16), :], extra))
    for i, (p, d) in enumerate(((p0, d0), (p1, d1), (p2, d2), (p3, d3))):
        pairs[0].append((p.at[pl.ds(0, n_out), :], rows_of(wo, i, n_out)))
        for h in range(2):
            pairs[1].append(
                (p.at[pl.ds(n_out + h * n_up, n_up), :], rows_of(up, i, n_up, pl.ds(h * half, half)))
            )
        pairs[2].append((d, rows_of(dn, i, n_down)))
    loads, at = [], 0
    for some in pairs:
        loads.append([pltpu.make_async_copy(a, b, sems.at[at + i]) for i, (a, b) in enumerate(some)])
        at += len(some)
    for some in loads:
        for copy in some:
            copy.start()
    wo_copy = pltpu.make_async_copy(wo, wo_far, end_sems.at[4])
    ffb[0:1, :] = ff_bias[...]
    for i in range(rows // length):
        here = slice(i * length, (i + 1) * length)
        pre[here, :] = tokens[here, :].astype(f32) + table[pl.ds(groups[info[3] + i], 1), :]
    for copy in loads[0]:
        copy.wait()
    wo_copy.start()

    spans = [slice(i * block, (i + 1) * block) for i in range(parts)]
    inv_one = []
    xs = [nn(ctx0[here, :], wo[0]) + nn(ctx1[here, :], wo[1]) for here in spans]
    for here, x in zip(spans, xs):
        x = pre[here, :] + (x + shifts[0:1, :])
        center = x - row_mean(x)
        inv_one.append(lax.rsqrt(row_mean(center * center) + EPS_NORM))
        unit = center * inv_one[-1]
        pre[here, :] = unit
        nl[here, :] = (unit * gains[0:1, :] + shifts[2:3, :]).astype(bf16)
    for some in loads[1:]:
        for copy in some:
            copy.wait()
    rest = extra[...].astype(f32)
    ffb[1:2, :half] = split_sum(rest, 0)
    ffb[1:2, half:] = split_sum(rest, 3)

    order = [(i, ch) for ch in range(4) for i in range(parts)]

    def lift(i, ch):
        g, o = ch // 2, (ch % 2) * half
        return nn(nl[spans[i], :], up[g, :, o : o + half])

    later = lift(*order[0])
    branch = [shifts[1:2, :]] * parts
    for k, (i, ch) in enumerate(order):
        g, o = ch // 2, (ch % 2) * half
        z = later + ffb[g : g + 1, o : o + half]
        if k + 1 < len(order):
            later = lift(*order[k + 1])
        a, d = gelu_pair(z)
        a = a.astype(bf16)
        act[spans[i], ch * half : (ch + 1) * half] = a
        slope[spans[i], ch * half : (ch + 1) * half] = d.astype(bf16)
        branch[i] = branch[i] + nn(a, dn[g, o : o + half, :])
    total = []
    tops = [0.0] * 3
    for here, x in zip(spans, branch):
        y = pre[here, :] * gains[0:1, :] + shifts[2:3, :] + x
        center = y - row_mean(y)
        inv_two = lax.rsqrt(row_mean(center * center) + EPS_NORM)
        unit_two = center * inv_two
        out[here, :] = unit_two * gains[1:2, :] + shifts[3:4, :]
        c = cot[here, :]
        g2 = c * gains[1:2, :]
        gp2 = (g2 - row_mean(g2) - unit_two * row_mean(g2 * unit_two)) * inv_two
        low = gp2.astype(bf16)
        gb[here, :] = low
        tops = [t + col_sum(x) for t, x in zip(tops, (c * unit_two, c, low.astype(f32)))]
        total.append(gp2)
    sums[...] = jnp.zeros_like(sums)
    sums[1:2, :] = tops[0]
    sums[5:6, :] = tops[1]
    sums[3:4, :] = tops[2]

    def lower(i, ch):
        g, o = ch // 2, (ch % 2) * half
        return nt(gb[spans[i], :], dn[g, o : o + half, :])

    later = lower(*order[0])
    for k, (i, ch) in enumerate(order):
        g, o = ch // 2, (ch % 2) * half
        p = later * slope[spans[i], ch * half : (ch + 1) * half].astype(f32)
        if k + 1 < len(order):
            later = lower(*order[k + 1])
        p = p.astype(bf16)
        gpre[spans[i], ch * half : (ch + 1) * half] = p
        sums[6 + ch : 7 + ch, :] += col_sum(p.astype(f32))
        total[i] = total[i] + nt(p, up[g, :, o : o + half])
    tops = [0.0] * 3
    for here, x, inv in zip(spans, total, inv_one):
        unit_one = pre[here, :]
        g1 = x * gains[0:1, :]
        gp = (g1 - row_mean(g1) - unit_one * row_mean(g1 * unit_one)) * inv
        gp1[here, :] = gp
        low_one = gp.astype(bf16)
        ga[here, :] = low_one
        tops = [t + col_sum(v) for t, v in zip(tops, (x * unit_one, x, low_one.astype(f32)))]
    sums[0:1, :] = tops[0]
    sums[4:5, :] = tops[1]
    sums[2:3, :] = tops[2]
    ends = [
        pltpu.make_async_copy(a, b, row_sems.at[j])
        for j, (a, b) in enumerate(((ga, ga_far), (gp1, gp1_far), (out, out_far)))
    ] + [wo_copy]
    for copy in ends[:3]:
        copy.start()
    for i in range(rows // length):
        spot = pl.ds(10 + groups[info[3] + i], 1)
        sums[spot, :] += col_sum(gp1[i * length : (i + 1) * length, :])
    nl_t[...] = nl[...].astype(f32).T.astype(bf16)
    gb_t[...] = gb[...].astype(f32).T.astype(bf16)
    n = buf.shape[1] // 2
    for g, ctx in ((1, ctx1), (0, ctx0)):
        buf[g, 2 * hid : 2 * hid + cols, :] = nn(ctx[...].astype(f32).T.astype(bf16), ga[...]).astype(bf16)
        for ch in (2 * g, 2 * g + 1):
            o = (ch % 2) * half
            at = slice(ch * half, (ch + 1) * half)
            buf[g, o : o + half, :] = nn(nl_t[...], gpre[:, at]).astype(bf16)
            buf[g, hid + o : hid + o + half, :] = nn(gb_t[...], act[:, at]).astype(bf16)
        for dst, spot in ((send, 1 - core), (keep, core)):
            copy = pltpu.make_async_copy(
                buf.at[g, pl.ds(pl.multiple_of(spot * n, 32), n), :], dst.at[g], end_sems.at[2 * g + (dst is keep)]
            )
            copy.start()
            ends.append(copy)
    for copy in ends:
        copy.wait()


def attend_back(length, scale, g, info, groups, ga, emb_in, wo, picks, wq_in, k_in, v_in, att, picked, *refs):
    last = g == 0
    if last:
        sums, tsum_far, total_far, *refs = refs
    gq, gk, gv, keep, send, *refs = refs
    if not last:
        tsum, total_out, *refs = refs
    gq_all, gk_all, gv_all, emb_t, wq, buf, *refs = refs
    if last:
        tsum, small, *refs = refs
    (sems,) = refs
    core = info[0]
    step = pl.program_id(0)
    width, rows = emb_t.shape
    block = ga.shape[0]
    per = block // length
    cols = wq.shape[2]
    half = width // 2
    mask = head_mask(cols)
    mask_low = mask.astype(f32).astype(bf16)
    late = [
        pltpu.make_async_copy(a, b, sems.at[8 + i]) for i, (a, b) in enumerate(((emb_in, emb_t), (wq_in, wq)))
    ]

    @pl.when(step == 0)
    def _():
        for copy in late:
            copy.start()
        tsum[...] = jnp.zeros_like(tsum)

    start = (info[1] if last else 0) + step * per
    spots = [slice(i * length, (i + 1) * length) for i in range(per)]
    g_ctx = nt(ga[...], wo[g]).astype(bf16)
    hots = [one_hot(picks, start + i, length) for i in range(per)]
    ge = [nn(down, g_ctx[here, :]) for here, (_, down) in zip(spots, hots)]
    ge = [jnp.where(mask, x, 0.0).astype(bf16) for x in ge]
    active = [nn(up, mask_low) for up, _ in hots]
    gprobs = [nt(x, v_in[here, :]) for here, x in zip(spots, ge)]
    low_t = [att[i].T.astype(bf16) for i in range(per)]
    gmean = [
        col_sum((1.0 - x) * g_ctx[here, :].astype(f32)) * (1.0 / length) for here, x in zip(spots, active)
    ]
    g_value = [nn(x, y) for x, y in zip(low_t, ge)]
    weighted = [att[i] * x for i, x in enumerate(gprobs)]
    graw = [(x - att[i] * jnp.sum(x, axis=-1, keepdims=True)) * scale for i, x in enumerate(weighted)]
    gpick = [nn(x.astype(bf16), k_in[here, :]) for here, x in zip(spots, graw)]
    graw_t = [x.T.astype(bf16) for x in graw]
    g_value = [(x + m).astype(bf16) for x, m in zip(g_value, gmean)]
    gpick = [jnp.where(mask, x, 0.0).astype(bf16) for x in gpick]
    g_key = [nn(x, picked[i]).astype(bf16) for i, x in enumerate(graw_t)]
    g_query = [nn(up, x).astype(bf16) for (up, _), x in zip(hots, gpick)]
    for i, three in enumerate(zip(g_query, g_key, g_value)):
        rows_here = pl.ds(pl.multiple_of(step * block + i * length, 32), length)
        group = groups[info[3] + step * per + i]
        for j, (x, dst, dst_all) in enumerate(zip(three, (gq, gk, gv), (gq_all, gk_all, gv_all))):
            dst[spots[i], :] = x
            dst_all[rows_here, :] = x
            tsum[pl.ds(2 * j + group, 1), :] += col_sum(x.astype(f32))

    @pl.when(step == rows // block - 1)
    def _():
        for copy in late:
            copy.wait()
        n = 3 * half // 2
        pairs = []
        for j, x in enumerate((gq_all, gk_all, gv_all)):
            r = nn(emb_t[...], x[...]).astype(bf16)
            buf[j * half : (j + 1) * half, :cols] = r[:half]
            buf[j * half : (j + 1) * half, cols:] = r[half:]
        for dst, spot in ((send, 1 - core), (keep, core)):
            pairs.append((buf.at[at_row(spot * n, n), :], dst.at[pl.ds(0, n), :]))
        copies = copy_all(pairs, sems)
        total = jnp.zeros((8, width), f32)
        for j in range(3):
            x = tsum[2 * j : 2 * j + 8, :]
            hi = x.astype(bf16)
            lo = (x - hi.astype(f32)).astype(bf16)
            total = total + nt(hi, wq[j]) + nt(lo, wq[j])
        if last:
            total = total + total_far[...]
            small[...] = jnp.zeros_like(small)
            for m, t in enumerate((tsum, tsum_far)):
                at = 16 * m
                small[at : at + 2, :] = total[0:2] + sums[10:12, :]
                small[at + 2 : at + 8, :] = sums[0:6, :]
                small[at + 8 : at + 10, :] = sums[6 + 2 * m : 8 + 2 * m, :]
                small[at + 10 : at + 11, :cols] = t[0:1, :] + t[1:2, :]
                small[at + 10 : at + 11, cols:] = t[4:5, :] + t[5:6, :]
            buf[2 * n :, :] = small[...].astype(bf16)
            more = [
                pltpu.make_async_copy(buf.at[pl.ds(2 * n, 32), :], dst.at[pl.ds(n, 32), :], sems.at[2 + i])
                for i, dst in enumerate((send, keep))
            ]
            for copy in more:
                copy.start()
            copies += more
        else:
            total_out[...] = total
        for copy in copies:
            copy.wait()


def input_grad(*refs):
    (*grads, wq0, wq1, gp1, out) = refs
    total = gp1[...]
    for i, x in enumerate(grads):
        total = total + nt(x[...], (wq0, wq1)[i // 3][i % 3])
    out[...] = total


def hop(x, *bits):
    heads = lax.axis_size("head")
    flip = sum((1 << k) * (heads if axis == "dp" else 1) for axis, k in bits)
    count = lax.axis_size("dp") * heads
    return lax.ppermute(x, ("dp", "head"), [(i, i ^ flip) for i in range(count)])


def side(bit):
    axis, k = bit
    return (lax.axis_index(axis) >> k) & 1


def subsets(bits):
    return [[b for i, b in enumerate(bits) if (r >> i) & 1] for r in range(1 << len(bits))]


def pair_sum(terms):
    while len(terms) > 1:
        terms = [terms[i] + terms[i + 1] for i in range(0, len(terms), 2)]
    return terms[0]


def pick(x, bits, far, flips):
    for bit in bits:
        flipped = bit in flips
        if bit == far:
            x = x[1:] if flipped else x[:1]
        else:
            n = x.shape[1] // 2
            x = lax.dynamic_slice_in_dim(x, (side(bit) ^ int(flipped)) * n, n, 1)
    return x


def scatter_sum(x, bits, far, small=None):
    terms, rest = [], []
    for flips in subsets(bits):
        part = pick(x, bits, far, flips)
        if small is not None:
            part = jnp.concatenate([part, pick(small, [far] if far in bits else [], far, flips)], 1)
        if flips:
            part = hop(part, *flips)
        terms.append(part.astype(f32))
    total = pair_sum(terms).astype(bf16)
    if small is None:
        return total
    n = total.shape[1] - small.shape[1]
    return total[:, :n], total[:, n:]


def gather(x, bits):
    parts = {}
    for r, flips in enumerate(subsets(bits)):
        parts[r] = hop(x, *flips) if flips else x
    for i, bit in enumerate(bits):
        m = side(bit) == 0
        parts = {
            r: jnp.where(m, parts[r], parts[r ^ (1 << i)]) for r in parts
        }
    order = sorted(parts, key=lambda r: [(r >> i) & 1 for i in range(len(bits))])
    return jnp.concatenate([parts[r] for r in order], axis=0)


def plus(a, b):
    return (a.astype(f32) + b.astype(f32)).astype(bf16)


def late_steps(small_rows, bits, far, core):
    stages = [[far, bits[0]]] + [bits[i : i + 2] for i in range(1, len(bits), 2)]

    def cores(state):
        x = plus(state[0], hop(state[1], core))
        return x[:, :-small_rows], x[:, -small_rows:]

    def down(stage):
        return lambda state: scatter_sum(state[0], stage, far, state[1])

    def up(stage):
        wanted = [b for b in stage if b != far]

        def step(state):
            x = state[0] if state[0].ndim == 2 else state[0][0]
            return gather(x, wanted), state[1]

        return step

    return [cores] + [down(s) for s in stages] + [up(s) for s in reversed(stages)] + [up([core])]


def early_steps(bits, far, core):
    first, second, rest = bits[0], bits[1], bits[2:]
    orders = ((far, first, second), (first, second, far), (second, far, first))

    def start(x):
        part = x.shape[1] // 3
        return down(0)([x[:, i * part : (i + 1) * part] for i in range(3)])

    def down(stage):
        return lambda chunks: [scatter_sum(c, [order[stage]], far) for c, order in zip(chunks, orders)]

    def swap(chunks):
        x = jnp.concatenate(chunks, axis=2)[0]
        for bit in rest:
            x = plus(x, hop(x, bit))
        width = x.shape[1] // 3
        return [x[:, : 2 * width], x[:, 2 * width :]]

    def up_one(parts):
        return [gather(parts[0], [second]), gather(parts[1], [first])]

    def up_two(parts):
        two, one = gather(parts[0], [first]), gather(parts[1], [second])
        width = one.shape[1]
        return jnp.concatenate([two[:, :width], two[:, width:], one], axis=0)

    return [start, down(1), down(2), swap, up_one, up_two, lambda x: gather(x, [core])]


def add(a, b):
    return a.astype(f32) + b.astype(f32)


def at_row(start, n):
    return pl.ds(pl.multiple_of(start, 16), n)


def merge_cores(info, keep, got, stay0, far0, stay1, first1, stay2, second2):
    n = keep.shape[1] // 3
    h = n // 2
    a, b = info[4], info[5]
    stay0[...] = add(keep[0, :n], got[0, :n]).astype(bf16)
    far0[...] = add(keep[1, :n], got[1, :n]).astype(bf16)
    for base, bit, stay, send in ((n, a, stay1, first1), (2 * n, b, stay2, second2)):
        for dst, m in ((stay, bit), (send, 1 - bit)):
            here = at_row(base + m * h, h)
            for g in range(2):
                dst[g] = add(keep[g, here], got[g, here]).astype(bf16)


def merge_two(info, stay0, got0, stay1, got1, stay2, got2, keep0, first0, keep1, second1, keep2, far2):
    a, b = info[4], info[5]
    h = stay0.shape[0] // 2
    for dst, m in ((keep0, a), (first0, 1 - a)):
        here = at_row(m * h, h)
        dst[...] = add(stay0[here], got0[here]).astype(bf16)
    q = stay1.shape[1] // 2
    for dst, m in ((keep1, b), (second1, 1 - b)):
        here = at_row(m * q, q)
        for g in range(2):
            dst[g] = add(stay1[g, here], got1[g, here]).astype(bf16)
    keep2[...] = add(stay2[0], got2[0]).astype(bf16)
    far2[...] = add(stay2[1], got2[1]).astype(bf16)


def merge_three(info, in0, got0, in1, got1, in2, got2, stay, to_second, to_far, to_first):
    a, b = info[4], info[5]
    q = to_far.shape[0]
    stay[:q] = add(in0[at_row(b * q, q)], got0[at_row(b * q, q)]).astype(bf16)
    to_second[...] = add(in0[at_row((1 - b) * q, q)], got0[at_row((1 - b) * q, q)]).astype(bf16)
    stay[q : 2 * q] = add(in1[0], got1[0]).astype(bf16)
    to_far[...] = add(in1[1], got1[1]).astype(bf16)
    stay[2 * q :] = add(in2[at_row(a * q, q)], got2[at_row(a * q, q)]).astype(bf16)
    to_first[...] = add(in2[at_row((1 - a) * q, q)], got2[at_row((1 - a) * q, q)]).astype(bf16)


def merge_four(info, stay, second, far, first, keep0, got0, keep1, got1, part, mine, to_first, to_far, to_both):
    q = second.shape[0]
    for i, x in enumerate((second, far, first)):
        part[i * q : (i + 1) * q] = add(stay[i * q : (i + 1) * q], x[...]).astype(bf16)
    a = info[4]
    h = mine.shape[0] - 16
    for dst, keep, got, g, m in (
        (mine, keep0, got0, 0, a), (to_first, keep0, got0, 0, 1 - a),
        (to_far, keep1, got1, 1, a), (to_both, keep1, got1, 1, 1 - a),
    ):
        here = at_row(m * h, h)
        tail = slice(2 * h + 16 * g, 2 * h + 16 * g + 16)
        dst[:h] = add(keep[here], got[here]).astype(bf16)
        dst[h:] = add(keep0[tail], got0[tail]).astype(bf16)


def merge_five(info, part, third, mine, first, far, both, own, to_second, to_first, to_third, to_both, total):
    q = part.shape[0] // 3
    to_second[: 2 * q] = add(part[: 2 * q], third[: 2 * q]).astype(bf16)
    to_first[...] = add(part[2 * q :], third[2 * q :]).astype(bf16)
    total[...] = (add(mine[...], first[...]) + add(far[...], both[...])).astype(bf16)
    n = own.shape[0] - 16
    spot = 2 * info[5] + info[6]
    for dst, base, flip in ((own, 0, 0), (to_second, 2 * q, 2), (to_third, 0, 1), (to_both, 0, 3)):
        dst[base : base + n] = total[at_row((spot ^ flip) * n, n)]
        dst[base + n : base + n + 16] = total[4 * n :]


def merge_six(info, near2, got2, near1, got1, own, third, both,
              to_first, to_second, to_third, table, gains, shifts, ff, bias):
    a, b = info[4], info[5]
    q = near1.shape[0]
    for c in range(2):
        to_first[at_row(2 * c * q + b * q, q)] = near2[c * q : (c + 1) * q]
        to_first[at_row(2 * c * q + (1 - b) * q, q)] = got2[c * q : (c + 1) * q]
    to_second[at_row(a * q, q)] = near1[...]
    to_second[at_row((1 - a) * q, q)] = got1[...]
    s = add(own[...], got2[2 * q :]) + add(third[...], both[...])
    h = own.shape[0] - 16
    to_third[...] = s[:h].astype(bf16)
    to_second[2 * q :] = to_third[...]
    s = s[h:]
    width = s.shape[1]
    table[...] = s[0:2]
    gains[...] = s[2:4]
    shifts[...] = s[4:8]
    ff[:, :width] = s[8:9]
    ff[:, width:] = s[9:10]
    bias[0:1] = s[10:11, : width // 2]
    bias[1:2] = s[10:11, width // 2 :]


def merge_seven(info, near1, got1, near2, got2, near3, got3, both, out, two):
    a, b = info[4], info[5]
    h = near1.shape[0] // 2
    for c in range(2):
        out[at_row(2 * c * h + a * h, h)] = near1[c * h : (c + 1) * h]
        out[at_row(2 * c * h + (1 - a) * h, h)] = got1[c * h : (c + 1) * h]
    out[at_row(4 * h + b * h, h)] = near2[:h]
    out[at_row(4 * h + (1 - b) * h, h)] = got2[:h]
    spot = 2 * b + info[6]
    n = near3.shape[0]
    for src, base, flip in ((near3, 0, 0), (got2, h, 2), (got3, 0, 1), (both, 0, 3)):
        two[at_row((spot ^ flip) * n, n)] = src[base : base + n]


def merge_eight(info, near, got, out):
    n = near.shape[0]
    out[at_row(info[4] * n, n)] = near[...]
    out[at_row((1 - info[4]) * n, n)] = got[...]


def merge(body, info, ins, outs, width, with_info=True):
    shapes = [(s if isinstance(s, tuple) else (s, width), bf16, VMEM) for s in outs]
    return call(
        body,
        shapes,
        [SMEM] * with_info + [VMEM] * len(ins),
        ((info,) if with_info else ()) + tuple(ins),
        [],
        24,
        2 * US,
        2e6,
        hbm_in=False,
        hbm_out=False,
    )


def sum_start(info, keep, send, bits, far, core):
    first, second, _ = bits
    width = keep.shape[2]
    n = keep.shape[1] // 3
    two = (2, n // 2, width)
    stay0, far0, stay1, first1, stay2, second2 = merge(
        merge_cores, info, (keep, hop(send, core)), (n, n, two, two, two, two), width
    )
    return (stay0, hop(far0, far), stay1, hop(first1, first), stay2, hop(second2, second))


def sum_middle(info, state, bits, far, width):
    first, second, _ = bits
    n = state[0].shape[0]
    q = n // 4
    keep0, first0, keep1, second1, keep2, far2 = merge(
        merge_two, info, state, (n // 2, n // 2, (2, q, width), (2, q, width), n // 2, n // 2), width
    )
    return (keep0, hop(first0, first), keep1, hop(second1, second), keep2, hop(far2, far))


def sum_finish(info, state, late, bits, far, core, beside):
    first, second, third = bits
    width = state[0].shape[1]
    q = state[0].shape[0] // 2
    keep0, send0, keep1, got1 = late
    stay, to_second, to_far, to_first = merge(merge_three, info, state, (3 * q, q, q, q), width)
    send0, stay = lax.optimization_barrier((send0, stay))
    got0 = hop(send0, core)
    h = keep1.shape[0] // 2
    part, mine, to_first, to_far, to_both = merge(
        merge_four,
        info,
        (stay, hop(to_second, second), hop(to_far, far), hop(to_first, first), keep0, got0, keep1, got1),
        (3 * q, h + 16, h + 16, h + 16, h + 16),
        width,
    )
    many = beside[0](part)
    got = hop(part, third), hop(to_first, first), hop(to_far, far), hop(to_both, first, far)
    part, many[0] = lax.optimization_barrier((part, many[0]))
    m = h // 4
    own, to_second, to_first, to_third, to_both, _ = merge(
        merge_five,
        info,
        (part, got[0], mine, *got[1:]),
        (m + 16, 2 * q + m + 16, q, m + 16, m + 16, h + 16),
        width,
    )
    few = beside[2](own)
    got = hop(to_second, second), hop(to_first, first), hop(to_third, third), hop(to_both, second, third)
    own, few[0] = lax.optimization_barrier((own, few[0]))
    to_first, to_second, to_third, *small = call(
        merge_six,
        [((4 * q, width), bf16, VMEM), ((2 * q + m, width), bf16, VMEM), ((m, width), bf16, VMEM)]
        + [(shape, f32, VMEM) for shape in ((2, width), (2, width), (4, width), (1, 2 * width), (2, width // 2))],
        [SMEM] + [VMEM] * 7,
        (info, to_second, got[0], to_first, got[1], own, got[2], got[3]),
        [],
        24,
        2 * US,
        2e6,
        hbm_in=False,
        hbm_out=False,
    )
    rows = beside[1](to_third)
    got = hop(to_first, first), hop(to_second, second), hop(to_third, third), hop(to_third, second, third)
    to_first, rows = lax.optimization_barrier((to_first, rows))
    one, two = merge(
        merge_seven, info, (to_first, got[0], to_second, got[1], to_third, got[2], got[3]), (12 * q, 4 * m), width
    )
    other = hop(one, core)
    got = hop(two, first)
    (two,) = merge(merge_eight, info, (two, got), (8 * m,), width)
    return (one, other), (two, hop(two, core)), small, (many, rows, few)


def wipe(*refs):
    sems = refs[-1]
    count = sems.shape[0]
    outs, zeros = refs[1 : 1 + count], refs[1 + count : -1]
    for zero in zeros:
        zero[...] = jnp.zeros_like(zero)
    copies = []
    for i, out in enumerate(outs):
        src = next(z for z in zeros if z.dtype == out.dtype and z.shape[1] == out.shape[1])
        rows = out.shape[0]
        n = next(c for c in (256, 192, 128, 64, 32, 16) if rows % c == 0)
        for at in range(0, rows, n):
            copies.append(
                pltpu.make_async_copy(
                    src.at[pl.ds(0, n), :], out.at[pl.ds(at, n), :], sems.at[i]
                )
            )
    for copy in copies:
        copy.start()
    for copy in copies:
        copy.wait()


def blanks_for(gate, likes):
    flat = [(math.prod(x.shape[:-1]), x.shape[-1]) for x in likes]
    widths = sorted({n for _, n in flat})
    outs = call(
        wipe,
        [(s, x.dtype, HBM) for s, x in zip(flat, likes)],
        [HBM],
        (gate,),
        [pltpu.VMEM((256, n), k) for n in widths for k in (f32, bf16)]
        + [pltpu.SemaphoreType.DMA((len(likes),))],
        8,
        US // 2,
        1e6,
        hbm_in=False,
    )
    return [x.reshape(like.shape) for x, like in zip(outs, likes)]


def moments(turned, m, v):
    first = BETA_ONE * m[...] + (1.0 - BETA_ONE) * turned
    second = BETA_TWO * v[...] + (1.0 - BETA_TWO) * (turned * turned)
    m[...] = first
    v[...] = second
    return (first / (jnp.sqrt(second) + EPS_ADAM)).astype(bf16)


def fetch(pairs, sems):
    for copy in copy_all(pairs, sems):
        copy.wait()


def step_wide(g, w, m, v, ql, qr, rate, scratch, ready):
    low_l, low_r, mid, back = scratch
    low_l[...] = ql[...].astype(bf16)
    low_r[...] = qr[...].astype(bf16)
    blocks, size = qr.shape[0], qr.shape[1]
    mid[...] = nn(ql[...].T.astype(bf16), g).astype(bf16)
    for b in range(blocks):
        at = slice(b * size, (b + 1) * size)
        u = moments(nn(mid[:, at], low_r[b]), m.at[:, at], v.at[:, at])
        back[:, at] = nt(u, low_r[b]).astype(bf16)
    ready()
    w[...] = w[...] - rate * nn(low_l[...], back[...])


def step_tall(g, w, m, v, ql, qr, rate, scratch, ready):
    low_r, mid, back = scratch
    low_r[...] = qr[...].astype(bf16)
    blocks, size = ql.shape[0], ql.shape[1]
    for b in range(blocks):
        at = slice(b * size, (b + 1) * size)
        mid[at, :] = nn(ql[b].T.astype(bf16), g[at, :]).astype(bf16)
    u = moments(nn(mid[...], low_r[...]), m, v)
    ready()
    back[...] = nt(u, low_r[...]).astype(bf16)
    for b in range(blocks):
        at = slice(b * size, (b + 1) * size)
        w[at, :] = w[at, :] - rate * nn(ql[b].astype(bf16), back[at, :])


def update_qkv(rate, mine, g, w_in, m_in, v_in, ql_in, qr_in, *refs):
    outs, (grad, new, mom, var, copy) = refs[:4], refs[4:9]
    w, m, v, c, ql, qr, low_l, low_r, mid, back, sems = refs[9:]
    for j in range(3):
        grad[j] = g[j].astype(f32)

        @pl.when(mine[j] == 1)
        def _():
            fetch(
                [(w_in.at[j], w), (m_in.at[j], m), (v_in.at[j], v), (ql_in.at[j], ql), (qr_in.at[j], qr)], sems
            )
            step_wide(g[j], w, m, v, ql, qr, rate, (low_l, low_r, mid, back), lambda: None)
            c[...] = w[...].astype(bf16)
            fetch([(w, new.at[j]), (m, mom.at[j]), (v, var.at[j]), (c, copy.at[j])], sems)


def update_rest(rate_out, rate_up, rate_down, mine, g_out, g_up, g_down_t, *refs):
    (wo_in, mo_in, vo_in, lo_in, ro_in, wu_in, mu_in, vu_in, lu_in, ru_in,
     wd_in, md_in, vd_in, ld_in, rd_in) = refs[:15]
    refs = refs[15 + 11 :]
    grad_o, grad_u, grad_d = refs[:3]
    new_o, moments_o, copy_o, new_u, mom_u, var_u, copy_u, new_d, mom_d, var_d, copy_d = refs[3:14]
    (wo, mo, vo, co, lo, ro, low_ro, mid_o, back_o,
     wu, mu, vu, cu, lu, ru, low_lu, low_ru, mid_u, back_u,
     wd, md, vd, cd, mid_d, back_d, sems) = refs[14:]
    grad_o[...] = g_out[...].astype(f32)
    grad_u[...] = g_up[...].astype(f32)
    grad_d[...] = g_down_t[...].astype(f32).T

    @pl.when(mine[3] == 1)
    def _():
        fetch([(wo_in, wo), (mo_in, mo), (vo_in, vo), (lo_in, lo), (ro_in, ro)], sems)
        step_tall(g_out[...], wo, mo, vo, lo, ro, rate_out, (low_ro, mid_o, back_o), lambda: None)
        co[...] = wo[...].astype(bf16)
        fetch([(wo, new_o), (mo, moments_o.at[0]), (vo, moments_o.at[1]), (co, copy_o)], sems)

    @pl.when(mine[4] == 1)
    def _():
        fetch([(wu_in, wu), (mu_in, mu), (vu_in, vu), (lu_in, lu), (ru_in, ru)], sems)
        step_wide(g_up[...], wu, mu, vu, lu, ru, rate_up, (low_lu, low_ru, mid_u, back_u), lambda: None)
        cu[...] = wu[...].astype(bf16)
        fetch([(wu, new_u), (mu, mom_u), (vu, var_u), (cu, copy_u)], sems)

    @pl.when(mine[5] == 1)
    def _():
        fetch([(wd_in, wd), (md_in, md), (vd_in, vd), (ld_in, ru), (rd_in, lu)], sems)
        step_tall(grad_d[...].astype(bf16), wd, md, vd, ru, lu, rate_down, (low_lu, mid_d, back_d), lambda: None)
        cd[...] = wd[...].astype(bf16)
        fetch([(wd, new_d), (md, mom_d), (vd, var_d), (cd, copy_d)], sems)


def update_all(rate_out, rate_wide, rate_down, cols, hid, owned, info, mine, other, mine_q, other_q, *refs):
    ins, refs = refs[:20], refs[20 + 15 :]
    grad_q, grad_o, grad_u, grad_d = refs[:4]
    outs, held, refs = refs[4:19], refs[19:39], refs[39:]
    wq, mq, vq, lq, rq, wo, mo, vo, lo, ro, wu, mu, vu, lu, ru, wd, md, vd, ld, rd = held
    new_q, mom_q, var_q, copy_q, new_o, mom_o, copy_o, new_u, mom_u, var_u, copy_u, new_d, mom_d, var_d, copy_d = outs
    buf, buf_q, gq, go, gu, gd, cq, co, cu, cd = refs[:10]
    low_l, low_r64, low_r256, mid_q, mid_o, mid_u, mid_d, back_q, back_o, back_u, back_d = refs[10:21]
    sems, in_sems, out_sems = refs[21:]
    core = info[0]
    loads = []
    for k in (4, 5, 3, 0, 1, 2):
        base = 5 * max(k - 2, 0)
        some = [(a.at[k], b.at[k]) if k < 3 else (a, b) for a, b in zip(ins[base : base + 5], held[base : base + 5])]
        some = [pltpu.make_async_copy(a, b, in_sems.at[k, i]) for i, (a, b) in enumerate(some)]
        loads.append((k, some))

        @pl.when(owned[k] == 1)
        def _(some=some):
            for copy in some:
                copy.start()

    loads = dict(loads)
    width = buf.shape[1]
    half = width // 2
    n = mine.shape[0]
    n_q = mine_q.shape[0]
    fills = copy_all(
        [(mine, buf.at[at_row(core * n, n)]), (other, buf.at[at_row((1 - core) * n, n)]),
         (mine_q, buf_q.at[at_row(core * n_q, n_q)]), (other_q, buf_q.at[at_row((1 - core) * n_q, n_q)])],
        sems,
    )
    pending = []

    def give(scratch, out, k):
        copy = pltpu.make_async_copy(scratch, out, sems.at[4 + k])
        copy.start()
        pending.append((None, copy))

    def finish(k, w, m, v, c, outs, run):
        stores = [
            pltpu.make_async_copy(a, b, out_sems.at[k, i]) for i, (a, b) in enumerate(zip((w, m, v, c), outs))
        ]

        @pl.when(owned[k] == 1)
        def _():
            for copy in loads[k]:
                copy.wait()

            def ready():
                stores[1].start()
                stores[2].start()

            run(ready)
            stores[0].start()
            c[...] = w[...].astype(bf16)
            stores[3].start()

        pending.extend((owned[k] == 1, copy) for copy in stores)

    fills[0].wait()
    fills[1].wait()
    h = hid // 2
    for i in range(2):
        gu[:, i * h : (i + 1) * h] = buf[i * width : (i + 1) * width, :].astype(f32)
    give(gu, grad_u, 0)
    finish(4, wu, mu, vu, cu, (new_u, mom_u, var_u, copy_u),
           lambda ready: step_wide(gu[...].astype(bf16), wu, mu, vu, lu, ru, rate_wide,
                                   (low_l, low_r256, mid_u, back_u), ready))
    for i in range(2):
        gd[i * h : (i + 1) * h, :] = buf[hid + i * width : hid + (i + 1) * width, :].astype(f32).T
    give(gd, grad_d, 1)
    finish(5, wd, md, vd, cd, (new_d, mom_d, var_d, copy_d),
           lambda ready: step_tall(gd[...].astype(bf16), wd, md, vd, ld, rd, rate_down,
                                   (low_l, mid_d, back_d), ready))
    go[...] = buf[2 * hid : 2 * hid + cols, :].astype(f32)
    give(go, grad_o, 2)
    finish(3, wo, mo, vo, co, (new_o, mom_o.at[0], mom_o.at[1], copy_o),
           lambda ready: step_tall(go[...].astype(bf16), wo, mo, vo, lo, ro, rate_out,
                                   (low_l, mid_o, back_o), ready))
    fills[2].wait()
    fills[3].wait()
    for j in range(3):
        x = buf_q[j * half : (j + 1) * half, :].astype(f32)
        gq[j, :half, :] = x[:, :cols]
        gq[j, half:, :] = x[:, cols:]
        give(gq.at[j], grad_q.at[j], 3 + j)
        finish(j, wq.at[j], mq.at[j], vq.at[j], cq.at[j], [x.at[j] for x in (new_q, mom_q, var_q, copy_q)],
               lambda ready, j=j: step_wide(gq[j].astype(bf16), wq.at[j], mq.at[j], vq.at[j], lq.at[j], rq.at[j],
                                            rate_wide, (low_l, low_r64, mid_q, back_q), ready))
    for flag, copy in pending:
        if flag is None:
            copy.wait()
        else:

            @pl.when(flag)
            def _(copy=copy):
                copy.wait()


def pad_picks(picks):
    windows, heads, slots = picks.shape
    return jnp.pad(picks, ((0, 0), (0, 0), (0, SLOTS - slots)), constant_values=-1).reshape(
        windows, heads * SLOTS
    )


def per_device(
    tokens_in,
    cotangent,
    data_table,
    window_group,
    query_picks,
    owner_list,
    weight_qkv,
    head_bias,
    weight_out,
    weight_up,
    ff_bias,
    weight_down,
    norm_gains,
    shifts,
    first_qkv,
    second_qkv,
    first_out,
    second_out,
    first_up,
    second_up,
    first_down,
    second_down,
    basis_qkv_left,
    basis_qkv_right,
    basis_out_left,
    basis_out_right,
    basis_up_left,
    basis_up_right,
    basis_down_left,
    basis_down_right,
):
    head_count = lax.axis_size("head")
    head = lax.axis_index("head")
    my_rank = lax.axis_index("dp")
    rows, width = tokens_in.shape
    length = rows * head_count // window_group.shape[0]
    windows = rows // length
    head_dim = basis_qkv_right.shape[-1]
    cols = GROUP * head_dim
    scale = 1.0 / math.sqrt(head_dim)
    head_bits = head_count.bit_length() - 1
    far = ("head", head_bits - 1)
    core_bit = ("dp", 0)
    dp_bits = lax.axis_size("dp").bit_length() - 1
    bits = [("dp", k) for k in range(1, dp_bits)] + [("head", k) for k in range(head_bits - 1)]
    core = my_rank & 1
    quarter = my_rank & 3
    second_bit = ("dp", 1)
    slots = GROUP * SLOTS
    half = width // 2

    if head_count == 2:
        n_qkv, n_bias, n_out, n_up, n_ff, n_down = (
            weight_qkv, head_bias, weight_out, weight_up, ff_bias, weight_down
        )
        picks = pad_picks(query_picks).astype(f32)
        near_at, far_at = head * windows, (1 - head) * windows
    else:
        def whole_of(x, dim):
            return lax.all_gather(x, "head", axis=dim, tiled=True)

        def pick_group(x, dim, g):
            n = x.shape[dim] // 2
            return lax.dynamic_slice_in_dim(x, (side(far) ^ g) * n, n, dim)

        both = [
            (whole_of(weight_qkv.astype(bf16), 2).astype(f32), 2),
            (whole_of(head_bias, 1), 1),
            (whole_of(weight_out.astype(bf16), 0).astype(f32), 0),
            (whole_of(weight_up.astype(bf16), 1).astype(f32), 1),
            (whole_of(ff_bias, 0), 0),
            (whole_of(weight_down.astype(bf16), 0).astype(f32), 0),
        ]
        n_qkv, n_bias, n_out, n_up, n_ff, n_down = (pick_group(x, d, 0) for x, d in both)
        away = [pick_group(x, d, 1) for x, d in both]
        picks = lax.dynamic_slice_in_dim(whole_of(query_picks, 1), head * windows, windows, 0)
        picks = jnp.concatenate([pad_picks(pick_group(picks, 1, g)) for g in range(2)]).astype(f32)
        near_at, far_at = jnp.int32(0), jnp.int32(windows)
    info = jnp.stack([core, near_at, far_at, head * windows] + [side(b) for b in bits[:3]] + [quarter]).astype(jnp.int32)
    quick = head_count == 2 and len(bits) == 3
    hid = n_up.shape[1]
    extra_rows = -(-(windows + 6) // 16) * 16
    buf_rows = 2 * hid + cols
    rest_rows = cols // 4 + width // 2 + 16

    def send_qkv(info, w, bias):
        return call(
            lambda *refs: pack_qkv(windows, *refs),
            [((3 * width // 4 + extra_rows, cols), bf16, VMEM)],
            [SMEM, HBM, VMEM, VMEM],
            (info, w, bias, picks),
            [
                pltpu.VMEM((3, width // 4, cols), f32),
                pltpu.VMEM((extra_rows, cols), f32),
                pltpu.SemaphoreType.DMA((3,)),
            ],
            12,
            2 * US,
            3e6,
            hbm_in=False,
            hbm_out=False,
        )

    def send_rest(info, w_out, w_up, w_down, bias):
        return call(
            pack_rest,
            [
                ((rest_rows, width), bf16, VMEM),
                ((hid // 4, width), bf16, VMEM),
                ((cols, width), bf16, VMEM),
                ((width, hid), bf16, VMEM),
                ((hid, width), bf16, VMEM),
            ],
            [SMEM, VMEM, VMEM, VMEM, VMEM],
            (info, w_out, w_up, w_down, bias[None]),
            [pltpu.VMEM((16, width), f32)],
            24,
            4 * US,
            8e6,
            hbm_in=False,
            hbm_out=False,
        )

    (qkv_piece,) = send_qkv(info, n_qkv, n_bias)
    if head_count == 2:
        qkv_y = hop(qkv_piece, far)
        rest_piece, down_piece, *near_low = send_rest(info, n_out, n_up, n_down, n_ff)
    else:
        near_low = send_rest(info, n_out, n_up, n_down, n_ff)[2:]
        others = [info.at[7].set(quarter ^ i) for i in range(4)]
        qkv_all = [send_qkv(m, away[0], away[1])[0] for m in others]
        rest_all, down_all = zip(*(send_rest(m, away[2], away[3], away[5], away[4])[:2] for m in others))

    block = 2 * length
    steps = (rows // block,)
    wide = 4 if windows % 4 == 0 else 2
    wide_block, wide_steps = wide * length, (windows // wide,)
    seen = [
        ((rows, cols), bf16, cut(wide_block, cols)),
        ((rows, cols), bf16, cut(wide_block, cols)),
        ((rows, cols), bf16, cut(wide_block, cols)),
        ((rows, cols), bf16, cut(wide_block, cols)),
        ((windows, slots, length), f32, cut(wide, slots, length)),
        ((windows, slots, cols), bf16, cut(wide, slots, cols)),
    ]
    q0, k0, v0, ctx0, att0, picked0, emb, emb_t, wq0 = call(
        lambda *refs: attend_own(length, scale, *refs),
        seen
        + [
            ((rows, width), bf16, cut(wide_block, width)),
            ((width, rows), bf16, pl.BlockSpec((width, wide_block), lambda i: (0, i))),
            ((3, width, cols), bf16, whole(3, width, cols)),
        ],
        [SMEM, SMEM, cut(wide_block, width), whole(NDATA, width), whole(3, width, cols),
         whole(2, cols), whole(*picks.shape)],
        (info, window_group, tokens_in, data_table, n_qkv, n_bias, picks),
        [],
        24,
        9 * US,
        6e6,
        grid=wide_steps,
        hbm_in=False,
    )
    if head_count == 2:

        def spread(x):
            across = hop(x, second_bit)
            return [x, hop(x, core_bit), across, hop(across, core_bit)]

        qkv_y, ctx0, rest_piece = lax.optimization_barrier((qkv_y, ctx0, rest_piece))
        rest_y = hop(rest_piece, far)
        qkv_all = spread(qkv_y)
        rest_y, emb, down_piece = lax.optimization_barrier((rest_y, emb, down_piece))
        down_y = hop(down_piece, far)
        rest_all = spread(rest_y)
    q1, k1, v1, ctx1, att1, picked1, wq1, picks1 = call(
        lambda *refs: attend_far(length, scale, *refs),
        seen + [((3, width, cols), bf16, whole(3, width, cols)), ((windows, slots), f32, whole(windows, slots))],
        [SMEM, cut(wide_block, width)] + [HBM] * 4,
        (info, emb, *qkv_all),
        [
            pltpu.VMEM((extra_rows, cols), bf16),
            pltpu.VMEM((2, cols), f32),
            pltpu.SemaphoreType.DMA((13,)),
        ],
        24,
        9 * US,
        6e6,
        grid=wide_steps,
        hbm_in=False,
    )
    if head_count == 2:
        down_y, ctx1 = lax.optimization_barrier((down_y, ctx1))
        down_all = spread(down_y)

    def kinds(x):
        return [jax.ShapeDtypeStruct(x.shape, k) for k in (f32, f32, f32, bf16)]

    few = kinds(first_qkv) + [
        jax.ShapeDtypeStruct(first_out.shape, f32),
        jax.ShapeDtypeStruct((2,) + first_out.shape, f32),
        jax.ShapeDtypeStruct(first_out.shape, bf16),
    ]
    many = kinds(first_up) + kinds(first_down)

    def make_few(gate):
        return blanks_for(gate, few)

    def make_many(gate):
        return blanks_for(gate, many)

    def make_input_grad(gp1):
        return call(
            input_grad,
            [((rows, width), f32, cut(block, width))],
            [cut(block, cols)] * 6 + [whole(3, width, cols)] * 2 + [cut(block, width)],
            (gq0, gk0, gv0, gq1, gk1, gv1, wq0, wq1, gp1),
            [],
            24,
            US // 2,
            1e6,
            grid=steps,
        )[0]

    parts = 2 if windows % 4 == 0 else 1
    output_rows, gp1, ga, keep_one, send_one, sums, wo = call(
        lambda *refs: feed_forward(length, parts, *refs),
        [
            ((rows, width), f32, HBM),
            ((rows, width), f32, HBM),
            ((rows, width), bf16, HBM),
            ((2, buf_rows // 2, width), bf16, HBM),
            ((2, buf_rows // 2, width), bf16, HBM),
            ((16, width), f32, VMEM),
            ((2, cols, width), bf16, HBM),
        ],
        [SMEM, SMEM, VMEM, VMEM, VMEM, VMEM] + [HBM] * 11 + [VMEM, VMEM, VMEM, HBM],
        (info, window_group, tokens_in, data_table, ctx0, ctx1, *near_low, *rest_all, *down_all,
         n_ff[None], norm_gains, shifts, cotangent),
        [
            pltpu.VMEM((2, cols, width), bf16),
            pltpu.VMEM((2, width, hid), bf16),
            pltpu.VMEM((2, hid, width), bf16),
            pltpu.VMEM((rows, 2 * hid), bf16),
            pltpu.VMEM((rows, 2 * hid), bf16),
            pltpu.VMEM((rows, 2 * hid), bf16),
            pltpu.VMEM((rows, width), bf16),
            pltpu.VMEM((rows, width), bf16),
            pltpu.VMEM((rows, width), bf16),
            pltpu.VMEM((rows, width), f32),
            pltpu.VMEM((rows, width), f32),
            pltpu.VMEM((rows, width), f32),
            pltpu.VMEM((rows, width), f32),
            pltpu.VMEM((width, rows), bf16),
            pltpu.VMEM((width, rows), bf16),
            pltpu.VMEM((2, hid), f32),
            pltpu.VMEM((16, width), bf16),
            pltpu.VMEM((2, buf_rows, width), bf16),
            pltpu.SemaphoreType.DMA((21,)),
            pltpu.SemaphoreType.DMA((3,)),
            pltpu.SemaphoreType.DMA((5,)),
        ],
        56,
        24 * US,
        20e6,
    )
    if quick:
        state_one = sum_start(info, keep_one, send_one, bits, far, core_bit)
        ga, held = lax.optimization_barrier((ga, state_one[0]))
        state_one = (held, *state_one[1:])
    else:
        sum_one = plus(keep_one, hop(send_one, core_bit))
        sum_one, ga = lax.optimization_barrier((sum_one, ga))

    def make_back(g, ga, picks, wq, k, v, att, picked, extra_in):
        last = g == 0
        n = 3 * half // 2 + 32 * last
        more = [((16, cols), f32, whole(16, cols)), ((8, width), f32, whole(8, width))]
        return call(
            lambda *refs: attend_back(length, scale, g, *refs),
            [((rows, cols), bf16, cut(wide_block, cols))] * 3
            + [((n, width), bf16, HBM)] * 2
            + ([] if last else more),
            [SMEM, SMEM, cut(wide_block, width), FAR, whole(2, cols, width), whole(*picks.shape), FAR,
             cut(wide_block, cols), cut(wide_block, cols), cut(wide, slots, length), cut(wide, slots, cols)]
            + [whole(*x.shape) for x in extra_in],
            (info, window_group, ga, emb_t, wo, picks, wq, k, v, att, picked, *extra_in),
            [pltpu.VMEM((rows, cols), bf16)] * 3
            + [
                pltpu.VMEM((width, rows), bf16),
                pltpu.VMEM((3, width, cols), bf16),
                pltpu.VMEM((3 * half + 32 * last, width), bf16),
            ]
            + ([pltpu.VMEM((16, cols), f32), pltpu.VMEM((32, width), f32)] if last else [])
            + [pltpu.SemaphoreType.DMA((10,))],
            32,
            6 * US,
            8e6,
            grid=wide_steps,
        )

    gq1, gk1, gv1, keep_far, send_far, tsum, table_far = make_back(
        1, ga, picks1, wq1, k1, v1, att1, picked1, ()
    )
    if quick:
        held, keep_far, send_far = lax.optimization_barrier((state_one[0], keep_far, send_far))
        state_one = sum_middle(info, (held, *state_one[1:]), bits, far, width)
        held, ga, send_far = lax.optimization_barrier((state_one[0], ga, send_far))
        state_one = (held, *state_one[1:])
        got_far = hop(send_far, core_bit)
    gq0, gk0, gv0, keep_near, send_near = make_back(
        0, ga, picks, wq0, k0, v0, att0, picked0, (sums, tsum, table_far)
    )

    shards = head_count // 2
    mine = head % shards

    def shard(x, dim):
        n = x.shape[dim] // shards
        return x if shards == 1 else lax.dynamic_slice_in_dim(x, mine * n, n, dim)

    owned = (owner_list == my_rank).astype(jnp.int32)

    rate_wide = width ** (-0.5)
    rate_out = max(width // head_dim, 1) ** (-0.5)
    rate_down = (n_down.shape[0] * 2) ** (-0.5)
    moments_in = (
        weight_qkv, first_qkv, second_qkv, basis_qkv_left, basis_qkv_right,
        weight_out, first_out, second_out, basis_out_left, basis_out_right,
        weight_up, first_up, second_up, basis_up_left, basis_up_right,
        weight_down, first_down, second_down, basis_down_left, basis_down_right,
    )
    if quick:
        held, keep_near, send_near = lax.optimization_barrier((state_one[0], keep_near, send_near))
        beside = (
            make_many,
            lambda gate: make_input_grad(lax.optimization_barrier((gp1, gate))[0]),
            make_few,
        )
        pieces_one, pieces_two, small, (many, grad_rows, few) = sum_finish(
            info, (held, *state_one[1:]), (keep_near, send_near, keep_far, got_far), bits, far, core_bit, beside
        )
        likes = [first_qkv, first_out, first_up, first_down]
        blanks = [*few, *many]
        temps = [first_qkv.shape[1:], first_out.shape, first_up.shape, first_down.shape]
        outs = call(
            lambda *refs: update_all(rate_out, rate_wide, rate_down, cols, hid, *refs),
            [(x.shape, f32, HBM) for x in likes] + [(x.shape, x.dtype, HBM) for x in blanks],
            [SMEM, SMEM] + [HBM] * 4 + [FAR] * 35,
            (owned, info, *pieces_one, *pieces_two, *moments_in, *blanks),
            [pltpu.VMEM(x.shape, f32) for x in moments_in]
            + [pltpu.VMEM((buf_rows, width), bf16), pltpu.VMEM((3 * half, width), bf16)]
            + [pltpu.VMEM(x.shape, f32) for x in likes]
            + [pltpu.VMEM(x.shape, bf16) for x in likes]
            + [
                pltpu.VMEM((width, width), bf16),
                pltpu.VMEM(basis_qkv_right.shape[1:], bf16),
                pltpu.VMEM(basis_up_right.shape, bf16),
            ]
            + [pltpu.VMEM(x, bf16) for x in temps * 2]
            + [
                pltpu.SemaphoreType.DMA((10,)),
                pltpu.SemaphoreType.DMA((6, 5)),
                pltpu.SemaphoreType.DMA((6, 4)),
            ],
            49,
            12 * US,
            30e6,
            {26 + i: 4 + i for i in range(15)},
        )
        grad_qkv_all, grad_out_all, grad_up_all, grad_down_all = outs[:4]
        qkv_outs, rest_outs = outs[3:8], outs[5:19]
        grad_table_all, grad_gains_all, grad_shifts_all, grad_ff_all, grad_bias_all = small
        grad_ff_all = grad_ff_all.reshape(-1)
    else:
        grad_rows = make_input_grad(gp1)
        n = 3 * half // 2
        keep_two, send_two = (
            jnp.stack([near[: n + 16], jnp.concatenate([away_part, near[n + 16 :]])])
            for near, away_part in ((keep_near, keep_far), (send_near, send_far))
        )
        blanks = make_few(sums) + make_many(sums)
        early, late = early_steps(bits, far, core_bit), late_steps(16, bits, far, core_bit)
        state_one, state_two = early[0](sum_one), (keep_two, send_two)
        for i in range(1, max(len(early), len(late) + 1)):
            state_one, state_two = lax.optimization_barrier((state_one, state_two))
            if i < len(early):
                state_one = early[i](state_one)
            if i <= len(late):
                state_two = late[i - 1](state_two)
        sum_one, (sum_two, small) = state_one, state_two
        small = small[0]
        g_up = shard(jnp.concatenate([sum_one[:width], sum_one[width : 2 * width]], 1), 1)
        g_down_t = shard(
            jnp.concatenate([sum_one[2 * width : 3 * width], sum_one[3 * width : 4 * width]], 1), 1
        )
        g_out = shard(sum_one[4 * width :], 0)

        def rest_body(*refs):
            update_rest(rate_out, rate_wide, rate_down, *refs)

        tall, wide, low = first_out.shape, first_up.shape, first_down.shape
        rest_outs = call(
            rest_body,
            [(tall, f32, VMEM), (wide, f32, VMEM), (low, f32, VMEM)]
            + [(x.shape, x.dtype, HBM) for x in blanks[4:]],
            [SMEM, VMEM, VMEM, VMEM] + [HBM] * (15 + 11),
            (owned, g_out, g_up, g_down_t,
             weight_out, first_out, second_out, basis_out_left, basis_out_right,
             weight_up, first_up, second_up, basis_up_left, basis_up_right,
             weight_down, first_down, second_down, basis_down_left, basis_down_right, *blanks[4:]),
            [pltpu.VMEM(tall, f32)] * 3
            + [
                pltpu.VMEM(tall, bf16),
                pltpu.VMEM(basis_out_left.shape, f32),
                pltpu.VMEM(basis_out_right.shape, f32),
                pltpu.VMEM(basis_out_right.shape, bf16),
                pltpu.VMEM(tall, bf16),
                pltpu.VMEM(tall, bf16),
            ]
            + [pltpu.VMEM(wide, f32)] * 3
            + [
                pltpu.VMEM(wide, bf16),
                pltpu.VMEM(basis_up_left.shape, f32),
                pltpu.VMEM(basis_up_right.shape, f32),
                pltpu.VMEM(basis_up_left.shape, bf16),
                pltpu.VMEM(basis_up_right.shape, bf16),
                pltpu.VMEM(wide, bf16),
                pltpu.VMEM(wide, bf16),
            ]
            + [pltpu.VMEM(low, f32)] * 3
            + [pltpu.VMEM(low, bf16)] * 3
            + [pltpu.SemaphoreType.DMA((5,))],
            48,
            12 * US,
            20e6,
            {4 + 15 + i: 3 + i for i in range(11)},
        )
        grad_out_all, grad_up_all, grad_down_all = rest_outs[:3]

        pairs = sum_two.reshape(3, half, width)
        g_qkv = shard(jnp.concatenate([pairs[:, :, :cols], pairs[:, :, cols:]], 1), 2)
        small = small.astype(f32)

        def qkv_body(*refs):
            update_qkv(rate_wide, *refs)

        one = first_qkv.shape[1:]
        qkv_outs = call(
            qkv_body,
            [(first_qkv.shape, f32, VMEM)] + [(x.shape, x.dtype, HBM) for x in blanks[:4]],
            [SMEM, VMEM] + [HBM] * 9,
            (owned, g_qkv, weight_qkv, first_qkv, second_qkv, basis_qkv_left, basis_qkv_right, *blanks[:4]),
            [pltpu.VMEM(one, f32)] * 3
            + [
                pltpu.VMEM(one, bf16),
                pltpu.VMEM(basis_qkv_left.shape[1:], f32),
                pltpu.VMEM(basis_qkv_right.shape[1:], f32),
                pltpu.VMEM(basis_qkv_left.shape[1:], bf16),
                pltpu.VMEM(basis_qkv_right.shape[1:], bf16),
                pltpu.VMEM(one, bf16),
                pltpu.VMEM(one, bf16),
                pltpu.SemaphoreType.DMA((5,)),
            ],
            24,
            6 * US,
            8e6,
            {7 + i: 1 + i for i in range(4)},
        )
        grad_qkv_all = qkv_outs[0]
        grad_table_all = small[0:2]
        grad_gains_all = small[2:4]
        grad_shifts_all = small[4:8]
        grad_ff_all = shard(small[8:10].reshape(-1), 0)
        grad_bias_all = shard(small[10].reshape(2, cols), 1)
    return (
        output_rows,
        grad_rows,
        grad_table_all,
        grad_gains_all,
        grad_shifts_all,
        grad_bias_all,
        grad_ff_all,
        grad_qkv_all,
        grad_out_all,
        grad_up_all,
        grad_down_all,
        *(x[None] for x in qkv_outs[1:]),
        *(x[None] for x in rest_outs[3:]),
    )


def solution(mesh):
    in_specs = (
        P(("dp", "head"), None),
        P(("dp", "head"), None),
        P(),
        P("dp"),
        P("dp", "head", None),
        P(),
        P(None, None, "head"),
        P(None, "head"),
        P("head", None),
        P(None, "head"),
        P("head"),
        P("head", None),
        P(),
        P(),
        P(None, None, "head"),
        P(None, None, "head"),
        P("head", None),
        P("head", None),
        P(None, "head"),
        P(None, "head"),
        P("head", None),
        P("head", None),
        P(),
        P(None, "head", None, None),
        P("head", None, None),
        P(),
        P(),
        P("head", None, None),
        P("head", None, None),
        P(),
    )
    out_specs = (
        P(("dp", "head"), None),
        P(("dp", "head"), None),
        P(),
        P(),
        P(),
        P(None, "head"),
        P("head"),
        P(None, None, "head"),
        P("head", None),
        P(None, "head"),
        P("head", None),
        P("dp", None, None, "head"),
        P("dp", None, None, "head"),
        P("dp", None, None, "head"),
        P("dp", None, None, "head"),
        P("dp", "head", None),
        P("dp", None, "head", None),
        P("dp", "head", None),
        P("dp", None, "head"),
        P("dp", None, "head"),
        P("dp", None, "head"),
        P("dp", None, "head"),
        P("dp", "head", None),
        P("dp", "head", None),
        P("dp", "head", None),
        P("dp", "head", None),
    )
    return jax.shard_map(
        per_device, mesh=mesh, in_specs=in_specs, out_specs=out_specs, check_vma=False
    )
```

time: 188 us -> 172 us (0.915); the launches traced: 191 us -> 168 us
  Pallas kernels: 102 us -> 83.1 us
  waiting for transfers between devices: 50.4 us -> 41.2 us
  starting transfers between devices: 29.5 us -> 36.7 us
    pallas_call x18 -> x19, Pallas kernels: 102 us -> 83.1 us  [call(): pl.pallas_call(body, grid=grid, out_shape=tuple((kind(s, d) for s, d, _ i...]
    ppermute x28 -> x39, waiting for transfers between devices: 50.4 us -> 41.2 us  [hop(): lax.ppermute(x, ('dp', 'head'), [(i, i ^ flip) for i in range(count)])]
    ppermute x28 -> x39, starting transfers between devices: 29.5 us -> 36.7 us  [hop(): lax.ppermute(x, ('dp', 'head'), [(i, i ^ flip) for i in range(count)])]
    unnamed x56 -> x72, local copies, waits for them, and re-layouts: 6.09 us -> 4.95 us
  transfers between devices with their start and end apart: 28 -> 39, of which waited for: 15 -> 19; matrix products, arithmetic and copies ran while one was open for 0% -> 0% of each run, Pallas kernels for 31% -> 23%
where the time goes in v1:
time: 172 us; the launch traced here: 168 us
  Pallas kernels  83.1 us (48%)
  waiting for transfers between devices  41.2 us (24%)
  starting transfers between devices  36.7 us (21%)
  local copies, waits for them, and re-layouts  5.12 us (3%)
    pallas_call x19, Pallas kernels, call(): pl.pallas_call(body, grid=grid, out_shape=tuple((kind(s, d) for s, d, _ i...  83.1 us
    ppermute x39, waiting for transfers between devices, hop(): lax.ppermute(x, ('dp', 'head'), [(i, i ^ flip) for i in range(count)])  41.2 us
    ppermute x39, starting transfers between devices, hop(): lax.ppermute(x, ('dp', 'head'), [(i, i ^ flip) for i in range(count)])  36.7 us
    unnamed x72, local copies, waits for them, and re-layouts  4.95 us
  transfers between devices with their start and end apart: 39, of which 19 were waited for; matrix products, arithmetic and copies ran while one was open for 0% of the time, Pallas kernels for 23%

profile of v1, /device:TPU:0, one launch (start us, length us, event | category | flops | bytes accessed | tf_op | source)
XLA Modules:
  0.0 168.4 jit_solution(14898888334460604249)
XLA Ops:
  1.6 1.4 copy-done.2
  3.7 1.1 shard_map.485
  4.9 3.0 %collective-permute-start = (bf16[400,256]{1,0:T(8,128)(2,1)S(1)}, bf16[400,256]{1,0:T(8,128)(2,1)S(1)}, u32[]{:S(2)}, u32[]{:S(2)}) collective-permute-start(bf16[400,256]{1,0:T(8,128)(2,1)S(1)} %shard_map.485), channel_id=1, source_target_pairs={{0,1},{1,0},{2,3},{3,2},{4,5},{5,4},{6,7},{7,6},{8,9},{9,8},{10,11... | collective-permute-start | bytes 614408 | tf_op jit(solution)/shard_map/ppermute | solution.py:500
  8.0 4.3 %shard_map.486 = (bf16[768,256]{1,0:T(8,128)(2,1)}, bf16[768,256]{1,0:T(8,128)(2,1)}, bf16[768,256]{1,0:T(8,128)(2,1)}, bf16[768,256]{1,0:T(8,128)(2,1)}, f32[8,...) custom-call(s32[8]{0:T(128)S(1)} %stack.32.refs_0_.info.refs_1_, ...), custom_call_target="tpu_custom_call" | custom-call | flops 8999999488 | bytes 6000000 | tf_op jit(solution)/shard_map/pallas_call | solution.py:67
  12.3 0.8 shard_map.487
  13.2 1.6 collective-permute-start.4
  14.8 1.5 collective-permute-start.1
  16.3 3.5 %collective-permute-done.4.refs_4_ = bf16[400,256]{1,0:T(8,128)(2,1)S(1)} collective-permute-done((bf16[400,256]{1,0:T(8,128)(2,1)S(1)}, bf16[400,256]{1,0:T(8,128)(2,1)S(1)}, u32[]{:S(2)}, u32[]{:S(2)}) %collective-permute-start.4) | collective-permute-done | bytes 204832 | tf_op jit(solution)/shard_map/ppermute | solution.py:500
  19.8 4.2 %collective-permute-done.1.refs_9_ = bf16[336,512]{1,0:T(8,128)(2,1)S(1)} collective-permute-done((bf16[336,512]{1,0:T(8,128)(2,1)S(1)}, bf16[336,512]{1,0:T(8,128)(2,1)S(1)}, u32[]{:S(2)}, u32[]{:S(2)}) %collective-permute-start.1) | collective-permute-done | bytes 344096 | tf_op jit(solution)/shard_map/ppermute | solution.py:500
  24.0 0.9 collective-permute-start.2
  25.5 5.1 %shard_map.488 = (bf16[768,256]{1,0:T(8,128)(2,1)}, bf16[768,256]{1,0:T(8,128)(2,1)}, bf16[768,256]{1,0:T(8,128)(2,1)}, bf16[768,256]{1,0:T(8,128)(2,1)}, f32[8,...) custom-call(s32[8]{0:T(128)S(1)} %stack.32.refs_0_.info.refs_1_, ...), custom_call_target="tpu_custom_call" | custom-call | flops 8999999488 | bytes 6000000 | tf_op jit(solution)/shard_map/pallas_call | solution.py:67
  30.6 1.6 collective-permute-start.10
  32.2 2.0 %collective-permute-done.7.refs_11_ = bf16[336,512]{1,0:T(8,128)(2,1)S(1)} collective-permute-done((bf16[336,512]{1,0:T(8,128)(2,1)S(1)}, bf16[336,512]{1,0:T(8,128)(2,1)S(1)}, u32[]{:S(2)}, u32[]{:S(2)}) %collective-permute-start.7) | collective-permute-done | bytes 344096 | tf_op jit(solution)/shard_map/ppermute | solution.py:500
  34.7 3.3 %collective-permute-done.10.refs_15_ = bf16[256,512]{1,0:T(8,128)(2,1)S(1)} collective-permute-done((bf16[256,512]{1,0:T(8,128)(2,1)S(1)}, bf16[256,512]{1,0:T(8,128)(2,1)S(1)}, u32[]{:S(2)}, u32[]{:S(2)}) %collective-permute-start.10) | collective-permute-done | bytes 262176 | tf_op jit(solution)/shard_map/ppermute | solution.py:500
  38.1 1.5 collective-permute-done.11.refs_16_
  40.2 24.4 %shard_map.489 = (f32[768,512]{1,0:T(8,128)}, f32[768,512]{1,0:T(8,128)}, bf16[768,512]{1,0:T(8,128)(2,1)}, bf16[2,1152,512]{2,1,0:T(8,128)(2,1)}, bf16[2,1152,5...) custom-call(s32[8]{0:T(128)} %copy-done.5, s32[16]{0:T(128)} %refs_1_.9, ...), custom_call_target="tpu_custom_call" | custom-call | flops 24000000000 | bytes 20000000 | tf_op jit(solution)/shard_map/pallas_call | solution.py:67
  64.9 4.6 %collective-permute-done.12.got = bf16[2,1152,512]{2,1,0:T(8,128)(2,1)S(1)} collective-permute-done((bf16[2,1152,512]{2,1,0:T(8,128)(2,1)}, bf16[2,1152,512]{2,1,0:T(8,128)(2,1)S(1)}, u32[]{:S(2)}, u32[]{:S(2)}) %collective-permute-start.12) | collective-permute-done | bytes 2359328 | tf_op jit(solution)/shard_map/ppermute | solution.py:500
  69.5 1.7 copy-done.14
  71.2 1.1 shard_map.490
  72.3 1.7 %collective-permute-start.13 = (bf16[384,512]{1,0:T(8,128)(2,1)S(1)}, bf16[384,512]{1,0:T(8,128)(2,1)S(1)}, u32[]{:S(2)}, u32[]{:S(2)}) collective-permute-start(bf16[384,512]{1,0:T(8,128)(2,1)S(1)} %get-tuple-element.197), channel_id=1, source_target_pairs={{0,1},{1,0},{2,3},{3,2},{4,5},{5,4},{6,7},{7,6},{8,9},{9,8},{10,11... | collective-permute-start | bytes 1179656 | tf_op jit(solution)/shard_map/ppermute | solution.py:500
  74.5 1.6 collective-permute-start.15
  76.1 7.0 %shard_map.491 = (bf16[768,256]{1,0:T(8,128)(2,1)}, bf16[768,256]{1,0:T(8,128)(2,1)}, bf16[768,256]{1,0:T(8,128)(2,1)}, bf16[384,512]{1,0:T(8,128)(2,1)}, bf16[3...) custom-call(s32[8]{0:T(128)S(1)} %copy-done.6, s32[16]{0:T(128)S(1)} %copy-done.13, ...), custom_call_target="tpu_custom_call" | custom-call | flops 6000000000 | bytes 8000000 | tf_op jit(solution)/shard_map/pallas_call | solution.py:67
  83.5 1.4 collective-permute-done.14.got1
  85.1 0.8 shard_map.492
  85.9 1.6 collective-permute-start.16
  87.5 1.6 collective-permute-start.17
  89.4 7.1 %shard_map.493 = (bf16[768,256]{1,0:T(8,128)(2,1)}, bf16[768,256]{1,0:T(8,128)(2,1)}, bf16[768,256]{1,0:T(8,128)(2,1)}, bf16[416,512]{1,0:T(8,128)(2,1)}, bf16[416,512]{1,0:T(8,128)(2,1)}) custom-call(s32[8]{0:T(128)S(1)} %copy-done.6, s32[16]{0:T(128)S(1)} %copy-done.13, bf16[768,512]{1,0:T(8,128)(2,1)} %get-tuple-element.205.refs_2_, ...), custom_call_target="tpu_custom_call" | custom-call | flops 6000000000 | bytes 8000000 | tf_op jit(solution)/shard_map/pallas_call | solution.py:67
  98.5 1.7 collective-permute-start.20
  100.7 2.2 %collective-permute-done.19.second = bf16[96,512]{1,0:T(8,128)(2,1)S(1)} collective-permute-done((bf16[96,512]{1,0:T(8,128)(2,1)S(1)}, bf16[96,512]{1,0:T(8,128)(2,1)S(1)}, u32[]{:S(2)}, u32[]{:S(2)}) %collective-permute-start.19) | collective-permute-done | bytes 98336 | tf_op jit(solution)/shard_map/ppermute | solution.py:500
  103.1 1.7 collective-permute-done.21.first
  104.8 0.8 shard_map.495
  105.6 2.6 %collective-permute-start.24 = (bf16[288,512]{1,0:T(8,128)(2,1)S(1)}, bf16[288,512]{1,0:T(8,128)(2,1)S(1)}, u32[]{:S(2)}, u32[]{:S(2)}) collective-permute-start(bf16[288,512]{1,0:T(8,128)(2,1)S(1)} %get-tuple-element.234.refs_0_.part), channel_id=1, source_target_pairs={{0,16},{1,17},{2,18},{3,19},{4,20},{5,21},{6,22},{7,23},{8,24},{9,... | collective-permute-start | bytes 884744 | tf_op jit(solution)/shard_map/ppermute | solution.py:500
  109.2 2.5 %collective-permute-start.27 = (bf16[208,512]{1,0:T(8,128)(2,1)S(1)}, bf16[208,512]{1,0:T(8,128)(2,1)S(1)}, u32[]{:S(2)}, u32[]{:S(2)}) collective-permute-start(bf16[208,512]{1,0:T(8,128)(2,1)S(1)} %get-tuple-element.238), channel_id=1, source_target_pairs={{0,5},{1,4},{2,7},{3,6},{4,1},{5,0},{6,3},{7,2},{8,13},{9,12},{10,... | collective-permute-start | bytes 638984 | tf_op jit(solution)/shard_map/ppermute | solution.py:500
  111.8 5.3 %shard_map.496 = (f32[512,1024]{1,0:T(8,128)}, f32[512,1024]{1,0:T(8,128)}, f32[512,1024]{1,0:T(8,128)}, bf16[512,1024]{1,0:T(8,128)(2,1)}, f32[1024,512]{1,0:T(...) custom-call(bf16[288,512]{1,0:T(8,128)(2,1)S(1)} %get-tuple-element.234.refs_0_.part), custom_call_target="tpu_custom_call" | custom-call | flops 500000000 | bytes 1000000 | tf_op jit(solution)/shard_map/pallas_call | solution.py:67
  117.1 1.5 collective-permute-done.26.far
  118.6 1.7 %collective-permute-done.24.third = bf16[288,512]{1,0:T(8,128)(2,1)S(1)} collective-permute-done((bf16[288,512]{1,0:T(8,128)(2,1)S(1)}, bf16[288,512]{1,0:T(8,128)(2,1)S(1)}, u32[]{:S(2)}, u32[]{:S(2)}) %collective-permute-start.24) | collective-permute-done | bytes 294944 | tf_op jit(solution)/shard_map/ppermute | solution.py:500
  120.3 1.5 shard_map.497
  123.0 3.4 %collective-permute-start.30 = (bf16[64,512]{1,0:T(8,128)(2,1)S(1)}, bf16[64,512]{1,0:T(8,128)(2,1)S(1)}, u32[]{:S(2)}, u32[]{:S(2)}) collective-permute-start(bf16[64,512]{1,0:T(8,128)(2,1)S(1)} %get-tuple-element.244), channel_id=1, source_target_pairs={{0,16},{1,17},{2,18},{3,19},{4,20},{5,21},{6,22},{7,23},{8,24},{9,... | collective-permute-start | bytes 196616 | tf_op jit(solution)/shard_map/ppermute | solution.py:500
  126.8 3.0 %shard_map.498 = (f32[1536,256]{1,0:T(8,128)}, f32[1536,256]{1,0:T(8,128)}, f32[1536,256]{1,0:T(8,128)}, bf16[1536,256]{1,0:T(8,128)(2,1)}, f32[256,512]{1,0:T(8...) custom-call(bf16[64,512]{1,0:T(8,128)(2,1)S(1)} %get-tuple-element.243.refs_0_.own), custom_call_target="tpu_custom_call" | custom-call | flops 500000000 | bytes 1000000 | tf_op jit(solution)/shard_map/pallas_call | solution.py:67
  130.3 4.3 %collective-permute-done.31.both = bf16[64,512]{1,0:T(8,128)(2,1)S(1)} collective-permute-done((bf16[64,512]{1,0:T(8,128)(2,1)S(1)}, bf16[64,512]{1,0:T(8,128)(2,1)S(1)}, u32[]{:S(2)}, u32[]{:S(2)}) %collective-permute-start.31) | collective-permute-done | bytes 65568 | tf_op jit(solution)/shard_map/ppermute | solution.py:500
  134.6 1.2 shard_map.499
  136.3 1.7 %collective-permute-start.35 = (bf16[48,512]{1,0:T(8,128)(2,1)S(1)}, bf16[48,512]{1,0:T(8,128)(2,1)S(1)}, u32[]{:S(2)}, u32[]{:S(2)}) collective-permute-start(bf16[48,512]{1,0:T(8,128)(2,1)S(1)} %get-tuple-element.254.near3), channel_id=1, source_target_pairs={{0,24},{1,25},{2,26},{3,27},{4,28},{5,29},{6,30},{7,31},{8,16},{9,... | collective-permute-start | bytes 147464 | tf_op jit(solution)/shard_map/ppermute | solution.py:500
  138.1 1.8 %collective-permute-start.34 = (bf16[48,512]{1,0:T(8,128)(2,1)S(1)}, bf16[48,512]{1,0:T(8,128)(2,1)S(1)}, u32[]{:S(2)}, u32[]{:S(2)}) collective-permute-start(bf16[48,512]{1,0:T(8,128)(2,1)S(1)} %get-tuple-element.254.near3), channel_id=1, source_target_pairs={{0,16},{1,17},{2,18},{3,19},{4,20},{5,21},{6,22},{7,23},{8,24},{9,... | collective-permute-start | bytes 147464 | tf_op jit(solution)/shard_map/ppermute | solution.py:500
  139.8 6.1 %shard_map.500 = f32[768,512]{1,0:T(8,128)} custom-call(bf16[768,256]{1,0:T(8,128)(2,1)} %get-tuple-element.247.refs_0_, bf16[768,256]{1,0:T(8,128)(2,1)} %get-tuple-element.248.refs_1_, bf16[768,256]{1,0:T(8,128)(2,1)} %get-tuple-element.249.refs_2_, bf16[768,256]{1,0:T(8,128)(2,1)} %get-tuple-element.250.refs_3_, ...), custom_call_target="tpu_custom_call" | custom-call | flops 500000000 | bytes 1000000 | tf_op jit(solution)/shard_map/pallas_call | solution.py:67
  147.0 1.3 collective-permute-start.37
  148.3 6.0 %collective-permute-done.37.got = bf16[192,512]{1,0:T(8,128)(2,1)S(1)} collective-permute-done((bf16[192,512]{1,0:T(8,128)(2,1)S(1)}, bf16[192,512]{1,0:T(8,128)(2,1)S(1)}, u32[]{:S(2)}, u32[]{:S(2)}) %collective-permute-start.37) | collective-permute-done | bytes 196640 | tf_op jit(solution)/shard_map/ppermute | solution.py:500
  155.0 1.7 %collective-permute-done.38.refs_5_ = bf16[384,512]{1,0:T(8,128)(2,1)S(1)} collective-permute-done((bf16[384,512]{1,0:T(8,128)(2,1)S(1)}, bf16[384,512]{1,0:T(8,128)(2,1)S(1)}, u32[]{:S(2)}, u32[]{:S(2)}) %collective-permute-start.38) | collective-permute-done | bytes 393248 | tf_op jit(solution)/shard_map/ppermute | solution.py:500
  156.7 11.5 %shard_map.503 = (f32[3,512,256]{2,1,0:T(8,128)}, f32[256,512]{1,0:T(8,128)}, f32[512,1024]{1,0:T(8,128)}, f32[1024,512]{1,0:T(8,128)}, f32[3,512,256]{2,1,0:T(8...) custom-call(s32[6]{0:T(128)S(1)} %compare_convert_fusion.refs_0_, ...), custom_call_target="tpu_custom_call", output_to_operand_aliasing={{4}: (26, {}), {5}: (27, {}), {6}: (28, {}), {7}: (29, {}),... | custom-call | flops 12000000000 | bytes 30000000 | tf_op jit(solution)/shard_map/pallas_call | solution.py:67
  (125 shorter events, 13.2 us)
Async XLA Ops:
  3.7 21.8 %copy-start.5 = (s32[8]{0:T(128)}, s32[8]{0:T(128)S(1)}, u32[]{:S(2)}) copy-start(s32[8]{0:T(128)S(1)} %stack.32.refs_0_.info.refs_1_) | copy-start | bytes 100
  4.9 8.2 %collective-permute-start = (bf16[400,256]{1,0:T(8,128)(2,1)S(1)}, bf16[400,256]{1,0:T(8,128)(2,1)S(1)}, u32[]{:S(2)}, u32[]{:S(2)}) collective-permute-start(bf16[400,256]{1,0:T(8,128)(2,1)S(1)} %shard_map.485), channel_id=1, source_target_pairs={{0,1},{1,0},{2,3},{3,2},{4,5},{5,4},{6,7},{7,6},{8,9},{9,8},{10,11... | collective-permute-start | bytes 614408 | tf_op jit(solution)/shard_map/ppermute | solution.py:500
  12.3 13.2 %copy-start.20 = (bf16[768,512]{1,0:T(8,128)(2,1)S(1)}, bf16[768,512]{1,0:T(8,128)(2,1)}, u32[]{:S(2)}) copy-start(bf16[768,512]{1,0:T(8,128)(2,1)} %get-tuple-element.170.refs_1_) | copy-start | bytes 2359300
  13.1 17.4 %copy-start.17 = (bf16[512,1024]{1,0:T(8,128)(2,1)}, bf16[512,1024]{1,0:T(8,128)(2,1)S(1)}, u32[]{:S(2)}) copy-start(bf16[512,1024]{1,0:T(8,128)(2,1)S(1)} %get-tuple-element.175.refs_7_) | copy-start | bytes 3145732
  13.2 17.4 %copy-start.18 = (bf16[1024,512]{1,0:T(8,128)(2,1)}, bf16[1024,512]{1,0:T(8,128)(2,1)S(1)}, u32[]{:S(2)}) copy-start(bf16[1024,512]{1,0:T(8,128)(2,1)S(1)} %get-tuple-element.176.refs_8_) | copy-start | bytes 3145732
  13.2 17.4 %copy-start.19 = (bf16[256,512]{1,0:T(8,128)(2,1)}, bf16[256,512]{1,0:T(8,128)(2,1)S(1)}, u32[]{:S(2)}) copy-start(bf16[256,512]{1,0:T(8,128)(2,1)S(1)} %get-tuple-element.174.refs_6_) | copy-start | bytes 786436
  13.2 6.6 %collective-permute-start.4 = (bf16[400,256]{1,0:T(8,128)(2,1)S(1)}, bf16[400,256]{1,0:T(8,128)(2,1)S(1)}, u32[]{:S(2)}, u32[]{:S(2)}) collective-permute-start(bf16[400,256]{1,0:T(8,128)(2,1)S(1)} %collective-permute-done.refs_2_), channel_id=1, source_target_pairs={{0,4},{1,5},{2,6},{3,7},{4,0},{5,1},{6,2},{7,3},{8,12},{9,13},{10,... | collective-permute-start | bytes 614408 | tf_op jit(solution)/shard_map/ppermute | solution.py:500
  14.8 9.2 %collective-permute-start.1 = (bf16[336,512]{1,0:T(8,128)(2,1)S(1)}, bf16[336,512]{1,0:T(8,128)(2,1)S(1)}, u32[]{:S(2)}, u32[]{:S(2)}) collective-permute-start(bf16[336,512]{1,0:T(8,128)(2,1)S(1)} %get-tuple-element.166), channel_id=1, source_target_pairs={{0,1},{1,0},{2,3},{3,2},{4,5},{5,4},{6,7},{7,6},{8,9},{9,8},{10,11... | collective-permute-start | bytes 1032200 | tf_op jit(solution)/shard_map/ppermute | solution.py:500
  16.3 9.2 %collective-permute-start.3 = (bf16[400,256]{1,0:T(8,128)(2,1)S(1)}, bf16[400,256]{1,0:T(8,128)(2,1)S(1)}, u32[]{:S(2)}, u32[]{:S(2)}) collective-permute-start(bf16[400,256]{1,0:T(8,128)(2,1)S(1)} %collective-permute-done.refs_2_), channel_id=1, source_target_pairs={{0,2},{1,3},{2,0},{3,1},{4,6},{5,7},{6,4},{7,5},{8,10},{9,11},{10,... | collective-permute-start | bytes 614408 | tf_op jit(solution)/shard_map/ppermute | solution.py:500
  19.8 5.7 %collective-permute-start.5 = (bf16[400,256]{1,0:T(8,128)(2,1)S(1)}, bf16[400,256]{1,0:T(8,128)(2,1)S(1)}, u32[]{:S(2)}, u32[]{:S(2)}) collective-permute-start(bf16[400,256]{1,0:T(8,128)(2,1)S(1)} %collective-permute-done.4.refs_4_), channel_id=1, source_target_pairs={{0,2},{1,3},{2,0},{3,1},{4,6},{5,7},{6,4},{7,5},{8,10},{9,11},{10,... | collective-permute-start | bytes 614408 | tf_op jit(solution)/shard_map/ppermute | solution.py:500
  24.0 6.6 %collective-permute-start.2 = (bf16[256,512]{1,0:T(8,128)(2,1)S(1)}, bf16[256,512]{1,0:T(8,128)(2,1)S(1)}, u32[]{:S(2)}, u32[]{:S(2)}) collective-permute-start(bf16[256,512]{1,0:T(8,128)(2,1)S(1)} %get-tuple-element.169), channel_id=1, source_target_pairs={{0,1},{1,0},{2,3},{3,2},{4,5},{5,4},{6,7},{7,6},{8,9},{9,8},{10,11... | collective-permute-start | bytes 786440 | tf_op jit(solution)/shard_map/ppermute | solution.py:500
  24.9 9.2 %collective-permute-start.7 = (bf16[336,512]{1,0:T(8,128)(2,1)S(1)}, bf16[336,512]{1,0:T(8,128)(2,1)S(1)}, u32[]{:S(2)}, u32[]{:S(2)}) collective-permute-start(bf16[336,512]{1,0:T(8,128)(2,1)S(1)} %collective-permute-done.1.refs_9_), channel_id=1, source_target_pairs={{0,4},{1,5},{2,6},{3,7},{4,0},{5,1},{6,2},{7,3},{8,12},{9,13},{10,... | collective-permute-start | bytes 1032200 | tf_op jit(solution)/shard_map/ppermute | solution.py:500
  30.6 8.9 %copy-start.31 = (bf16[256,512]{1,0:T(8,128)(2,1)}, bf16[256,512]{1,0:T(8,128)(2,1)S(1)}, u32[]{:S(2)}) copy-start(bf16[256,512]{1,0:T(8,128)(2,1)S(1)} %collective-permute-done.2.refs_13_) | copy-start | bytes 786436
  30.6 7.4 %collective-permute-start.10 = (bf16[256,512]{1,0:T(8,128)(2,1)S(1)}, bf16[256,512]{1,0:T(8,128)(2,1)S(1)}, u32[]{:S(2)}, u32[]{:S(2)}) collective-permute-start(bf16[256,512]{1,0:T(8,128)(2,1)S(1)} %collective-permute-done.2.refs_13_), channel_id=1, source_target_pairs={{0,4},{1,5},{2,6},{3,7},{4,0},{5,1},{6,2},{7,3},{8,12},{9,13},{10,... | collective-permute-start | bytes 786440 | tf_op jit(solution)/shard_map/ppermute | solution.py:500
  32.2 5.8 %collective-permute-start.6 = (bf16[336,512]{1,0:T(8,128)(2,1)S(1)}, bf16[336,512]{1,0:T(8,128)(2,1)S(1)}, u32[]{:S(2)}, u32[]{:S(2)}) collective-permute-start(bf16[336,512]{1,0:T(8,128)(2,1)S(1)} %collective-permute-done.1.refs_9_), channel_id=1, source_target_pairs={{0,2},{1,3},{2,0},{3,1},{4,6},{5,7},{6,4},{7,5},{8,10},{9,11},{10,... | collective-permute-start | bytes 1032200 | tf_op jit(solution)/shard_map/ppermute | solution.py:500
  34.2 3.9 %collective-permute-start.8 = (bf16[336,512]{1,0:T(8,128)(2,1)S(1)}, bf16[336,512]{1,0:T(8,128)(2,1)S(1)}, u32[]{:S(2)}, u32[]{:S(2)}) collective-permute-start(bf16[336,512]{1,0:T(8,128)(2,1)S(1)} %collective-permute-done.7.refs_11_), channel_id=1, source_target_pairs={{0,2},{1,3},{2,0},{3,1},{4,6},{5,7},{6,4},{7,5},{8,10},{9,11},{10,... | collective-permute-start | bytes 1032200 | tf_op jit(solution)/shard_map/ppermute | solution.py:500
  34.2 3.9 %collective-permute-start.9 = (bf16[256,512]{1,0:T(8,128)(2,1)S(1)}, bf16[256,512]{1,0:T(8,128)(2,1)S(1)}, u32[]{:S(2)}, u32[]{:S(2)}) collective-permute-start(bf16[256,512]{1,0:T(8,128)(2,1)S(1)} %collective-permute-done.2.refs_13_), channel_id=1, source_target_pairs={{0,2},{1,3},{2,0},{3,1},{4,6},{5,7},{6,4},{7,5},{8,10},{9,11},{10,... | collective-permute-start | bytes 786440 | tf_op jit(solution)/shard_map/ppermute | solution.py:500
  38.0 1.5 collective-permute-start.11
  40.2 29.3 %copy-start.6 = (s32[8]{0:T(128)S(1)}, s32[8]{0:T(128)}, u32[]{:S(2)}) copy-start(s32[8]{0:T(128)} %copy-done.5) | copy-start | bytes 100
  64.7 4.8 %collective-permute-start.12 = (bf16[2,1152,512]{2,1,0:T(8,128)(2,1)}, bf16[2,1152,512]{2,1,0:T(8,128)(2,1)S(1)}, u32[]{:S(2)}, u32[]{:S(2)}) collective-permute-start(bf16[2,1152,512]{2,1,0:T(8,128)(2,1)} %get-tuple-element.182), channel_id=1, source_target_pairs={{0,2},{1,3},{2,0},{3,1},{4,6},{5,7},{6,4},{7,5},{8,10},{9,11},{10,... | collective-permute-start | bytes 7077896 | tf_op jit(solution)/shard_map/ppermute | solution.py:500
  72.3 11.2 %collective-permute-start.13 = (bf16[384,512]{1,0:T(8,128)(2,1)S(1)}, bf16[384,512]{1,0:T(8,128)(2,1)S(1)}, u32[]{:S(2)}, u32[]{:S(2)}) collective-permute-start(bf16[384,512]{1,0:T(8,128)(2,1)S(1)} %get-tuple-element.197), channel_id=1, source_target_pairs={{0,1},{1,0},{2,3},{3,2},{4,5},{5,4},{6,7},{7,6},{8,9},{9,8},{10,11... | collective-permute-start | bytes 1179656 | tf_op jit(solution)/shard_map/ppermute | solution.py:500
  74.0 10.9 %collective-permute-start.14 = (bf16[2,192,512]{2,1,0:T(8,128)(2,1)S(1)}, bf16[2,192,512]{2,1,0:T(8,128)(2,1)S(1)}, u32[]{:S(2)}, u32[]{:S(2)}) collective-permute-start(bf16[2,192,512]{2,1,0:T(8,128)(2,1)S(1)} %get-tuple-element.199), channel_id=1, source_target_pairs={{0,4},{1,5},{2,6},{3,7},{4,0},{5,1},{6,2},{7,3},{8,12},{9,13},{10,... | collective-permute-start | bytes 1179656 | tf_op jit(solution)/shard_map/ppermute | solution.py:500
  74.5 10.6 %collective-permute-start.15 = (bf16[2,192,512]{2,1,0:T(8,128)(2,1)S(1)}, bf16[2,192,512]{2,1,0:T(8,128)(2,1)S(1)}, u32[]{:S(2)}, u32[]{:S(2)}) collective-permute-start(bf16[2,192,512]{2,1,0:T(8,128)(2,1)S(1)} %get-tuple-element.201), channel_id=1, source_target_pairs={{0,8},{1,9},{2,10},{3,11},{4,12},{5,13},{6,14},{7,15},{8,0},{9,1},... | collective-permute-start | bytes 1179656 | tf_op jit(solution)/shard_map/ppermute | solution.py:500
  85.9 10.6 %collective-permute-start.16 = (bf16[192,512]{1,0:T(8,128)(2,1)S(1)}, bf16[192,512]{1,0:T(8,128)(2,1)S(1)}, u32[]{:S(2)}, u32[]{:S(2)}) collective-permute-start(bf16[192,512]{1,0:T(8,128)(2,1)S(1)} %get-tuple-element.218), channel_id=1, source_target_pairs={{0,4},{1,5},{2,6},{3,7},{4,0},{5,1},{6,2},{7,3},{8,12},{9,13},{10,... | collective-permute-start | bytes 589832 | tf_op jit(solution)/shard_map/ppermute | solution.py:500
  87.5 9.0 %collective-permute-start.17 = (bf16[2,96,512]{2,1,0:T(8,128)(2,1)S(1)}, bf16[2,96,512]{2,1,0:T(8,128)(2,1)S(1)}, u32[]{:S(2)}, u32[]{:S(2)}) collective-permute-start(bf16[2,96,512]{2,1,0:T(8,128)(2,1)S(1)} %get-tuple-element.220), channel_id=1, source_target_pairs={{0,8},{1,9},{2,10},{3,11},{4,12},{5,13},{6,14},{7,15},{8,0},{9,1},... | collective-permute-start | bytes 589832 | tf_op jit(solution)/shard_map/ppermute | solution.py:500
  89.1 7.5 %collective-permute-start.18 = (bf16[192,512]{1,0:T(8,128)(2,1)S(1)}, bf16[192,512]{1,0:T(8,128)(2,1)S(1)}, u32[]{:S(2)}, u32[]{:S(2)}) collective-permute-start(bf16[192,512]{1,0:T(8,128)(2,1)S(1)} %get-tuple-element.222), channel_id=1, source_target_pairs={{0,1},{1,0},{2,3},{3,2},{4,5},{5,4},{6,7},{7,6},{8,9},{9,8},{10,11... | collective-permute-start | bytes 589832 | tf_op jit(solution)/shard_map/ppermute | solution.py:500
  96.6 8.2 %copy-start.15 = (bf16[416,512]{1,0:T(8,128)(2,1)S(1)}, bf16[416,512]{1,0:T(8,128)(2,1)}, u32[]{:S(2)}) copy-start(bf16[416,512]{1,0:T(8,128)(2,1)} %get-tuple-element.228.keep0) | copy-start | bytes 1277956
  96.6 8.2 %copy-start.16 = (bf16[384,512]{1,0:T(8,128)(2,1)S(1)}, bf16[384,512]{1,0:T(8,128)(2,1)}, u32[]{:S(2)}) copy-start(bf16[384,512]{1,0:T(8,128)(2,1)} %get-tuple-element.230.keep1) | copy-start | bytes 1179652
  97.6 7.2 %collective-permute-start.22 = (bf16[416,512]{1,0:T(8,128)(2,1)S(1)}, bf16[416,512]{1,0:T(8,128)(2,1)S(1)}, u32[]{:S(2)}, u32[]{:S(2)}) collective-permute-start(bf16[416,512]{1,0:T(8,128)(2,1)S(1)} %copy-done.25), channel_id=1, source_target_pairs={{0,2},{1,3},{2,0},{3,1},{4,6},{5,7},{6,4},{7,5},{8,10},{9,11},{10,... | collective-permute-start | bytes 1277960 | tf_op jit(solution)/shard_map/ppermute | solution.py:500
  97.7 7.1 %collective-permute-start.23 = (bf16[384,512]{1,0:T(8,128)(2,1)S(1)}, bf16[384,512]{1,0:T(8,128)(2,1)S(1)}, u32[]{:S(2)}, u32[]{:S(2)}) collective-permute-start(bf16[384,512]{1,0:T(8,128)(2,1)S(1)} %copy-done.26), channel_id=1, source_target_pairs={{0,2},{1,3},{2,0},{3,1},{4,6},{5,7},{6,4},{7,5},{8,10},{9,11},{10,... | collective-permute-start | bytes 1179656 | tf_op jit(solution)/shard_map/ppermute | solution.py:500
  98.1 4.8 %collective-permute-start.19 = (bf16[96,512]{1,0:T(8,128)(2,1)S(1)}, bf16[96,512]{1,0:T(8,128)(2,1)S(1)}, u32[]{:S(2)}, u32[]{:S(2)}) collective-permute-start(bf16[96,512]{1,0:T(8,128)(2,1)S(1)} %get-tuple-element.225), channel_id=1, source_target_pairs={{0,8},{1,9},{2,10},{3,11},{4,12},{5,13},{6,14},{7,15},{8,0},{9,1},... | collective-permute-start | bytes 294920 | tf_op jit(solution)/shard_map/ppermute | solution.py:500
  98.5 4.6 %collective-permute-start.20 = (bf16[96,512]{1,0:T(8,128)(2,1)S(1)}, bf16[96,512]{1,0:T(8,128)(2,1)S(1)}, u32[]{:S(2)}, u32[]{:S(2)}) collective-permute-start(bf16[96,512]{1,0:T(8,128)(2,1)S(1)} %get-tuple-element.226), channel_id=1, source_target_pairs={{0,1},{1,0},{2,3},{3,2},{4,5},{5,4},{6,7},{7,6},{8,9},{9,8},{10,11... | collective-permute-start | bytes 294920 | tf_op jit(solution)/shard_map/ppermute | solution.py:500
  100.2 4.6 %collective-permute-start.21 = (bf16[96,512]{1,0:T(8,128)(2,1)S(1)}, bf16[96,512]{1,0:T(8,128)(2,1)S(1)}, u32[]{:S(2)}, u32[]{:S(2)}) collective-permute-start(bf16[96,512]{1,0:T(8,128)(2,1)S(1)} %get-tuple-element.227), channel_id=1, source_target_pairs={{0,4},{1,5},{2,6},{3,7},{4,0},{5,1},{6,2},{7,3},{8,12},{9,13},{10,... | collective-permute-start | bytes 294920 | tf_op jit(solution)/shard_map/ppermute | solution.py:500
  105.6 14.7 %collective-permute-start.24 = (bf16[288,512]{1,0:T(8,128)(2,1)S(1)}, bf16[288,512]{1,0:T(8,128)(2,1)S(1)}, u32[]{:S(2)}, u32[]{:S(2)}) collective-permute-start(bf16[288,512]{1,0:T(8,128)(2,1)S(1)} %get-tuple-element.234.refs_0_.part), channel_id=1, source_target_pairs={{0,16},{1,17},{2,18},{3,19},{4,20},{5,21},{6,22},{7,23},{8,24},{9,... | collective-permute-start | bytes 884744 | tf_op jit(solution)/shard_map/ppermute | solution.py:500
  108.3 8.8 %collective-permute-start.25 = (bf16[208,512]{1,0:T(8,128)(2,1)S(1)}, bf16[208,512]{1,0:T(8,128)(2,1)S(1)}, u32[]{:S(2)}, u32[]{:S(2)}) collective-permute-start(bf16[208,512]{1,0:T(8,128)(2,1)S(1)} %get-tuple-element.236), channel_id=1, source_target_pairs={{0,4},{1,5},{2,6},{3,7},{4,0},{5,1},{6,2},{7,3},{8,12},{9,13},{10,... | collective-permute-start | bytes 638984 | tf_op jit(solution)/shard_map/ppermute | solution.py:500
  108.8 9.8 %collective-permute-start.26 = (bf16[208,512]{1,0:T(8,128)(2,1)S(1)}, bf16[208,512]{1,0:T(8,128)(2,1)S(1)}, u32[]{:S(2)}, u32[]{:S(2)}) collective-permute-start(bf16[208,512]{1,0:T(8,128)(2,1)S(1)} %get-tuple-element.237), channel_id=1, source_target_pairs={{0,1},{1,0},{2,3},{3,2},{4,5},{5,4},{6,7},{7,6},{8,9},{9,8},{10,11... | collective-permute-start | bytes 638984 | tf_op jit(solution)/shard_map/ppermute | solution.py:500
  109.2 9.3 %collective-permute-start.27 = (bf16[208,512]{1,0:T(8,128)(2,1)S(1)}, bf16[208,512]{1,0:T(8,128)(2,1)S(1)}, u32[]{:S(2)}, u32[]{:S(2)}) collective-permute-start(bf16[208,512]{1,0:T(8,128)(2,1)S(1)} %get-tuple-element.238), channel_id=1, source_target_pairs={{0,5},{1,4},{2,7},{3,6},{4,1},{5,0},{6,3},{7,2},{8,13},{9,12},{10,... | collective-permute-start | bytes 638984 | tf_op jit(solution)/shard_map/ppermute | solution.py:500
  121.8 12.8 %collective-permute-start.28 = (bf16[256,512]{1,0:T(8,128)(2,1)S(1)}, bf16[256,512]{1,0:T(8,128)(2,1)S(1)}, u32[]{:S(2)}, u32[]{:S(2)}) collective-permute-start(bf16[256,512]{1,0:T(8,128)(2,1)S(1)} %get-tuple-element.239.near2), channel_id=1, source_target_pairs={{0,8},{1,9},{2,10},{3,11},{4,12},{5,13},{6,14},{7,15},{8,0},{9,1},... | collective-permute-start | bytes 786440 | tf_op jit(solution)/shard_map/ppermute | solution.py:500
  122.5 12.1 %collective-permute-start.29 = (bf16[96,512]{1,0:T(8,128)(2,1)S(1)}, bf16[96,512]{1,0:T(8,128)(2,1)S(1)}, u32[]{:S(2)}, u32[]{:S(2)}) collective-permute-start(bf16[96,512]{1,0:T(8,128)(2,1)S(1)} %get-tuple-element.240.near1), channel_id=1, source_target_pairs={{0,4},{1,5},{2,6},{3,7},{4,0},{5,1},{6,2},{7,3},{8,12},{9,13},{10,... | collective-permute-start | bytes 294920 | tf_op jit(solution)/shard_map/ppermute | solution.py:500
  123.0 7.3 %collective-permute-start.30 = (bf16[64,512]{1,0:T(8,128)(2,1)S(1)}, bf16[64,512]{1,0:T(8,128)(2,1)S(1)}, u32[]{:S(2)}, u32[]{:S(2)}) collective-permute-start(bf16[64,512]{1,0:T(8,128)(2,1)S(1)} %get-tuple-element.244), channel_id=1, source_target_pairs={{0,16},{1,17},{2,18},{3,19},{4,20},{5,21},{6,22},{7,23},{8,24},{9,... | collective-permute-start | bytes 196616 | tf_op jit(solution)/shard_map/ppermute | solution.py:500
  126.4 8.2 %collective-permute-start.31 = (bf16[64,512]{1,0:T(8,128)(2,1)S(1)}, bf16[64,512]{1,0:T(8,128)(2,1)S(1)}, u32[]{:S(2)}, u32[]{:S(2)}) collective-permute-start(bf16[64,512]{1,0:T(8,128)(2,1)S(1)} %get-tuple-element.245), channel_id=1, source_target_pairs={{0,24},{1,25},{2,26},{3,27},{4,28},{5,29},{6,30},{7,31},{8,16},{9,... | collective-permute-start | bytes 196616 | tf_op jit(solution)/shard_map/ppermute | solution.py:500
  135.8 10.5 %collective-permute-start.32 = (bf16[384,512]{1,0:T(8,128)(2,1)S(1)}, bf16[384,512]{1,0:T(8,128)(2,1)S(1)}, u32[]{:S(2)}, u32[]{:S(2)}) collective-permute-start(bf16[384,512]{1,0:T(8,128)(2,1)S(1)} %get-tuple-element.262.near1), channel_id=1, source_target_pairs={{0,4},{1,5},{2,6},{3,7},{4,0},{5,1},{6,2},{7,3},{8,12},{9,13},{10,... | collective-permute-start | bytes 1179656 | tf_op jit(solution)/shard_map/ppermute | solution.py:500
  136.3 9.7 %collective-permute-start.33 = (bf16[240,512]{1,0:T(8,128)(2,1)S(1)}, bf16[240,512]{1,0:T(8,128)(2,1)S(1)}, u32[]{:S(2)}, u32[]{:S(2)}) collective-permute-start(bf16[240,512]{1,0:T(8,128)(2,1)S(1)} %get-tuple-element.263.near2), channel_id=1, source_target_pairs={{0,8},{1,9},{2,10},{3,11},{4,12},{5,13},{6,14},{7,15},{8,0},{9,1},... | collective-permute-start | bytes 737288 | tf_op jit(solution)/shard_map/ppermute | solution.py:500
  136.3 9.6 %collective-permute-start.35 = (bf16[48,512]{1,0:T(8,128)(2,1)S(1)}, bf16[48,512]{1,0:T(8,128)(2,1)S(1)}, u32[]{:S(2)}, u32[]{:S(2)}) collective-permute-start(bf16[48,512]{1,0:T(8,128)(2,1)S(1)} %get-tuple-element.254.near3), channel_id=1, source_target_pairs={{0,24},{1,25},{2,26},{3,27},{4,28},{5,29},{6,30},{7,31},{8,16},{9,... | collective-permute-start | bytes 147464 | tf_op jit(solution)/shard_map/ppermute | solution.py:500
  138.1 7.9 %collective-permute-start.34 = (bf16[48,512]{1,0:T(8,128)(2,1)S(1)}, bf16[48,512]{1,0:T(8,128)(2,1)S(1)}, u32[]{:S(2)}, u32[]{:S(2)}) collective-permute-start(bf16[48,512]{1,0:T(8,128)(2,1)S(1)} %get-tuple-element.254.near3), channel_id=1, source_target_pairs={{0,16},{1,17},{2,18},{3,19},{4,20},{5,21},{6,22},{7,23},{8,24},{9,... | collective-permute-start | bytes 147464 | tf_op jit(solution)/shard_map/ppermute | solution.py:500
  146.9 9.8 %collective-permute-start.36 = (bf16[1152,512]{1,0:T(8,128)(2,1)S(1)}, bf16[1152,512]{1,0:T(8,128)(2,1)S(1)}, u32[]{:S(2)}, u32[]{:S(2)}) collective-permute-start(bf16[1152,512]{1,0:T(8,128)(2,1)S(1)} %get-tuple-element.264.refs_2_), channel_id=1, source_target_pairs={{0,2},{1,3},{2,0},{3,1},{4,6},{5,7},{6,4},{7,5},{8,10},{9,11},{10,... | collective-permute-start | bytes 3538952 | tf_op jit(solution)/shard_map/ppermute | solution.py:500
  147.0 7.3 %collective-permute-start.37 = (bf16[192,512]{1,0:T(8,128)(2,1)S(1)}, bf16[192,512]{1,0:T(8,128)(2,1)S(1)}, u32[]{:S(2)}, u32[]{:S(2)}) collective-permute-start(bf16[192,512]{1,0:T(8,128)(2,1)S(1)} %get-tuple-element.265.near), channel_id=1, source_target_pairs={{0,4},{1,5},{2,6},{3,7},{4,0},{5,1},{6,2},{7,3},{8,12},{9,13},{10,... | collective-permute-start | bytes 589832 | tf_op jit(solution)/shard_map/ppermute | solution.py:500
  154.9 1.8 %collective-permute-start.38 = (bf16[384,512]{1,0:T(8,128)(2,1)S(1)}, bf16[384,512]{1,0:T(8,128)(2,1)S(1)}, u32[]{:S(2)}, u32[]{:S(2)}) collective-permute-start(bf16[384,512]{1,0:T(8,128)(2,1)S(1)} %shard_map.502.refs_4_), channel_id=1, source_target_pairs={{0,2},{1,3},{2,0},{3,1},{4,6},{5,7},{6,4},{7,5},{8,10},{9,11},{10,... | collective-permute-start | bytes 1179656 | tf_op jit(solution)/shard_map/ppermute | solution.py:500
  (27 other events, 107.9 us)
